TPU v7x, 512 devices: a whole 4x4x16 slice. The times are simulated.
512 devices in a mesh: ex: 8 (over y, core), par: 64 (over x, z).
Axes of the slice: x: 4, y: 4, z: 16, core: 2. Of those that a mesh axis runs over, the one named last changes fastest.
Arguments:
- activations: bfloat16 [16, 512, 16384], P('ex', None, 'par'), may hold values from -6 to 6
- out_grads: bfloat16 [16, 512, 4096], P('ex', None, 'par'), may hold values from -0.25 to 0.25
- sign_words: int32 [4096, 1024], P(None, 'par'), may hold values from 0 to 65535
- indices: int32 [8192], replicated, may hold values from 0 to 67108863, as said below
Outputs:
- sketch: float32 [16, 8192], P('ex', 'par')
Inputs may be any that keep to these rules, and one draw needn't show every extreme that they name: `indices`: entries 128 q to 128 q + 127 are increasing and distinct and lie in [q * 1048576, (q + 1) * 1048576); the first entry is 0 and the last is 67108863.
All inputs are finite; a program needn't handle non-finite values.
Results may differ from a plain program's by a relative error of at most 0.0029.
Values may be sent and summed in bfloat16 or wider, within the bound.
No kernel may reach another device: no remote copies, remote signals or barrier semaphores. Data moves between devices by JAX's collectives and lax.ppermute only.
A program may use at most 64 MiB of HBM per device.

v0:
```python
import math

import jax
import jax.numpy as jnp
from jax import lax
from jax.sharding import PartitionSpec as P

D = 4096
FF = 16384
KDEV = 128


def parity_sign(values, matrix_order):
    bit_count = jnp.zeros(values.shape, jnp.int32)
    for bit_level in range(matrix_order.bit_length() - 1):
        bit_count = bit_count + jnp.bitwise_and(jnp.right_shift(values, bit_level), 1)
    return (1 - 2 * (bit_count % 2)).astype(jnp.float32)


def hadamard_matrix(matrix_order):
    row_ids = jnp.arange(matrix_order, dtype=jnp.int32)[:, None]
    col_ids = jnp.arange(matrix_order, dtype=jnp.int32)[None, :]
    return parity_sign(jnp.bitwise_and(row_ids, col_ids), matrix_order)


def unpack_signs(packed):
    shifts = jnp.arange(16, dtype=jnp.int32)
    bitset = jnp.bitwise_and(jnp.right_shift(packed[:, :, None], shifts), 1)
    return (1 - 2 * bitset).astype(jnp.float32).reshape(packed.shape[0], packed.shape[1] * 16)


def shards(activations, out_grads, sign_words, indices):
    ex_dev, tok_rows, local_cols = activations.shape
    par_size = lax.axis_size("par")
    position = lax.axis_index("par")
    sign_values = unpack_signs(sign_words)
    pieces = []
    for example in range(ex_dev):

        def example_rows(shard_piece, start_row, example_acts=activations[example]):
            return lax.dot_general(
                shard_piece,
                example_acts,
                (((0,), (0,)), ((), ())),
                preferred_element_type=jnp.float32,
            )

        pieces.append(
            example_rows(
                lax.all_gather(out_grads[example], "par", axis=1, tiled=True), jnp.int32(0)
            )
        )
    gradient = jnp.stack(pieces)
    signed = gradient * sign_values
    depth_bits = D.bit_length() - 1
    upper_order = 1 << depth_bits // 2
    lower_order = D // upper_order
    transformed = jnp.einsum(
        "edl,lm->edm", signed, hadamard_matrix(local_cols), precision=lax.Precision.HIGHEST
    )
    transformed = transformed.reshape(ex_dev, upper_order, lower_order, local_cols)
    transformed = jnp.einsum(
        "ia,eabl->eibl", hadamard_matrix(upper_order), transformed, precision=lax.Precision.HIGHEST
    )
    transformed = jnp.einsum(
        "jb,eibl->eijl", hadamard_matrix(lower_order), transformed, precision=lax.Precision.HIGHEST
    )
    partial_value = (transformed.reshape(ex_dev, D, local_cols) * (1.0 / math.sqrt(D * FF))).astype(
        jnp.bfloat16
    )
    rows_dev = D // par_size
    weights = hadamard_matrix(par_size)
    received = lax.all_to_all(partial_value, "par", split_axis=1, concat_axis=0, tiled=True)
    shaped = received.reshape(par_size, ex_dev, rows_dev, received.shape[-1]).astype(jnp.float32)
    combined = jnp.einsum("tp,pejl->etjl", weights, shaped, precision=lax.Precision.HIGHEST)
    own_block = lax.dynamic_slice_in_dim(indices, position * KDEV, KDEV)
    offset = own_block - position * (rows_dev * FF)
    local_row = offset // FF
    column = offset % FF
    block_idx = column // local_cols
    within = column % local_cols
    flat_index = block_idx * (rows_dev * local_cols) + local_row * local_cols + within
    sketch = combined.reshape(ex_dev, -1)[:, flat_index]
    example_sum = lax.psum(jnp.sum(sketch, axis=0), "ex")
    return sketch - example_sum[None, :] / (ex_dev * lax.axis_size("ex"))


def solution(mesh):
    return jax.shard_map(
        shards,
        mesh=mesh,
        in_specs=(P("ex", None, "par"), P("ex", None, "par"), P(None, "par"), P()),
        out_specs=P("ex", "par"),
        check_vma=False,
    )
```

profile of v0, /device:TPU:1, one launch (start us, length us, event | category | flops | bytes accessed | tf_op | source)
XLA Modules:
  0.0 621.8 jit_solution(2996070009873196841)
XLA Ops:
  6.5 1.5 fusion.100
  8.1 0.0 all-gather.5.cloned.1.call-start
  8.1 0.7 all-gather.5.cloned.1.call-update
  8.9 0.1 shift_right_arithmetic.122
  8.9 3.7 fusion.13
  12.6 5.7 copy.9
  18.3 135.8 %all-gather.7.cloned.1.call-done = bf16[1,512,4096]{1,2,0:T(8,128)(2,1)} async-done(((bf16[1,512,64]{1,2,0:T(8,128)(2,1)}), bf16[1,512,4096]{1,2,0:T(8,128)(2,1)}) %all-gather.7.cloned.1.call-update) | async-done | bytes 4194320 | tf_op jit(solution)/shard_map/all_gather | solution.py:50
  154.1 5.4 convolution_bitcast_fusion
  159.5 138.8 %all-gather.5.cloned.1.call-done = bf16[1,512,4096]{1,2,0:T(8,128)(2,1)} async-done(((bf16[1,512,64]{1,2,0:T(8,128)(2,1)}), bf16[1,512,4096]{1,2,0:T(8,128)(2,1)}) %all-gather.5.cloned.1.call-update) | async-done | bytes 4194320 | tf_op jit(solution)/shard_map/all_gather | solution.py:50
  298.2 3.6 convolution_bitcast_fusion.1
  301.8 1.1 copy-done.1
  303.0 7.6 %fusion = f32[2,4096,256]{2,1,0:T(8,128)S(1)} fusion(f32[1,4096,256]{2,1,0:T(8,128)S(1)} %copy-done.1, f32[1,4096,256]{2,1,0:T(8,128)S(1)} %convolution_bitcast_fusion.1, f32[4096,256]{1,0:T(8,128)S(1)} %copy-done), kind=kOutput, calls=%fused_computation.2 | convolution fusion | flops 6449135616 | bytes 20971520 | tf_op jit(solution)/shard_map/edl,lm->edm/dot_general | solution.py:58
  310.5 13.4 %fusion.19 = f32[2,64,64,256]{3,1,2,0:T(8,128)S(1)} fusion(f32[2,64,64,256]{3,2,1,0:T(8,128)S(1)} %bitcast.55), kind=kOutput, calls=%fused_computation.23 | convolution fusion | flops 1610743808 | bytes 16777216 | tf_op jit(solution)/shard_map/ia,eabl->eibl/dot_general | solution.py:62
  324.0 11.8 %multiply_convert_fusion = bf16[2,64,256,64]{2,3,1,0:T(8,128)(2,1)S(1)} fusion(f32[2,64,64,256]{3,1,2,0:T(8,128)S(1)} %fusion.19), kind=kOutput, calls=%fused_computation.9 | convolution fusion | flops 1614938112 | bytes 12582912 | tf_op jit(solution)/shard_map/jb,eibl->eijl/dot_general | solution.py:65
  335.8 27.2 %copy.12 = bf16[2,4096,256]{2,0,1:T(2,128)(2,1)} copy(bf16[2,4096,256]{2,1,0:T(8,128)(2,1)S(1)} %bitcast.57) | data formatting | bytes 8388608 | tf_op jit(solution)/shard_map/convert_element_type | solution.py:68
  363.0 8.9 %all-to-all-start = ((bf16[2,4096,256]{2,0,1:T(2,128)(2,1)}), bf16[2,4096,256]{2,0,1:T(2,128)(2,1)}, u32[]{:S(2)}, u32[]{:S(2)}) async-start(bf16[2,4096,256]{2,0,1:T(2,128)(2,1)} %copy.12), calls=%async_computation | async-start | bytes 8388608 | tf_op jit(solution)/shard_map/all_to_all | solution.py:73
  372.0 0.8 compare_select_fusion
  372.8 171.9 %all-to-all-done = bf16[2,4096,256]{2,0,1:T(2,128)(2,1)} async-done(((bf16[2,4096,256]{2,0,1:T(2,128)(2,1)}), bf16[2,4096,256]{2,0,1:T(2,128)(2,1)}, u32[]{:S(2)}, u32[]{:S(2)}) %all-to-all-start) | async-done | bytes 4194336 | tf_op jit(solution)/shard_map/all_to_all | solution.py:73
  544.6 11.0 %fusion.22 = f32[2,64,64,256]{3,1,2,0:T(8,128)S(1)} fusion(bf16[2,64,64,256]{3,0,2,1:T(2,128)(2,1)} %bitcast.14), kind=kOutput, calls=%fused_computation.24 | convolution fusion | flops 1610743808 | bytes 12582912 | tf_op jit(solution)/shard_map/tp,pejl->etjl/dot_general | solution.py:75
  555.6 4.9 copy.15
  560.5 23.8 %copy.19 = f32[1,2,4096,256]{3,1,2,0:T(2,128)} copy(f32[1,2,4096,256]{3,2,1,0:T(8,128)S(1)} %bitcast.56) | data formatting | bytes 16777216
  584.3 1.9 gather_fusion
  586.2 27.7 %psum.7 = f32[128]{0:T(128)S(1)} all-reduce(f32[128]{0:T(128)S(1)} %reduce_sum.9), channel_id=1, replica_groups=mesh['ex'=8,'par'=64] {'ex'}, use_global_device_ids=true, to_apply=%region_1.2 | all-reduce | flops 128 | bytes 1024 | tf_op jit(solution)/shard_map/psum | solution.py:84
  613.9 0.6 subtract_bitcast_fusion
  (11 shorter events, 0.1 us)
Async XLA Ops:
  6.5 147.5 %all-gather.7.cloned.1.call-start = ((), (), s32[]{:S(2)}) async-start(), calls=%async_computation.2 | async-start | bytes 4259840 | tf_op jit(solution)/shard_map/all_gather | solution.py:50
  8.1 290.1 %all-gather.5.cloned.1.call-start = ((), (), s32[]{:S(2)}) async-start(), calls=%async_computation.1 | async-start | bytes 4259840 | tf_op jit(solution)/shard_map/all_gather | solution.py:50
  12.6 141.5 %copy-start.2 = (bf16[2,512,256]{2,1,0:T(8,128)(2,1)S(1)}, bf16[2,512,256]{2,1,0:T(8,128)(2,1)}, u32[]{:S(2)}) copy-start(bf16[2,512,256]{2,1,0:T(8,128)(2,1)} %param.4) | copy-start | bytes 1572868
  298.2 3.6 copy-start
  298.2 4.7 copy-start.1
  363.0 181.6 %all-to-all-start = ((bf16[2,4096,256]{2,0,1:T(2,128)(2,1)}), bf16[2,4096,256]{2,0,1:T(2,128)(2,1)}, u32[]{:S(2)}, u32[]{:S(2)}) async-start(bf16[2,4096,256]{2,0,1:T(2,128)(2,1)} %copy.12), calls=%async_computation | async-start | bytes 8388608 | tf_op jit(solution)/shard_map/all_to_all | solution.py:73
Sparse Core Ops, SparseCore 0:
  10.3 143.7 all-gather.6
  157.0 141.1 all-gather.4
where the time goes:
time: 632 us; the launch traced here: 622 us
  waiting for transfers between devices  447 us (71%)
  local copies, waits for them, and re-layouts  66.2 us (10%)
  matrix products  52.8 us (8%)
  blocking collectives  27.7 us (4%)
  between operations  14 us (2%)
  starting transfers between devices  8.98 us (1%)
    all_gather x2, waiting for transfers between devices, shards(): lax.all_gather(out_grads[example], 'par', axis=1, tiled=True)  275 us
    all_to_all x1, waiting for transfers between devices, shards(): lax.all_to_all(partial_value, 'par', split_axis=1, concat_axis=0, tiled=T...  172 us
    psum x1, blocking collectives, shards(): example_sum = lax.psum(jnp.sum(sketch, axis=0), 'ex')  27.7 us
    convert_element_type x1, local copies, waits for them, and re-layouts, shards(): (transformed.reshape(ex_dev, D, local_cols) * (1.0 / math.sqrt(D * FF)))....  27.2 us
    unnamed x7, local copies, waits for them, and re-layouts  24.9 us
    dot_general x1, matrix products, shards(): jnp.einsum('ia,eabl->eibl', hadamard_matrix(upper_order), transformed, pr...  13.4 us
  transfers between devices with their start and end apart: 3, of which 3 were waited for; matrix products, arithmetic and copies ran while one was open for 3% of the time, Pallas kernels for 0%

commit v1 on v0

v1 whole, which is shorter than its diff:
```python
import jax
import jax.numpy as jnp
from jax import lax
from jax.experimental import pallas as pl
from jax.experimental.pallas import tpu as pltpu
from jax.sharding import Mesh, PartitionSpec as P

D = 4096
FF = 16384
TOK = 512
NX = 4
NZ = 16
ROWS = D // NX
COLS = 256
LOW = 64
TILES = ROWS // LOW
KDEV = 128
SAMPLES = NX * KDEV
WIRE = 131072.0
SCALE = 1.0 / 8192.0 / WIRE
VMEM_BYTES = 56 * 1024 * 1024


def sign_of(bits):
    bits = bits ^ (bits >> 4)
    bits = bits ^ (bits >> 2)
    bits = bits ^ (bits >> 1)
    return (1 - 2 * (bits & 1)).astype(jnp.float32)


def prep_kernel(pos_ref, idx_ref, w0, w1, w2, w3, had_ref, hs_ref, js_ref, sign_ref):
    x, z = pos_ref[0], pos_ref[1]
    row = lax.broadcasted_iota(jnp.int32, (COLS, 2 * COLS), 0)
    col = lax.broadcasted_iota(jnp.int32, (COLS, 2 * COLS), 1) & (COLS - 1)
    had_ref[...] = sign_of(row & col).astype(jnp.bfloat16)

    def tile_body(tile, carry):
        idx = idx_ref[pl.ds(tile, 1), :]
        line = lax.broadcasted_iota(jnp.int32, (16, SAMPLES), 0)
        low_signs = sign_of(line & idx)
        high_signs = sign_of(line & (idx >> 4))
        for a in range(16):
            block_rows = low_signs * high_signs[a : a + 1]
            hs_ref[tile, pl.ds(16 * a, 16), :] = block_rows.astype(jnp.bfloat16)
        block = lax.broadcasted_iota(jnp.int32, (NX, SAMPLES), 0)
        sx = (idx >> 12) & 3
        sz = (idx >> 8) & 15
        tx = (idx >> 24) & 3
        js_ref[tile] = sign_of((block & sx) | ((sz & z) << 2) | ((tx & x) << 6)) * SCALE
        return carry

    lax.fori_loop(0, TILES, tile_body, 0)

    byte_row = lax.broadcasted_iota(jnp.int32, (32, COLS), 0)
    byte_col = lax.broadcasted_iota(jnp.int32, (32, COLS), 1)
    spread = (byte_row == (byte_col >> 4) + 16 * ((byte_col >> 3) & 1)).astype(jnp.float32)
    spread = spread.astype(jnp.bfloat16)
    shift = lax.broadcasted_iota(jnp.int32, (ROWS, COLS), 1) & 7
    for delta, w_ref in enumerate((w0, w1, w2, w3)):
        words = w_ref[...]
        two = jnp.concatenate([words & 255, (words >> 8) & 255], axis=0)
        two = two.astype(jnp.float32).astype(jnp.bfloat16)
        value = lax.dot_general(
            two, spread, (((0,), (0,)), ((), ())), preferred_element_type=jnp.float32
        )
        bit = (value.astype(jnp.int32) >> shift) & 1
        sign_ref[x ^ delta] = (1 - 2 * bit).astype(jnp.float32).astype(jnp.bfloat16)


def split(values):
    high = values.astype(jnp.bfloat16)
    return high, (values - high.astype(jnp.float32)).astype(jnp.bfloat16)


def main_kernel(
    pos_ref, idx_ref, js_ref, had_ref, grads_in, acts_in, sign_in, hs_in,
    out_ref, grads, acts, signs, hs, tiles, grad_sem, act_sem, sign_sem, hs_sem,
):
    def load(source, target, sem):
        pltpu.make_async_copy(source, target, sem).start()

    for example in range(2):
        load(grads_in.at[:, example], grads.at[example], grad_sem.at[example])
        for block in range(NX):
            load(acts_in.at[block, example], acts.at[example, block], act_sem.at[example, block])
            if example == 0:
                load(sign_in.at[block], signs.at[block], sign_sem.at[block])
        if example == 0:
            load(hs_in, hs, hs_sem)

    def wait(target, sem):
        pltpu.make_async_copy(target, target, sem).wait()

    had = had_ref[...]
    for example in range(2):
        wait(grads.at[example], grad_sem.at[example])

        def block_body(block, carry, example=example):
            wait(acts.at[example, block], act_sem.at[example, block])
            if example == 0:
                wait(signs.at[block], sign_sem.at[block])
            grad = jnp.dot(
                grads[example].reshape(ROWS, TOK),
                acts[example, block],
                preferred_element_type=jnp.float32,
            )
            signed = grad * signs[block].astype(jnp.float32)
            parts = []
            for b in range(4):
                both = jnp.concatenate(split(signed[b * COLS : (b + 1) * COLS]), axis=0)
                parts.append(jnp.dot(had, both, preferred_element_type=jnp.float32))
            p0, p1 = parts[0] + parts[1], parts[0] - parts[1]
            p2, p3 = parts[2] + parts[3], parts[2] - parts[3]
            for a, value in enumerate((p0 + p2, p1 + p3, p0 - p2, p1 - p3)):
                value = value.astype(jnp.bfloat16)
                for i in range(4):
                    tiles[4 * a + i, example, block] = value[i * LOW : (i + 1) * LOW]
            return carry

        lax.fori_loop(0, NX, block_body, 0)

    wait(hs, hs_sem)

    def tile_body(tile, carry):
        low_row = (idx_ref[pl.ds(tile, 1), :] >> 14) & (LOW - 1)
        chosen = lax.broadcasted_iota(jnp.int32, (LOW, SAMPLES), 0) == low_row
        weights = js_ref[tile]
        left = tiles[tile].reshape(2 * NX * LOW, COLS)
        both = jnp.dot(left, hs[tile], preferred_element_type=jnp.float32)
        for example in range(2):
            total = jnp.zeros((LOW, SAMPLES), jnp.float32)
            for j in range(NX):
                start = (example * NX + j) * LOW
                total = total + both[start : start + LOW] * weights[j : j + 1]
            picked = jnp.sum(jnp.where(chosen, total, 0.0), axis=0, keepdims=True)
            for tx in range(NX):
                out_ref[tile, tx, pl.ds(example, 1), :] = picked[:, tx * KDEV : (tx + 1) * KDEV]
        return carry

    lax.fori_loop(0, TILES, tile_body, 0)


def shards(activations, out_grads, sign_words, indices):
    ex_size = lax.axis_size("ex")
    x, z = lax.axis_index("x"), lax.axis_index("z")
    position = jnp.stack([x, z]).astype(jnp.int32)

    acts = lax.all_gather(activations, "x", axis=0, tiled=False)

    wire = jnp.transpose(out_grads, (0, 2, 1)).astype(jnp.float32) * WIRE
    wire = lax.all_gather(wire.astype(jnp.float16), "z", axis=0, tiled=False)
    grads = wire.astype(jnp.float32).astype(jnp.bfloat16)

    words = jnp.transpose(sign_words, (1, 0)).reshape(FF // 1024, NX, ROWS)
    own_words = []
    for delta in range(NX):
        part = lax.dynamic_index_in_dim(words, x ^ delta, axis=1, keepdims=False)
        if delta:
            part = lax.ppermute(part, "x", [(i, i ^ delta) for i in range(NX)])
        own_words.append(part)
    order = indices.reshape(NX, TILES, KDEV).transpose(1, 0, 2).reshape(TILES, SAMPLES)
    vmem = pl.BlockSpec(memory_space=pltpu.VMEM)
    smem = pl.BlockSpec(memory_space=pltpu.SMEM)
    anywhere = pl.BlockSpec(memory_space=pl.ANY)
    had, hs, js, signs = pl.pallas_call(
        prep_kernel,
        out_shape=[
            jax.ShapeDtypeStruct((COLS, 2 * COLS), jnp.bfloat16),
            jax.ShapeDtypeStruct((TILES, COLS, SAMPLES), jnp.bfloat16),
            jax.ShapeDtypeStruct((TILES, NX, SAMPLES), jnp.float32),
            jax.ShapeDtypeStruct((NX, ROWS, COLS), jnp.bfloat16),
        ],
        in_specs=[smem] + [vmem] * 5,
        out_specs=[vmem] * 4,
        compiler_params=pltpu.CompilerParams(vmem_limit_bytes=VMEM_BYTES),
        cost_estimate=pl.CostEstimate(
            flops=40 * 1024 * 1024, bytes_accessed=8 * 1024 * 1024, transcendentals=0
        ),
        name="prepare_signs",
    )(position, order, *own_words)

    values = pl.pallas_call(
        main_kernel,
        out_shape=jax.ShapeDtypeStruct((TILES, NX, 2, KDEV), jnp.float32),
        in_specs=[smem] + [vmem] * 3 + [anywhere] * 4,
        out_specs=vmem,
        scratch_shapes=[
            pltpu.VMEM((2, NZ, LOW, TOK), jnp.bfloat16),
            pltpu.VMEM((2, NX, TOK, COLS), jnp.bfloat16),
            pltpu.VMEM((NX, ROWS, COLS), jnp.bfloat16),
            pltpu.VMEM((TILES, COLS, SAMPLES), jnp.bfloat16),
            pltpu.VMEM((TILES, 2, NX, LOW, COLS), jnp.bfloat16),
            pltpu.SemaphoreType.DMA((2,)),
            pltpu.SemaphoreType.DMA((2, NX)),
            pltpu.SemaphoreType.DMA((NX,)),
            pltpu.SemaphoreType.DMA,
        ],
        compiler_params=pltpu.CompilerParams(vmem_limit_bytes=VMEM_BYTES),
        cost_estimate=pl.CostEstimate(
            flops=7 * 10**9, bytes_accessed=16 * 1024 * 1024, transcendentals=0
        ),
        name="gradient_transform_sample",
    )(position, order, js, had, grads, acts, signs, hs)

    along_z = lax.all_to_all(values, "z", split_axis=0, concat_axis=0, tiled=True)
    half = jnp.sum(along_z, axis=0)
    sent = jnp.broadcast_to(half[None], (ex_size, NX, 2, KDEV)).reshape(ex_size * NX, 2, KDEV)
    received = lax.all_to_all(sent, ("ex", "x"), split_axis=0, concat_axis=0, tiled=True)
    raw = jnp.sum(received.reshape(ex_size, NX, 2, KDEV), axis=1)
    own_raw = lax.dynamic_index_in_dim(raw, lax.axis_index("ex"), axis=0, keepdims=False)
    return own_raw - jnp.sum(raw, axis=(0, 1))[None, :] / (2 * ex_size)


def solution(mesh):
    ex_size = mesh.shape["ex"]
    grid = Mesh(mesh.devices.reshape(ex_size, NX, NZ), ("ex", "x", "z"))
    return jax.shard_map(
        shards,
        mesh=grid,
        in_specs=(P("ex", None, ("x", "z")), P("ex", None, ("x", "z")), P(None, ("x", "z")), P()),
        out_specs=P("ex", ("x", "z")),
        check_vma=False,
    )
```

time: 632 us -> 141 us (0.22); the launches traced: 622 us -> 140 us
  waiting for transfers between devices: 447 us -> 7.93 us
  local copies, waits for them, and re-layouts: 66.2 us -> 3.98 us
  matrix products: 52.8 us -> 0 us
  blocking collectives: 27.7 us -> 62.9 us
  Pallas kernels: 0 us -> 23.4 us
  starting transfers between devices: 8.98 us -> 25.2 us
    all_gather x2 -> x1, waiting for transfers between devices: 275 us -> 0.01 us  [shards(): acts = lax.all_gather(activations, 'x', axis=0, tiled=False)]
    all_to_all x1, waiting for transfers between devices: 172 us -> 7.21 us  [shards(): lax.all_to_all(sent, ('ex', 'x'), split_axis=0, concat_axis=0, tiled=True)]
    dot_general x6 -> x0, matrix products: 52.8 us -> none  [the longest x1 13.4 us: shards(): jnp.einsum('ia,eabl->eibl', hadamard_matrix(upper_order), transformed, pr...]
    all_gather x0 -> x1, blocking collectives: none -> 44.7 us  [shards(): wire = lax.all_gather(wire.astype(jnp.float16), 'z', axis=0, tiled=False)]
    convert_element_type x2 -> x0, local copies, waits for them, and re-layouts: 32.9 us -> none  [the longest x1 27.2 us: shards(): (transformed.reshape(ex_dev, D, local_cols) * (1.0 / math.sqrt(D * FF)))....]
    psum x1 -> x0, blocking collectives: 27.7 us -> none  [shards(): example_sum = lax.psum(jnp.sum(sketch, axis=0), 'ex')]
    unnamed x7 -> x14, local copies, waits for them, and re-layouts: 24.9 us -> 1.35 us
    pallas_call x0 -> x2, Pallas kernels: none -> 23.4 us  [the longest x1 18.1 us: shards(): pl.pallas_call(main_kernel, out_shape=jax.ShapeDtypeStruct((TILES, NX, 2,...]
  transfers between devices with their start and end apart: 3 -> 5, of which waited for: 3 -> 1; matrix products, arithmetic and copies ran while one was open for 3% -> 4% of each run, Pallas kernels for 0% -> 4%
where the time goes in v1:
time: 141 us; the launch traced here: 140 us
  blocking collectives  62.9 us (45%)
  starting transfers between devices  25.2 us (18%)
  Pallas kernels  23.4 us (17%)
  between operations  13.5 us (10%)
  waiting for transfers between devices  7.93 us (6%)
  local copies, waits for them, and re-layouts  3.98 us (3%)
  other arithmetic  3.19 us (2%)
    all_gather x1, blocking collectives, shards(): wire = lax.all_gather(wire.astype(jnp.float16), 'z', axis=0, tiled=False)  44.7 us
    all_to_all x1, blocking collectives, shards(): lax.all_to_all(values, 'z', split_axis=0, concat_axis=0, tiled=True)  18.2 us
    pallas_call x1, Pallas kernels, shards(): pl.pallas_call(main_kernel, out_shape=jax.ShapeDtypeStruct((TILES, NX, 2,...  18.1 us
    all_to_all x1, starting transfers between devices, shards(): lax.all_to_all(sent, ('ex', 'x'), split_axis=0, concat_axis=0, tiled=True)  15 us
    ppermute x3, starting transfers between devices, shards(): part = lax.ppermute(part, 'x', [(i, i ^ delta) for i in range(NX)])  10.2 us
    all_to_all x1, waiting for transfers between devices, shards(): lax.all_to_all(sent, ('ex', 'x'), split_axis=0, concat_axis=0, tiled=True)  7.21 us
    pallas_call x1, Pallas kernels, shards(): pl.pallas_call(prep_kernel, out_shape=[jax.ShapeDtypeStruct((COLS, 2 * CO...  5.29 us
  transfers between devices with their start and end apart: 5, of which 1 were waited for; matrix products, arithmetic and copies ran while one was open for 4% of the time, Pallas kernels for 4%

profile of v1, /device:TPU:1, one launch (start us, length us, event | category | flops | bytes accessed | tf_op | source)
XLA Modules:
  0.0 140.2 jit_solution(11796335138559808435)
XLA Ops:
  6.5 0.7 all-gather.5.cloned.1.call-update
  7.3 1.1 reshape.22
  8.4 0.3 constant_dynamic-slice_fusion.1
  8.7 3.9 %collective-permute-start = (s32[16,1024]{1,0:T(8,128)S(1)}, s32[16,1024]{1,0:T(8,128)S(1)}, u32[]{:S(2)}, u32[]{:S(2)}) collective-permute-start(s32[16,1024]{1,0:T(8,128)S(1)} %bitcast.40), channel_id=1, source_target_pairs={{0,16},{16,0},{32,48},{48,32},{1,17},{17,1},{33,49},{49,33},{2,18}... | collective-permute-start | bytes 196616 | tf_op jit(solution)/shard_map/ppermute | solution.py:159
  12.7 4.4 %collective-permute-start.1 = (s32[16,1024]{1,0:T(8,128)S(1)}, s32[16,1024]{1,0:T(8,128)S(1)}, u32[]{:S(2)}, u32[]{:S(2)}) collective-permute-start(s32[16,1024]{1,0:T(8,128)S(1)} %bitcast.41), channel_id=1, source_target_pairs={{0,32},{16,48},{32,0},{48,16},{1,33},{17,49},{33,1},{49,17},{2,34}... | collective-permute-start | bytes 196616 | tf_op jit(solution)/shard_map/ppermute | solution.py:159
  17.1 1.9 %collective-permute-start.2 = (s32[16,1024]{1,0:T(8,128)S(1)}, s32[16,1024]{1,0:T(8,128)S(1)}, u32[]{:S(2)}, u32[]{:S(2)}) collective-permute-start(s32[16,1024]{1,0:T(8,128)S(1)} %bitcast.42), channel_id=1, source_target_pairs={{0,48},{16,32},{32,16},{48,0},{1,49},{17,33},{33,17},{49,1},{2,50}... | collective-permute-start | bytes 196616 | tf_op jit(solution)/shard_map/ppermute | solution.py:159
  19.0 0.6 copy.48
  19.7 0.6 copy.49
  20.3 44.7 %all-gather.6 = f16[32,64,512]{2,1,0:T(8,128)(2,1)S(1)} all-gather(f16[2,64,512]{2,1,0:T(8,128)(2,1)S(1)} %fusion), channel_id=2, replica_groups=mesh['ex'=8,'x'=4,'z'=16] {'z'}, dimensions={0}, use_global_device_ids=true | all-gather | bytes 2228224 | tf_op jit(solution)/shard_map/all_gather | solution.py:151
  65.0 1.8 %convert_convert_fusion = bf16[32,64,512]{2,1,0:T(8,128)(2,1)} fusion(f16[32,64,512]{2,1,0:T(8,128)(2,1)S(1)} %all-gather.6), kind=kLoop, calls=%fused_computation | loop fusion | flops 2097152 | bytes 4194304 | tf_op jit(solution)/shard_map/convert_element_type | solution.py:152
  66.8 0.7 pad_add_fusion.pos_ref
  67.5 0.0 collective-permute-done.w1
  67.5 0.0 collective-permute-done.1.w2
  67.5 0.6 copy-done.1
  68.1 0.0 copy-done.2
  68.2 0.0 copy-done.3
  68.2 5.3 %prepare_signs.1 = (bf16[256,512]{1,0:T(8,128)(2,1)}, bf16[16,256,512]{2,1,0:T(8,128)(2,1)}, f32[16,4,512]{2,1,0:T(4,128)}, bf16[4,1024,256]{2,1,0:T(8,128)(2,1)}) custom-call(s32[2]{0:T(128)} %pad_add_fusion.pos_ref, s32[16,512]{1,0:T(8,128)} %bitcast.38, s32[16,1024]{1,0:T(8,128)} %bitcast.37, s32[16,1024]{1,0:T(8,128)} %copy-done.1, ...), custom_call_target="tpu_custom_call" | custom-call | flops 41943040 | bytes 8388608 | tf_op jit(solution)/shard_map/prepare_signs/pallas_call | solution.py:165
  73.5 18.1 %gradient_transform_sample.1 = f32[16,4,2,128]{3,2,1,0:T(2,128)} custom-call(s32[2]{0:T(128)} %pad_add_fusion.pos_ref, s32[16,512]{1,0:T(8,128)} %bitcast.39, f32[16,4,512]{2,1,0:T(4,128)} %get-tuple-element.9.js_ref, bf16[256,512]{1,0:T(8,128)(2,1)} %get-tuple-element.10.had_ref, bf16[16,2,64,512]{3,2,1,0:T(8,128)(2,1)} %bitcast.35, ...), custom_call_target="tpu_custom_call" | custom-call | flops 7000000000 | bytes 16777216 | tf_op jit(solution)/shard_map/gradient_transform_sample/pallas_call | solution.py:182
  91.6 18.2 %all_to_all.10 = f32[16,4,2,128]{3,2,1,0:T(2,128)S(1)} all-to-all(f32[16,4,2,128]{3,2,1,0:T(2,128)} %gradient_transform_sample.1), channel_id=1, replica_groups=mesh['ex'=8,'x'=4,'z'=16] {'z'}, dimensions={0} | all-to-all | bytes 131072 | tf_op jit(solution)/shard_map/all_to_all | solution.py:205
  109.8 0.6 broadcast_in_dim.2
  110.5 15.0 %all-to-all-start.1 = ((f32[32,2,128]{2,1,0:T(2,128)}), f32[32,2,128]{2,1,0:T(2,128)S(1)}, u32[]{:S(2)}, u32[]{:S(2)}) async-start(f32[32,2,128]{2,1,0:T(2,128)} %bitcast.12), calls=%async_computation.1 | async-start | bytes 65536 | tf_op jit(solution)/shard_map/all_to_all | solution.py:208
  125.5 7.2 %all-to-all-done.1 = f32[32,2,128]{2,1,0:T(2,128)S(1)} async-done(((f32[32,2,128]{2,1,0:T(2,128)}), f32[32,2,128]{2,1,0:T(2,128)S(1)}, u32[]{:S(2)}, u32[]{:S(2)}) %all-to-all-start.1) | async-done | bytes 32800 | tf_op jit(solution)/shard_map/all_to_all | solution.py:208
  132.7 0.1 reduce_sum.29
  132.8 0.6 fusion.2
  (17 shorter events, 0.2 us)
Async XLA Ops:
  6.5 13.1 %copy-start.4 = (s32[8192]{0:T(1024)S(1)}, s32[8192]{0:T(1024)}, u32[]{:S(2)}) copy-start(s32[8192]{0:T(1024)} %param.7) | copy-start | bytes 98308
  6.5 13.7 %copy-start = (bf16[2,512,64]{1,2,0:T(8,128)(2,1)S(1)}, bf16[2,512,64]{1,2,0:T(8,128)(2,1)}, u32[]{:S(2)}) copy-start(bf16[2,512,64]{1,2,0:T(8,128)(2,1)} %param.5) | copy-start | bytes 393220
  6.5 67.0 %all-gather.5.cloned.1.call-start = ((), (), s32[]{:S(2)}) async-start(), calls=%async_computation.2 | async-start | bytes 2621440 | tf_op jit(solution)/shard_map/all_gather | solution.py:148
  8.7 58.8 %collective-permute-start = (s32[16,1024]{1,0:T(8,128)S(1)}, s32[16,1024]{1,0:T(8,128)S(1)}, u32[]{:S(2)}, u32[]{:S(2)}) collective-permute-start(s32[16,1024]{1,0:T(8,128)S(1)} %bitcast.40), channel_id=1, source_target_pairs={{0,16},{16,0},{32,48},{48,32},{1,17},{17,1},{33,49},{49,33},{2,18}... | collective-permute-start | bytes 196616 | tf_op jit(solution)/shard_map/ppermute | solution.py:159
  12.7 54.8 %collective-permute-start.1 = (s32[16,1024]{1,0:T(8,128)S(1)}, s32[16,1024]{1,0:T(8,128)S(1)}, u32[]{:S(2)}, u32[]{:S(2)}) collective-permute-start(s32[16,1024]{1,0:T(8,128)S(1)} %bitcast.41), channel_id=1, source_target_pairs={{0,32},{16,48},{32,0},{48,16},{1,33},{17,49},{33,1},{49,17},{2,34}... | collective-permute-start | bytes 196616 | tf_op jit(solution)/shard_map/ppermute | solution.py:159
  17.1 50.4 %collective-permute-start.2 = (s32[16,1024]{1,0:T(8,128)S(1)}, s32[16,1024]{1,0:T(8,128)S(1)}, u32[]{:S(2)}, u32[]{:S(2)}) collective-permute-start(s32[16,1024]{1,0:T(8,128)S(1)} %bitcast.42), channel_id=1, source_target_pairs={{0,48},{16,32},{32,16},{48,0},{1,49},{17,33},{33,17},{49,1},{2,50}... | collective-permute-start | bytes 196616 | tf_op jit(solution)/shard_map/ppermute | solution.py:159
  67.5 0.6 copy-start.1
  67.5 0.7 copy-start.2
  67.5 0.7 copy-start.3
  110.5 22.2 %all-to-all-start.1 = ((f32[32,2,128]{2,1,0:T(2,128)}), f32[32,2,128]{2,1,0:T(2,128)S(1)}, u32[]{:S(2)}, u32[]{:S(2)}) async-start(f32[32,2,128]{2,1,0:T(2,128)} %bitcast.12), calls=%async_computation.1 | async-start | bytes 65536 | tf_op jit(solution)/shard_map/all_to_all | solution.py:208
Sparse Core Ops, SparseCore 0:
  9.5 43.7 all-gather.4

commit v2 on v1

v2 whole, which is shorter than its diff:
```python
import jax
import jax.numpy as jnp
from jax import lax
from jax.experimental import pallas as pl
from jax.experimental.pallas import tpu as pltpu
from jax.sharding import Mesh, PartitionSpec as P

D = 4096
FF = 16384
TOK = 512
NX = 4
NZ = 16
ROWS = D // NX
COLS = 256
LOW = 64
TILES = ROWS // LOW
KDEV = 128
SAMPLES = NX * KDEV
WIRE = 131072.0
SCALE = 1.0 / 8192.0 / WIRE
VMEM_BYTES = 56 * 1024 * 1024


def sign_of(bits):
    bits = bits ^ (bits >> 4)
    bits = bits ^ (bits >> 2)
    bits = bits ^ (bits >> 1)
    return (1 - 2 * (bits & 1)).astype(jnp.float32)


def split(values):
    high = values.astype(jnp.bfloat16)
    return high, (values - high.astype(jnp.float32)).astype(jnp.bfloat16)


def main_kernel(
    idx_ref, w0, w1, w2, w3, grads_in, acts_in,
    out_ref, grads, acts, words, signs, tiles, grad_sem, act_sem,
):
    x, z = lax.axis_index("x"), lax.axis_index("z")
    flip = lax.axis_index("core") * (NZ - 1)

    def load(source, target, sem):
        pltpu.make_async_copy(source, target, sem).start()

    def wait(target, sem):
        pltpu.make_async_copy(target, target, sem).wait()

    for example in range(2):
        for i in range(NZ):
            load(grads_in.at[i ^ flip, example], grads.at[example, i], grad_sem.at[example, i])
        load(acts_in.at[0, example], acts.at[example, 0], act_sem.at[example, 0])
    for block in range(1, NX):
        for example in range(2):
            load(acts_in.at[block, example], acts.at[example, block], act_sem.at[example, block])

    row = lax.broadcasted_iota(jnp.int32, (COLS, COLS), 0)
    col = lax.broadcasted_iota(jnp.int32, (COLS, COLS), 1)
    had = sign_of(row & col).astype(jnp.bfloat16)
    had = jnp.concatenate([had, had], axis=1)
    byte_row = lax.broadcasted_iota(jnp.int32, (32, COLS), 0)
    byte_col = lax.broadcasted_iota(jnp.int32, (32, COLS), 1)
    spread = (byte_row == (byte_col >> 4) + 16 * ((byte_col >> 3) & 1)).astype(jnp.float32)
    spread = spread.astype(jnp.bfloat16)
    for delta, w_ref in enumerate((w0, w1, w2, w3)):
        words[x ^ delta] = w_ref[...]

    for example in range(2):
        for i in range(NZ):
            wait(grads.at[example, i], grad_sem.at[example, i])

    def block_body(block, carry):
        word = words[block]
        two = jnp.concatenate([word & 255, (word >> 8) & 255], axis=0)
        two = two.astype(jnp.float32).astype(jnp.bfloat16)
        value = lax.dot_general(
            two, spread, (((0,), (0,)), ((), ())), preferred_element_type=jnp.float32
        )
        shift = lax.broadcasted_iota(jnp.int32, (ROWS, COLS), 1) & 7
        signs[block] = (1 - 2 * ((value.astype(jnp.int32) >> shift) & 1)).astype(jnp.float32)
        for example in range(2):
            wait(acts.at[example, block], act_sem.at[example, block])
            grad = jnp.dot(
                grads[example].reshape(ROWS, TOK),
                acts[example, block],
                preferred_element_type=jnp.float32,
            )
            signed = grad * signs[block]
            parts = []
            for b in range(4):
                both = jnp.concatenate(split(signed[b * COLS : (b + 1) * COLS]), axis=0)
                parts.append(jnp.dot(had, both, preferred_element_type=jnp.float32))
            p0, p1 = parts[0] + parts[1], parts[0] - parts[1]
            p2, p3 = parts[2] + parts[3], parts[2] - parts[3]
            for a, value in enumerate((p0 + p2, p1 + p3, p0 - p2, p1 - p3)):
                value = value.astype(jnp.bfloat16)
                for i in range(4):
                    tiles[4 * a + i, example, block] = value[i * LOW : (i + 1) * LOW]
        return carry

    lax.fori_loop(0, NX, block_body, 0, unroll=True)

    def tile_body(tile, carry):
        idx = jnp.concatenate([idx_ref[pl.ds(tx * NZ + tile, 1), :] for tx in range(NX)], axis=1)
        line = lax.broadcasted_iota(jnp.int32, (16, SAMPLES), 0)
        low_signs = sign_of(line & idx)
        high_signs = sign_of(line & (idx >> 4))
        weights = jnp.concatenate(
            [(low_signs * high_signs[a : a + 1]).astype(jnp.bfloat16) for a in range(16)], axis=0
        )
        sign_z = sign_of((idx >> 8) & 15 & z)
        sign_1 = sign_of((idx >> 12) & 1)
        sign_2 = sign_of((idx >> 13) & 1)
        chosen = lax.broadcasted_iota(jnp.int32, (LOW, SAMPLES), 0) == ((idx >> 14) & (LOW - 1))
        left = tiles[tile].reshape(2 * NX * LOW, COLS)
        both = jnp.dot(left, weights, preferred_element_type=jnp.float32)
        for example in range(2):
            b0, b1, b2, b3 = [
                both[(example * NX + j) * LOW : (example * NX + j + 1) * LOW] for j in range(NX)
            ]
            total = (b0 + b1 * sign_1) + (b2 + b3 * sign_1) * sign_2
            picked = jnp.sum(jnp.where(chosen, total, 0.0), axis=0, keepdims=True) * sign_z
            for tx in range(NX):
                out_ref[tile, tx, pl.ds(example, 1), :] = picked[:, tx * KDEV : (tx + 1) * KDEV]
        return carry

    lax.fori_loop(0, TILES, tile_body, 0, unroll=4)


def shards(activations, out_grads, sign_words, indices):
    ex = ("y", "core")
    ex_size = lax.axis_size(ex)
    x = lax.axis_index("x")

    acts = lax.all_gather(activations, "x", axis=0, tiled=False)

    words = jnp.transpose(sign_words, (1, 0))
    own_words = []
    for delta in range(NX):
        part = lax.dynamic_slice_in_dim(words, (x ^ delta) * ROWS, ROWS, axis=1)
        if delta:
            part = lax.ppermute(part, "x", [(i, i ^ delta) for i in range(NX)])
        own_words.append(part)

    wire = jnp.transpose(out_grads, (0, 2, 1)).astype(jnp.float32) * WIRE
    wire = lax.all_gather(
        wire.astype(jnp.float16), ("core", "z"), axis=0, tiled=False,
        axis_index_groups=[list(range(NZ)), list(range(2 * NZ - 1, NZ - 1, -1))],
    )
    grads = wire.astype(jnp.float32).astype(jnp.bfloat16)

    vmem = pl.BlockSpec(memory_space=pltpu.VMEM)
    anywhere = pl.BlockSpec(memory_space=pl.ANY)
    values = pl.pallas_call(
        main_kernel,
        out_shape=jax.ShapeDtypeStruct((TILES, NX, 2, KDEV), jnp.float32),
        in_specs=[vmem] * 5 + [anywhere] * 2,
        out_specs=vmem,
        scratch_shapes=[
            pltpu.VMEM((2, NZ, LOW, TOK), jnp.bfloat16),
            pltpu.VMEM((2, NX, TOK, COLS), jnp.bfloat16),
            pltpu.VMEM((NX, FF // 1024, ROWS), jnp.int32),
            pltpu.VMEM((NX, ROWS, COLS), jnp.float32),
            pltpu.VMEM((TILES, 2, NX, LOW, COLS), jnp.bfloat16),
            pltpu.SemaphoreType.DMA((2, NZ)),
            pltpu.SemaphoreType.DMA((2, NX)),
        ],
        compiler_params=pltpu.CompilerParams(vmem_limit_bytes=VMEM_BYTES),
        cost_estimate=pl.CostEstimate(
            flops=7 * 10**9, bytes_accessed=8 * 1024 * 1024, transcendentals=0
        ),
        name="gradient_transform_sample",
    )(indices.reshape(NX * NZ, KDEV), *own_words, grads, acts)

    along_z = lax.all_to_all(values, "z", split_axis=0, concat_axis=0, tiled=True)
    own_indices = lax.dynamic_index_in_dim(
        indices.reshape(NX, NZ, KDEV), lax.axis_index("z"), axis=1, keepdims=False
    )
    half = jnp.sum(along_z, axis=0) * (sign_of((own_indices >> 24) & x) * SCALE)[:, None, :]
    sent = jnp.broadcast_to(half[None], (ex_size, NX, 2, KDEV)).reshape(ex_size * NX, 2, KDEV)
    received = lax.all_to_all(sent, ex + ("x",), split_axis=0, concat_axis=0, tiled=True)
    raw = jnp.sum(received.reshape(ex_size, NX, 2, KDEV), axis=1)
    own_raw = lax.dynamic_index_in_dim(raw, lax.axis_index(ex), axis=0, keepdims=False)
    return own_raw - jnp.sum(raw, axis=(0, 1))[None, :] / (2 * ex_size)


def solution(mesh):
    grid = Mesh(mesh.devices.reshape(-1, 2, NX, NZ), ("y", "core", "x", "z"))
    ex, par = ("y", "core"), ("x", "z")
    return jax.shard_map(
        shards,
        mesh=grid,
        in_specs=(P(ex, None, par), P(ex, None, par), P(None, par), P()),
        out_specs=P(ex, par),
        check_vma=False,
    )
```

time: 141 us -> 133 us (0.943)
  blocking collectives: 62.9 us -> 43.3 us
  waiting for transfers between devices: 7.93 us -> 18.8 us
  starting transfers between devices: 25.2 us -> 33.3 us
  Pallas kernels: 23.4 us -> 16.7 us
    all_to_all x1 -> x0, blocking collectives: 18.2 us -> none  [shards(): lax.all_to_all(values, 'z', split_axis=0, concat_axis=0, tiled=True)]
    all_to_all x1 -> x2, waiting for transfers between devices: 7.21 us -> 18 us  [the longest x1 10.8 us: shards(): lax.all_to_all(values, 'z', split_axis=0, concat_axis=0, tiled=True)]
    all_to_all x1 -> x2, starting transfers between devices: 15 us -> 23.1 us  [the longest x1 15.5 us: shards(): lax.all_to_all(sent, ex + ('x',), split_axis=0, concat_axis=0, tiled=True)]
    pallas_call x1 -> x0, Pallas kernels: 5.29 us -> none  [shards(): pl.pallas_call(prep_kernel, out_shape=[jax.ShapeDtypeStruct((COLS, 2 * CO...]
    dynamic_slice x1 -> x2, local copies, waits for them, and re-layouts: 0.27 us -> 2.31 us  [the longest x1 1.58 us: shards(): part = lax.dynamic_slice_in_dim(words, (x ^ delta) * ROWS, ROWS, axis=1)]
    reshape x2 -> x0, local copies, waits for them, and re-layouts: 1.74 us -> none  [the longest x1 1.13 us: shards(): words = jnp.transpose(sign_words, (1, 0)).reshape(FF // 1024, NX, ROWS)]
    pallas_call x1, Pallas kernels: 18.1 us -> 16.7 us  [shards(): pl.pallas_call(main_kernel, out_shape=jax.ShapeDtypeStruct((TILES, NX, 2,...]
  transfers between devices with their start and end apart: 5 -> 6, of which waited for: 1 -> 2; matrix products, arithmetic and copies ran while one was open for 4% -> 4% of each run, Pallas kernels for 4% -> 0%
where the time goes in v2:
time: 133 us
  blocking collectives  43.3 us (33%)
  starting transfers between devices  33.3 us (25%)
  waiting for transfers between devices  18.8 us (14%)
  Pallas kernels  16.7 us (13%)
  between operations  13.5 us (10%)
  local copies, waits for them, and re-layouts  3.55 us (3%)
  other arithmetic  3.42 us (3%)
    all_gather x1, blocking collectives, shards(): lax.all_gather(wire.astype(jnp.float16), ('core', 'z'), axis=0, tiled=Fal...  43.3 us
    pallas_call x1, Pallas kernels, shards(): pl.pallas_call(main_kernel, out_shape=jax.ShapeDtypeStruct((TILES, NX, 2,...  16.7 us
    all_to_all x1, starting transfers between devices, shards(): lax.all_to_all(sent, ex + ('x',), split_axis=0, concat_axis=0, tiled=True)  15.5 us
    all_to_all x1, waiting for transfers between devices, shards(): lax.all_to_all(values, 'z', split_axis=0, concat_axis=0, tiled=True)  10.8 us
    ppermute x3, starting transfers between devices, shards(): part = lax.ppermute(part, 'x', [(i, i ^ delta) for i in range(NX)])  10.2 us
    all_to_all x1, starting transfers between devices, shards(): lax.all_to_all(values, 'z', split_axis=0, concat_axis=0, tiled=True)  7.61 us
    all_to_all x1, waiting for transfers between devices, shards(): lax.all_to_all(sent, ex + ('x',), split_axis=0, concat_axis=0, tiled=True)  7.21 us
  transfers between devices with their start and end apart: 6, of which 2 were waited for; matrix products, arithmetic and copies ran while one was open for 4% of the time, Pallas kernels for 0%

profile of v2, /device:TPU:1, one launch (start us, length us, event | category | flops | bytes accessed | tf_op | source)
XLA Modules:
  0.0 132.6 jit_solution(12006666429252709136)
XLA Ops:
  6.5 0.7 all-gather.5.cloned.1.call-update
  7.3 1.6 %dynamic-slice_bitcast_fusion = (s32[16,1024]{1,0:T(8,128)S(1)}, s32[16,1024]{1,0:T(8,128)S(1)}, s32[16,1024]{1,0:T(8,128)}, s32[16,1024]{1,0:T(8,128)S(1)}) fusion(s32[4096,16]{0,1:T(8,128)} %param.6, s32[]{:T(128)S(6)} %select_n.23, s32[]{:T(128)S(6)} %select_n.21, s32[]{:T(128)S(6)} %select_n.20, s32[]{:T(128)S(6)} %select_n.22), kind=kLoop, calls=%fused_computation.3 | loop fusion | bytes 524304 | tf_op jit(solution)/shard_map/dynamic_slice | solution.py:140
  8.9 3.9 %collective-permute-start = (s32[16,1024]{1,0:T(8,128)S(1)}, s32[16,1024]{1,0:T(8,128)S(1)}, u32[]{:S(2)}, u32[]{:S(2)}) collective-permute-start(s32[16,1024]{1,0:T(8,128)S(1)} %get-tuple-element.6), channel_id=1, source_target_pairs={{0,16},{16,0},{32,48},{48,32},{1,17},{17,1},{33,49},{49,33},{2,18}... | collective-permute-start | bytes 196616 | tf_op jit(solution)/shard_map/ppermute | solution.py:142
  12.8 4.4 %collective-permute-start.1 = (s32[16,1024]{1,0:T(8,128)S(1)}, s32[16,1024]{1,0:T(8,128)S(1)}, u32[]{:S(2)}, u32[]{:S(2)}) collective-permute-start(s32[16,1024]{1,0:T(8,128)S(1)} %get-tuple-element.8), channel_id=1, source_target_pairs={{0,32},{16,48},{32,0},{48,16},{1,33},{17,49},{33,1},{49,17},{2,34}... | collective-permute-start | bytes 196616 | tf_op jit(solution)/shard_map/ppermute | solution.py:142
  17.2 1.9 %collective-permute-start.2 = (s32[16,1024]{1,0:T(8,128)S(1)}, s32[16,1024]{1,0:T(8,128)S(1)}, u32[]{:S(2)}, u32[]{:S(2)}) collective-permute-start(s32[16,1024]{1,0:T(8,128)S(1)} %get-tuple-element.5), channel_id=1, source_target_pairs={{0,48},{16,32},{32,16},{48,0},{1,49},{17,33},{33,17},{49,1},{2,50}... | collective-permute-start | bytes 196616 | tf_op jit(solution)/shard_map/ppermute | solution.py:142
  19.1 0.9 fusion
  20.0 43.3 %all-gather.6 = f16[32,64,512]{2,1,0:T(8,128)(2,1)S(1)} all-gather(f16[2,64,512]{2,1,0:T(8,128)(2,1)S(1)} %fusion), channel_id=2, replica_groups={{0,1,2,3,4,5,6,7,8,9,10,11,12,13,14,15},{79,78,77,76,75,74,73,72,71,70,..., dimensions={0}, use_global_device_ids=true | all-gather | bytes 2228224 | tf_op jit(solution)/shard_map/all_gather | solution.py:146
  63.4 1.8 %convert_convert_fusion = bf16[32,64,512]{2,1,0:T(8,128)(2,1)} fusion(f16[32,64,512]{2,1,0:T(8,128)(2,1)S(1)} %all-gather.6), kind=kLoop, calls=%fused_computation | loop fusion | flops 2097152 | bytes 4194304 | tf_op jit(solution)/shard_map/convert_element_type | solution.py:150
  65.1 0.0 collective-permute-done.w1
  65.2 0.0 collective-permute-done.1.w2
  65.2 0.0 collective-permute-done.2.w3
  65.2 0.0 all-gather.5.cloned.1.call-done
  65.2 0.5 copy-done
  65.8 0.0 copy-done.1
  65.8 0.0 copy-done.2
  65.8 16.7 %gradient_transform_sample.1 = f32[16,4,2,128]{3,2,1,0:T(2,128)} custom-call(s32[64,128]{1,0:T(8,128)} %bitcast.28, s32[16,1024]{1,0:T(8,128)} %get-tuple-element.7.w0, s32[16,1024]{1,0:T(8,128)} %copy-done, s32[16,1024]{1,0:T(8,128)} %copy-done.1, s32[16,1024]{1,0:T(8,128)} %copy-done.2, bf16[16,2,64,512]{3,2,1,0:T(8,128)(2,1)} %bitcast.26, ...), custom_call_target="tpu_custom_call" | custom-call | flops 7000000000 | bytes 8388608 | tf_op jit(solution)/shard_map/gradient_transform_sample/pallas_call | solution.py:154
  82.5 7.6 %all-to-all-start = ((f32[16,4,2,128]{3,2,1,0:T(2,128)}), f32[16,4,2,128]{3,2,1,0:T(2,128)S(1)}, u32[]{:S(2)}, u32[]{:S(2)}) async-start(f32[16,4,2,128]{3,2,1,0:T(2,128)} %gradient_transform_sample.1), calls=%async_computation | async-start | bytes 131072 | tf_op jit(solution)/shard_map/all_to_all | solution.py:175
  90.1 0.7 constant_dynamic-slice_fusion.1
  90.9 10.8 %all-to-all-done = f32[16,4,2,128]{3,2,1,0:T(2,128)S(1)} async-done(((f32[16,4,2,128]{3,2,1,0:T(2,128)}), f32[16,4,2,128]{3,2,1,0:T(2,128)S(1)}, u32[]{:S(2)}, u32[]{:S(2)}) %all-to-all-start) | async-done | bytes 65568 | tf_op jit(solution)/shard_map/all_to_all | solution.py:175
  101.7 0.6 broadcast_in_dim.2
  102.4 15.5 %all-to-all-start.1 = ((f32[32,2,128]{2,1,0:T(2,128)}), f32[32,2,128]{2,1,0:T(2,128)S(1)}, u32[]{:S(2)}, u32[]{:S(2)}) async-start(f32[32,2,128]{2,1,0:T(2,128)} %bitcast.10), calls=%async_computation.1 | async-start | bytes 65536 | tf_op jit(solution)/shard_map/all_to_all | solution.py:181
  117.9 7.2 %all-to-all-done.1 = f32[32,2,128]{2,1,0:T(2,128)S(1)} async-done(((f32[32,2,128]{2,1,0:T(2,128)}), f32[32,2,128]{2,1,0:T(2,128)S(1)}, u32[]{:S(2)}, u32[]{:S(2)}) %all-to-all-start.1) | async-done | bytes 32800 | tf_op jit(solution)/shard_map/all_to_all | solution.py:181
  125.1 0.1 reduce_sum.29
  125.2 0.6 fusion.8
  (9 shorter events, 0.1 us)
Async XLA Ops:
  6.5 58.7 %all-gather.5.cloned.1.call-start = ((), (), s32[]{:S(2)}) async-start(), calls=%async_computation.2 | async-start | bytes 2621440 | tf_op jit(solution)/shard_map/all_gather | solution.py:135
  8.9 56.3 %collective-permute-start = (s32[16,1024]{1,0:T(8,128)S(1)}, s32[16,1024]{1,0:T(8,128)S(1)}, u32[]{:S(2)}, u32[]{:S(2)}) collective-permute-start(s32[16,1024]{1,0:T(8,128)S(1)} %get-tuple-element.6), channel_id=1, source_target_pairs={{0,16},{16,0},{32,48},{48,32},{1,17},{17,1},{33,49},{49,33},{2,18}... | collective-permute-start | bytes 196616 | tf_op jit(solution)/shard_map/ppermute | solution.py:142
  12.8 52.3 %collective-permute-start.1 = (s32[16,1024]{1,0:T(8,128)S(1)}, s32[16,1024]{1,0:T(8,128)S(1)}, u32[]{:S(2)}, u32[]{:S(2)}) collective-permute-start(s32[16,1024]{1,0:T(8,128)S(1)} %get-tuple-element.8), channel_id=1, source_target_pairs={{0,32},{16,48},{32,0},{48,16},{1,33},{17,49},{33,1},{49,17},{2,34}... | collective-permute-start | bytes 196616 | tf_op jit(solution)/shard_map/ppermute | solution.py:142
  17.2 48.0 %collective-permute-start.2 = (s32[16,1024]{1,0:T(8,128)S(1)}, s32[16,1024]{1,0:T(8,128)S(1)}, u32[]{:S(2)}, u32[]{:S(2)}) collective-permute-start(s32[16,1024]{1,0:T(8,128)S(1)} %get-tuple-element.5), channel_id=1, source_target_pairs={{0,48},{16,32},{32,16},{48,0},{1,49},{17,33},{33,17},{49,1},{2,50}... | collective-permute-start | bytes 196616 | tf_op jit(solution)/shard_map/ppermute | solution.py:142
  65.1 0.6 copy-start
  65.2 0.6 copy-start.1
  65.2 0.7 copy-start.2
  82.5 19.2 %all-to-all-start = ((f32[16,4,2,128]{3,2,1,0:T(2,128)}), f32[16,4,2,128]{3,2,1,0:T(2,128)S(1)}, u32[]{:S(2)}, u32[]{:S(2)}) async-start(f32[16,4,2,128]{3,2,1,0:T(2,128)} %gradient_transform_sample.1), calls=%async_computation | async-start | bytes 131072 | tf_op jit(solution)/shard_map/all_to_all | solution.py:175
  102.4 22.7 %all-to-all-start.1 = ((f32[32,2,128]{2,1,0:T(2,128)}), f32[32,2,128]{2,1,0:T(2,128)S(1)}, u32[]{:S(2)}, u32[]{:S(2)}) async-start(f32[32,2,128]{2,1,0:T(2,128)} %bitcast.10), calls=%async_computation.1 | async-start | bytes 65536 | tf_op jit(solution)/shard_map/all_to_all | solution.py:181
Sparse Core Ops, SparseCore 0:
  9.5 43.7 all-gather.4

commit v3 on v2

v3 whole, which is shorter than its diff:
```python
import jax
import jax.numpy as jnp
from jax import lax
from jax.experimental import pallas as pl
from jax.experimental.pallas import tpu as pltpu
from jax.sharding import Mesh, PartitionSpec as P

D = 4096
FF = 16384
TOK = 512
NX = 4
NZ = 16
Z = ("zh", "zl")
ROWS = D // NX
COLS = 256
LOW = 64
TILES = ROWS // LOW
KDEV = 128
SAMPLES = NX * KDEV
WIRE = 131072.0
SCALE = 1.0 / 8192.0 / WIRE
VMEM_BYTES = 36 * 1024 * 1024


def sign_of(bits):
    bits = bits ^ (bits >> 4)
    bits = bits ^ (bits >> 2)
    bits = bits ^ (bits >> 1)
    return (1 - 2 * (bits & 1)).astype(jnp.float32)


def split(values):
    high = values.astype(jnp.bfloat16)
    return high, (values - high.astype(jnp.float32)).astype(jnp.bfloat16)


def pack_kernel(acts_ref, words_ref, own_ref, *payloads):
    x = lax.axis_index("x")
    for delta, ref in enumerate((own_ref,) + payloads):
        start = pl.multiple_of((x ^ delta) * ROWS, ROWS)
        word = words_ref[:, pl.ds(start, ROWS)]
        two = jnp.concatenate([word & 255, (word >> 8) & 255], axis=0)
        two = two.astype(jnp.float32).astype(jnp.bfloat16)
        first = 2 * TOK if delta else 0
        for q in range(4):
            ref[pl.ds(first + 32 * q, 32), :] = two[:, q * COLS : (q + 1) * COLS]
        if delta:
            for example in range(2):
                ref[pl.ds(example * TOK, TOK), :] = acts_ref[example]


def main_kernel(idx_ref, grads, own_bytes, own_acts, p1, p2, p3, out_ref, signs, tiles):
    x, z = lax.axis_index("x"), lax.axis_index(Z)

    row = lax.broadcasted_iota(jnp.int32, (COLS, COLS), 0)
    col = lax.broadcasted_iota(jnp.int32, (COLS, COLS), 1)
    had = sign_of(row & col).astype(jnp.bfloat16)
    had = jnp.concatenate([had, had], axis=1)
    byte_row = lax.broadcasted_iota(jnp.int32, (32, COLS), 0)
    byte_col = lax.broadcasted_iota(jnp.int32, (32, COLS), 1)
    spread = (byte_row == (byte_col >> 4) + 16 * ((byte_col >> 3) & 1)).astype(jnp.float32)
    spread = spread.astype(jnp.bfloat16)
    shift = lax.broadcasted_iota(jnp.int32, (COLS, COLS), 1) & 7

    for delta, payload in enumerate((None, p1, p2, p3)):
        block = x ^ delta
        for q in range(4):
            if delta:
                two = payload[pl.ds(2 * TOK + 32 * q, 32), :]
            else:
                two = own_bytes[pl.ds(32 * q, 32), :]
            value = lax.dot_general(
                two, spread, (((0,), (0,)), ((), ())), preferred_element_type=jnp.float32
            )
            bit = (value.astype(jnp.int32) >> shift) & 1
            signs[delta, pl.ds(q * COLS, COLS), :] = (1 - 2 * bit).astype(jnp.float32)
        for example in range(2):
            if delta:
                act = payload[pl.ds(example * TOK, TOK), :]
            else:
                act = own_acts[example]
            grad = jnp.dot(grads[example], act, preferred_element_type=jnp.float32)
            signed = grad * signs[delta]
            parts = []
            for b in range(4):
                both = jnp.concatenate(split(signed[b * COLS : (b + 1) * COLS]), axis=0)
                parts.append(jnp.dot(had, both, preferred_element_type=jnp.float32))
            p0_, p1_ = parts[0] + parts[1], parts[0] - parts[1]
            p2_, p3_ = parts[2] + parts[3], parts[2] - parts[3]
            for a, value in enumerate((p0_ + p2_, p1_ + p3_, p0_ - p2_, p1_ - p3_)):
                value = value.astype(jnp.bfloat16)
                for i in range(4):
                    tiles[4 * a + i, example, block] = value[i * LOW : (i + 1) * LOW]

    def tile_body(tile, carry):
        idx = jnp.concatenate([idx_ref[pl.ds(tx * NZ + tile, 1), :] for tx in range(NX)], axis=1)
        line = lax.broadcasted_iota(jnp.int32, (16, SAMPLES), 0)
        low_signs = sign_of(line & idx)
        high_signs = sign_of(line & (idx >> 4))
        weights = jnp.concatenate(
            [(low_signs * high_signs[a : a + 1]).astype(jnp.bfloat16) for a in range(16)], axis=0
        )
        sign_xz = sign_of(((idx >> 8) & 15 & z) | (((idx >> 24) & 3 & x) << 4))
        sign_1 = sign_of((idx >> 12) & 1)
        sign_2 = sign_of((idx >> 13) & 1)
        chosen = lax.broadcasted_iota(jnp.int32, (LOW, SAMPLES), 0) == ((idx >> 14) & (LOW - 1))
        left = tiles[tile].reshape(2 * NX * LOW, COLS)
        both = jnp.dot(left, weights, preferred_element_type=jnp.float32)
        for example in range(2):
            b0, b1, b2, b3 = [
                both[(example * NX + j) * LOW : (example * NX + j + 1) * LOW] for j in range(NX)
            ]
            total = (b0 + b1 * sign_1) + (b2 + b3 * sign_1) * sign_2
            picked = jnp.sum(jnp.where(chosen, total, 0.0), axis=0, keepdims=True) * sign_xz
            for tx in range(NX):
                out_ref[tx, tile & 3, tile >> 2, pl.ds(example, 1), :] = picked[:, tx * KDEV : (tx + 1) * KDEV]
        return carry

    lax.fori_loop(0, TILES, tile_body, 0, unroll=4)


def shards(activations, out_grads, sign_words, indices):
    ex = ("y", "core")
    ex_size = lax.axis_size(ex)
    vmem = pl.BlockSpec(memory_space=pltpu.VMEM)
    own_bytes, *payloads = pl.pallas_call(
        pack_kernel,
        out_shape=[jax.ShapeDtypeStruct((128, COLS), jnp.bfloat16)]
        + [jax.ShapeDtypeStruct((2 * TOK + 128, COLS), jnp.bfloat16)] * 3,
        in_specs=[vmem] * 2,
        out_specs=[vmem] * 4,
        compiler_params=pltpu.CompilerParams(vmem_limit_bytes=16 * 1024 * 1024),
        name="pack_columns_and_words",
    )(activations, jnp.transpose(sign_words, (1, 0)))
    payloads = [
        lax.ppermute(payload, "x", [(i, i ^ delta) for i in range(NX)])
        for delta, payload in enumerate(payloads, 1)
    ]

    wire = jnp.transpose(out_grads, (0, 2, 1)).astype(jnp.float32) * WIRE
    wire = lax.all_gather(wire.astype(jnp.float16), Z, axis=1, tiled=True)
    grads = wire.astype(jnp.float32).astype(jnp.bfloat16)

    values = pl.pallas_call(
        main_kernel,
        out_shape=jax.ShapeDtypeStruct((NX, 4, 4, 2, KDEV), jnp.float32),
        in_specs=[vmem] * 7,
        out_specs=vmem,
        scratch_shapes=[
            pltpu.VMEM((NX, ROWS, COLS), jnp.float32),
            pltpu.VMEM((TILES, 2, NX, LOW, COLS), jnp.bfloat16),
        ],
        compiler_params=pltpu.CompilerParams(vmem_limit_bytes=VMEM_BYTES),
        cost_estimate=pl.CostEstimate(
            flops=7 * 10**9, bytes_accessed=8 * 1024 * 1024, transcendentals=0
        ),
        name="gradient_transform_sample",
    )(indices.reshape(NX * NZ, KDEV), grads, own_bytes, activations, *payloads)

    near = lax.all_to_all(
        values.reshape(16, 4, 2, KDEV), ("x", "zl"), split_axis=0, concat_axis=0, tiled=True
    )
    half = jnp.sum(near, axis=0) * SCALE
    sent = jnp.broadcast_to(half[None], (ex_size, 4, 2, KDEV)).reshape(ex_size * 4, 2, KDEV)
    received = lax.all_to_all(sent, ex + ("zh",), split_axis=0, concat_axis=0, tiled=True)
    raw = jnp.sum(received.reshape(ex_size, 4, 2, KDEV), axis=1)
    own_raw = lax.dynamic_index_in_dim(raw, lax.axis_index(ex), axis=0, keepdims=False)
    return own_raw - jnp.sum(raw, axis=(0, 1))[None, :] / (2 * ex_size)


def solution(mesh):
    grid = Mesh(mesh.devices.reshape(-1, 2, NX, 4, 4), ("y", "core", "x") + Z)
    ex, par = ("y", "core"), ("x",) + Z
    return jax.shard_map(
        shards,
        mesh=grid,
        in_specs=(P(ex, None, par), P(ex, None, par), P(None, par), P()),
        out_specs=P(ex, par),
        check_vma=False,
    )
```

time: 133 us -> 114 us (0.86)
  between operations: 13.5 us -> 0.09 us
  blocking collectives: 43.3 us -> 55.6 us
  Pallas kernels: 16.7 us -> 9.5 us
  starting transfers between devices: 33.3 us -> 28.3 us
  waiting for transfers between devices: 18.8 us -> 14.4 us
  other arithmetic: 3.42 us -> 2.03 us
    all_to_all x0 -> x1, blocking collectives: none -> 11.1 us  [shards(): lax.all_to_all(values.reshape(16, 4, 2, KDEV), ('x', 'zl'), split_axis=0,...]
    pallas_call x1 -> x2, Pallas kernels: 16.7 us -> 9.5 us  [the longest x1 9.38 us: shards(): pl.pallas_call(main_kernel, out_shape=jax.ShapeDtypeStruct((NX, 4, 4, 2,...]
    all_to_all x2 -> x1, starting transfers between devices: 23.1 us -> 18.1 us  [shards(): lax.all_to_all(sent, ex + ('zh',), split_axis=0, concat_axis=0, tiled=True)]
    all_to_all x2 -> x1, waiting for transfers between devices: 18 us -> 14.4 us  [shards(): lax.all_to_all(sent, ex + ('zh',), split_axis=0, concat_axis=0, tiled=True)]
    dynamic_slice x2 -> x0, local copies, waits for them, and re-layouts: 2.31 us -> none  [the longest x1 1.58 us: shards(): part = lax.dynamic_slice_in_dim(words, (x ^ delta) * ROWS, ROWS, axis=1)]
    unnamed x6 -> x8, local copies, waits for them, and re-layouts: 0.62 us -> 2.59 us
    convert_element_type x1, other arithmetic: 1.78 us -> 0.41 us  [shards(): grads = wire.astype(jnp.float32).astype(jnp.bfloat16)]
  transfers between devices with their start and end apart: 6 -> 4, of which waited for: 2 -> 1; matrix products, arithmetic and copies ran while one was open for 4% -> 1% of each run, Pallas kernels for 0% -> 0%
where the time goes in v3:
time: 114 us; the launch traced here: 113 us
  blocking collectives  55.6 us (49%)
  starting transfers between devices  28.3 us (25%)
  waiting for transfers between devices  14.4 us (13%)
  Pallas kernels  9.5 us (8%)
  local copies, waits for them, and re-layouts  3.21 us (3%)
  other arithmetic  2.03 us (2%)
    all_gather x1, blocking collectives, shards(): wire = lax.all_gather(wire.astype(jnp.float16), Z, axis=1, tiled=True)  44.5 us
    all_to_all x1, starting transfers between devices, shards(): lax.all_to_all(sent, ex + ('zh',), split_axis=0, concat_axis=0, tiled=True)  18.1 us
    all_to_all x1, waiting for transfers between devices, shards(): lax.all_to_all(sent, ex + ('zh',), split_axis=0, concat_axis=0, tiled=True)  14.4 us
    all_to_all x1, blocking collectives, shards(): lax.all_to_all(values.reshape(16, 4, 2, KDEV), ('x', 'zl'), split_axis=0,...  11.1 us
    ppermute x3, starting transfers between devices, shards(): lax.ppermute(payload, 'x', [(i, i ^ delta) for i in range(NX)])  10.2 us
    pallas_call x1, Pallas kernels, shards(): pl.pallas_call(main_kernel, out_shape=jax.ShapeDtypeStruct((NX, 4, 4, 2,...  9.38 us
    unnamed x8, local copies, waits for them, and re-layouts  2.59 us
  transfers between devices with their start and end apart: 4, of which 1 were waited for; matrix products, arithmetic and copies ran while one was open for 1% of the time, Pallas kernels for 0%

profile of v3, /device:TPU:1, one launch (start us, length us, event | category | flops | bytes accessed | tf_op | source)
XLA Modules:
  0.0 113.2 jit_solution(3832167992513190223)
XLA Ops:
  0.0 0.0 copy-start
  0.0 1.0 copy-done
  1.0 0.0 copy-start.2
  1.0 0.9 copy-done.2
  2.0 0.1 pack_columns_and_words.1
  2.1 3.9 %collective-permute-start = (bf16[1152,256]{1,0:T(8,128)(2,1)S(1)}, bf16[1152,256]{1,0:T(8,128)(2,1)S(1)}, u32[]{:S(2)}, u32[]{:S(2)}) collective-permute-start(bf16[1152,256]{1,0:T(8,128)(2,1)S(1)} %get-tuple-element.10), channel_id=1, source_target_pairs={{0,16},{16,0},{32,48},{48,32},{1,17},{17,1},{33,49},{49,33},{2,18}... | collective-permute-start | bytes 1769480 | tf_op jit(solution)/shard_map/ppermute | solution.py:136
  6.1 4.4 %collective-permute-start.1 = (bf16[1152,256]{1,0:T(8,128)(2,1)S(1)}, bf16[1152,256]{1,0:T(8,128)(2,1)S(1)}, u32[]{:S(2)}, u32[]{:S(2)}) collective-permute-start(bf16[1152,256]{1,0:T(8,128)(2,1)S(1)} %get-tuple-element.11), channel_id=1, source_target_pairs={{0,32},{16,48},{32,0},{48,16},{1,33},{17,49},{33,1},{49,17},{2,34}... | collective-permute-start | bytes 1769480 | tf_op jit(solution)/shard_map/ppermute | solution.py:136
  10.4 1.9 %collective-permute-start.2 = (bf16[1152,256]{1,0:T(8,128)(2,1)S(1)}, bf16[1152,256]{1,0:T(8,128)(2,1)S(1)}, u32[]{:S(2)}, u32[]{:S(2)}) collective-permute-start(bf16[1152,256]{1,0:T(8,128)(2,1)S(1)} %get-tuple-element.12), channel_id=1, source_target_pairs={{0,48},{16,32},{32,16},{48,0},{1,49},{17,33},{33,17},{49,1},{2,50}... | collective-permute-start | bytes 1769480 | tf_op jit(solution)/shard_map/ppermute | solution.py:136
  12.4 0.9 fusion
  13.3 44.5 %all-gather.1 = f16[2,1024,512]{2,1,0:T(8,128)(2,1)S(1)} all-gather(f16[2,64,512]{2,1,0:T(8,128)(2,1)S(1)} %fusion), channel_id=1, replica_groups=mesh['y'=4,'core'=2,'x'=4,'zh'=4,'zl'=4] {'zh','zl'}, dimensions={1}, use_global_device_ids=true | all-gather | bytes 2228224 | tf_op jit(solution)/shard_map/all_gather | solution.py:141
  57.8 0.0 copy-start.1
  57.8 0.4 convert_convert_fusion.grads
  58.2 0.0 collective-permute-done.p1
  58.2 0.0 collective-permute-done.1.p2
  58.2 0.0 collective-permute-done.2.p3
  58.2 0.6 copy-done.1
  58.8 0.0 copy-done.3
  58.8 9.4 %gradient_transform_sample.1 = f32[4,4,4,2,128]{4,3,2,1,0:T(2,128)S(1)} custom-call(s32[64,128]{1,0:T(8,128)S(1)} %bitcast.14, bf16[2,1024,512]{2,1,0:T(8,128)(2,1)S(1)} %convert_convert_fusion.grads, bf16[128,256]{1,0:T(8,128)(2,1)S(1)} %get-tuple-element.9.own_bytes, bf16[2,512,256]{2,1,0:T(8,128)(2,1)S(1)} %copy-done.1, ...), custom_call_target="tpu_custom_call" | custom-call | flops 7000000000 | bytes 8388608 | tf_op jit(solution)/shard_map/gradient_transform_sample/pallas_call | solution.py:144
  68.2 11.1 %all_to_all.10 = f32[16,4,2,128]{3,2,1,0:T(2,128)S(1)} all-to-all(f32[16,4,2,128]{3,2,1,0:T(2,128)S(1)} %bitcast.13), channel_id=1, replica_groups=mesh['y'=4,'core'=2,'x'=4,'zh'=4,'zl'=4] {'x','zl'}, dimensions={0} | all-to-all | bytes 131072 | tf_op jit(solution)/shard_map/all_to_all | solution.py:160
  79.3 0.6 broadcast_in_dim.2
  80.0 18.1 %all-to-all-start.1 = ((f32[32,2,128]{2,1,0:T(2,128)}), f32[32,2,128]{2,1,0:T(2,128)S(1)}, u32[]{:S(2)}, u32[]{:S(2)}) async-start(f32[32,2,128]{2,1,0:T(2,128)} %bitcast.4), calls=%async_computation.1 | async-start | bytes 65536 | tf_op jit(solution)/shard_map/all_to_all | solution.py:165
  98.1 14.4 %all-to-all-done.1 = f32[32,2,128]{2,1,0:T(2,128)S(1)} async-done(((f32[32,2,128]{2,1,0:T(2,128)}), f32[32,2,128]{2,1,0:T(2,128)S(1)}, u32[]{:S(2)}, u32[]{:S(2)}) %all-to-all-start.1) | async-done | bytes 32800 | tf_op jit(solution)/shard_map/all_to_all | solution.py:165
  112.5 0.1 reduce_sum.29
  112.6 0.6 bitcast_subtract_fusion
  (5 shorter events, 0.1 us)
Async XLA Ops:
  0.0 1.0 copy-start
  1.0 0.9 copy-start.2
  2.1 56.1 %collective-permute-start = (bf16[1152,256]{1,0:T(8,128)(2,1)S(1)}, bf16[1152,256]{1,0:T(8,128)(2,1)S(1)}, u32[]{:S(2)}, u32[]{:S(2)}) collective-permute-start(bf16[1152,256]{1,0:T(8,128)(2,1)S(1)} %get-tuple-element.10), channel_id=1, source_target_pairs={{0,16},{16,0},{32,48},{48,32},{1,17},{17,1},{33,49},{49,33},{2,18}... | collective-permute-start | bytes 1769480 | tf_op jit(solution)/shard_map/ppermute | solution.py:136
  6.1 52.1 %collective-permute-start.1 = (bf16[1152,256]{1,0:T(8,128)(2,1)S(1)}, bf16[1152,256]{1,0:T(8,128)(2,1)S(1)}, u32[]{:S(2)}, u32[]{:S(2)}) collective-permute-start(bf16[1152,256]{1,0:T(8,128)(2,1)S(1)} %get-tuple-element.11), channel_id=1, source_target_pairs={{0,32},{16,48},{32,0},{48,16},{1,33},{17,49},{33,1},{49,17},{2,34}... | collective-permute-start | bytes 1769480 | tf_op jit(solution)/shard_map/ppermute | solution.py:136
  10.4 47.8 %collective-permute-start.2 = (bf16[1152,256]{1,0:T(8,128)(2,1)S(1)}, bf16[1152,256]{1,0:T(8,128)(2,1)S(1)}, u32[]{:S(2)}, u32[]{:S(2)}) collective-permute-start(bf16[1152,256]{1,0:T(8,128)(2,1)S(1)} %get-tuple-element.12), channel_id=1, source_target_pairs={{0,48},{16,32},{32,16},{48,0},{1,49},{17,33},{33,17},{49,1},{2,50}... | collective-permute-start | bytes 1769480 | tf_op jit(solution)/shard_map/ppermute | solution.py:136
  57.8 1.0 copy-start.1
  57.8 1.0 copy-start.3
  80.0 32.6 %all-to-all-start.1 = ((f32[32,2,128]{2,1,0:T(2,128)}), f32[32,2,128]{2,1,0:T(2,128)S(1)}, u32[]{:S(2)}, u32[]{:S(2)}) async-start(f32[32,2,128]{2,1,0:T(2,128)} %bitcast.4), calls=%async_computation.1 | async-start | bytes 65536 | tf_op jit(solution)/shard_map/all_to_all | solution.py:165

commit v4 on v3

--- a/solution.py
+++ b/solution.py
@@ -10,7 +10,6 @@
 TOK = 512
 NX = 4
 NZ = 16
-Z = ("zh", "zl")
 ROWS = D // NX
 COLS = 256
 LOW = 64
@@ -34,23 +33,37 @@
     return high, (values - high.astype(jnp.float32)).astype(jnp.bfloat16)
 
 
-def pack_kernel(acts_ref, words_ref, own_ref, *payloads):
+def pack_kernel(acts_in, words_in, *refs):
+    payloads, (words, packed, word_sem, act_sem, out_sem) = refs[:NX], refs[NX:]
     x = lax.axis_index("x")
-    for delta, ref in enumerate((own_ref,) + payloads):
+    copies = []
+    for delta in range(NX):
         start = pl.multiple_of((x ^ delta) * ROWS, ROWS)
-        word = words_ref[:, pl.ds(start, ROWS)]
+        source = words_in.at[:, pl.ds(start, ROWS)]
+        copies.append(pltpu.make_async_copy(source, words.at[delta], word_sem.at[delta]))
+    for delta in range(NX):
+        for example in range(2):
+            target = payloads[delta].at[pl.ds(example * TOK, TOK)]
+            sem = act_sem.at[delta, example]
+            copies.append(pltpu.make_async_copy(acts_in.at[example], target, sem))
+    for copy in copies:
+        copy.start()
+    for delta in range(NX):
+        copies[delta].wait()
+        word = words[delta]
         two = jnp.concatenate([word & 255, (word >> 8) & 255], axis=0)
         two = two.astype(jnp.float32).astype(jnp.bfloat16)
-        first = 2 * TOK if delta else 0
         for q in range(4):
-            ref[pl.ds(first + 32 * q, 32), :] = two[:, q * COLS : (q + 1) * COLS]
-        if delta:
-            for example in range(2):
-                ref[pl.ds(example * TOK, TOK), :] = acts_ref[example]
+            packed[delta, pl.ds(32 * q, 32), :] = two[:, q * COLS : (q + 1) * COLS]
+        target = payloads[delta].at[pl.ds(2 * TOK, 128)]
+        copies.append(pltpu.make_async_copy(packed.at[delta], target, out_sem.at[delta]))
+        copies[-1].start()
+    for copy in copies[NX:]:
+        copy.wait()
 
 
-def main_kernel(idx_ref, grads, own_bytes, own_acts, p1, p2, p3, out_ref, signs, tiles):
-    x, z = lax.axis_index("x"), lax.axis_index(Z)
+def main_kernel(idx_ref, grads, p0, p1, p2, p3, out_ref, signs, tiles):
+    x, z = lax.axis_index("x"), lax.axis_index("z")
 
     row = lax.broadcasted_iota(jnp.int32, (COLS, COLS), 0)
     col = lax.broadcasted_iota(jnp.int32, (COLS, COLS), 1)
@@ -62,23 +75,17 @@
     spread = spread.astype(jnp.bfloat16)
     shift = lax.broadcasted_iota(jnp.int32, (COLS, COLS), 1) & 7
 
-    for delta, payload in enumerate((None, p1, p2, p3)):
+    for delta, payload in enumerate((p0, p1, p2, p3)):
         block = x ^ delta
         for q in range(4):
-            if delta:
-                two = payload[pl.ds(2 * TOK + 32 * q, 32), :]
-            else:
-                two = own_bytes[pl.ds(32 * q, 32), :]
+            two = payload[pl.ds(2 * TOK + 32 * q, 32), :]
             value = lax.dot_general(
                 two, spread, (((0,), (0,)), ((), ())), preferred_element_type=jnp.float32
             )
             bit = (value.astype(jnp.int32) >> shift) & 1
             signs[delta, pl.ds(q * COLS, COLS), :] = (1 - 2 * bit).astype(jnp.float32)
         for example in range(2):
-            if delta:
-                act = payload[pl.ds(example * TOK, TOK), :]
-            else:
-                act = own_acts[example]
+            act = payload[pl.ds(example * TOK, TOK), :]
             grad = jnp.dot(grads[example], act, preferred_element_type=jnp.float32)
             signed = grad * signs[delta]
             parts = []
@@ -113,7 +120,7 @@
             total = (b0 + b1 * sign_1) + (b2 + b3 * sign_1) * sign_2
             picked = jnp.sum(jnp.where(chosen, total, 0.0), axis=0, keepdims=True) * sign_xz
             for tx in range(NX):
-                out_ref[tx, tile & 3, tile >> 2, pl.ds(example, 1), :] = picked[:, tx * KDEV : (tx + 1) * KDEV]
+                out_ref[tile, tx, pl.ds(example, 1), :] = picked[:, tx * KDEV : (tx + 1) * KDEV]
         return carry
 
     lax.fori_loop(0, TILES, tile_body, 0, unroll=4)
@@ -123,28 +130,38 @@
     ex = ("y", "core")
     ex_size = lax.axis_size(ex)
     vmem = pl.BlockSpec(memory_space=pltpu.VMEM)
-    own_bytes, *payloads = pl.pallas_call(
+    hbm = pl.BlockSpec(memory_space=pltpu.HBM)
+    payloads = pl.pallas_call(
         pack_kernel,
-        out_shape=[jax.ShapeDtypeStruct((128, COLS), jnp.bfloat16)]
-        + [jax.ShapeDtypeStruct((2 * TOK + 128, COLS), jnp.bfloat16)] * 3,
-        in_specs=[vmem] * 2,
-        out_specs=[vmem] * 4,
-        compiler_params=pltpu.CompilerParams(vmem_limit_bytes=16 * 1024 * 1024),
+        out_shape=[jax.ShapeDtypeStruct((2 * TOK + 128, COLS), jnp.bfloat16)] * NX,
+        in_specs=[hbm] * 2,
+        out_specs=[hbm] * NX,
+        scratch_shapes=[
+            pltpu.VMEM((NX, FF // 1024, ROWS), jnp.int32),
+            pltpu.VMEM((NX, 128, COLS), jnp.bfloat16),
+            pltpu.SemaphoreType.DMA((NX,)),
+            pltpu.SemaphoreType.DMA((NX, 2)),
+            pltpu.SemaphoreType.DMA((NX,)),
+        ],
+        compiler_params=pltpu.CompilerParams(vmem_limit_bytes=60 * 1024 * 1024),
         name="pack_columns_and_words",
     )(activations, jnp.transpose(sign_words, (1, 0)))
     payloads = [
-        lax.ppermute(payload, "x", [(i, i ^ delta) for i in range(NX)])
-        for delta, payload in enumerate(payloads, 1)
+        lax.ppermute(payload, "x", [(i, i ^ delta) for i in range(NX)]) if delta else payload
+        for delta, payload in enumerate(payloads)
     ]
 
     wire = jnp.transpose(out_grads, (0, 2, 1)).astype(jnp.float32) * WIRE
-    wire = lax.all_gather(wire.astype(jnp.float16), Z, axis=1, tiled=True)
-    grads = wire.astype(jnp.float32).astype(jnp.bfloat16)
+    wire = lax.all_gather(wire.astype(jnp.float16), ("z", "core"), axis=1, tiled=True)
+    wire = lax.dynamic_index_in_dim(
+        wire.reshape(2, NZ, 2, LOW, TOK), lax.axis_index("core"), axis=2, keepdims=False
+    )
+    grads = wire.reshape(2, ROWS, TOK).astype(jnp.float32).astype(jnp.bfloat16)
 
     values = pl.pallas_call(
         main_kernel,
-        out_shape=jax.ShapeDtypeStruct((NX, 4, 4, 2, KDEV), jnp.float32),
-        in_specs=[vmem] * 7,
+        out_shape=jax.ShapeDtypeStruct((TILES, NX, 2, KDEV), jnp.float32),
+        in_specs=[vmem] * 6,
         out_specs=vmem,
         scratch_shapes=[
             pltpu.VMEM((NX, ROWS, COLS), jnp.float32),
@@ -155,22 +172,20 @@
             flops=7 * 10**9, bytes_accessed=8 * 1024 * 1024, transcendentals=0
         ),
         name="gradient_transform_sample",
-    )(indices.reshape(NX * NZ, KDEV), grads, own_bytes, activations, *payloads)
+    )(indices.reshape(NX * NZ, KDEV), grads, *payloads)
 
-    near = lax.all_to_all(
-        values.reshape(16, 4, 2, KDEV), ("x", "zl"), split_axis=0, concat_axis=0, tiled=True
-    )
-    half = jnp.sum(near, axis=0) * SCALE
-    sent = jnp.broadcast_to(half[None], (ex_size, 4, 2, KDEV)).reshape(ex_size * 4, 2, KDEV)
-    received = lax.all_to_all(sent, ex + ("zh",), split_axis=0, concat_axis=0, tiled=True)
-    raw = jnp.sum(received.reshape(ex_size, 4, 2, KDEV), axis=1)
+    along_z = lax.all_to_all(values, "z", split_axis=0, concat_axis=0, tiled=True)
+    half = jnp.sum(along_z, axis=0) * SCALE
+    sent = jnp.broadcast_to(half[None], (ex_size, NX, 2, KDEV)).reshape(ex_size * NX, 2, KDEV)
+    received = lax.all_to_all(sent, ex + ("x",), split_axis=0, concat_axis=0, tiled=True)
+    raw = jnp.sum(received.reshape(ex_size, NX, 2, KDEV), axis=1)
     own_raw = lax.dynamic_index_in_dim(raw, lax.axis_index(ex), axis=0, keepdims=False)
     return own_raw - jnp.sum(raw, axis=(0, 1))[None, :] / (2 * ex_size)
 
 
 def solution(mesh):
-    grid = Mesh(mesh.devices.reshape(-1, 2, NX, 4, 4), ("y", "core", "x") + Z)
-    ex, par = ("y", "core"), ("x",) + Z
+    grid = Mesh(mesh.devices.reshape(-1, 2, NX, NZ), ("y", "core", "x", "z"))
+    ex, par = ("y", "core"), ("x", "z")
     return jax.shard_map(
         shards,
         mesh=grid,

time: 114 us -> 176 us (1.54)
  Pallas kernels: 9.5 us -> 74.2 us
  blocking collectives: 55.6 us -> 70.8 us
  starting transfers between devices: 28.3 us -> 19 us
  waiting for transfers between devices: 14.4 us -> 7.22 us
  local copies, waits for them, and re-layouts: 3.21 us -> 0.62 us
    pallas_call x2, Pallas kernels: 9.5 us -> 74.2 us  [the longest x1 64.8 us: shards(): pl.pallas_call(pack_kernel, out_shape=[jax.ShapeDtypeStruct((2 * TOK + 12...]
    all_to_all x1, starting transfers between devices: 18.1 us -> 8.79 us  [shards(): lax.all_to_all(sent, ex + ('x',), split_axis=0, concat_axis=0, tiled=True)]
    all_gather x1, blocking collectives: 44.5 us -> 52.6 us  [shards(): lax.all_gather(wire.astype(jnp.float16), ('z', 'core'), axis=1, tiled=True)]
    all_to_all x1, waiting for transfers between devices: 14.4 us -> 7.21 us  [shards(): lax.all_to_all(sent, ex + ('x',), split_axis=0, concat_axis=0, tiled=True)]
    all_to_all x1, blocking collectives: 11.1 us -> 18.2 us  [shards(): lax.all_to_all(values, 'z', split_axis=0, concat_axis=0, tiled=True)]
    unnamed x8 -> x4, local copies, waits for them, and re-layouts: 2.59 us -> 0.01 us
  transfers between devices with their start and end apart: 4 -> 4, of which waited for: 1 -> 1; matrix products, arithmetic and copies ran while one was open for 1% -> 2% of each run, Pallas kernels for 0% -> 0%
where the time goes in v4:
time: 176 us
  Pallas kernels  74.2 us (42%)
  blocking collectives  70.8 us (40%)
  starting transfers between devices  19 us (11%)
  waiting for transfers between devices  7.22 us (4%)
  other arithmetic  3.74 us (2%)
    pallas_call x1, Pallas kernels, shards(): pl.pallas_call(pack_kernel, out_shape=[jax.ShapeDtypeStruct((2 * TOK + 12...  64.8 us
    all_gather x1, blocking collectives, shards(): lax.all_gather(wire.astype(jnp.float16), ('z', 'core'), axis=1, tiled=True)  52.6 us
    all_to_all x1, blocking collectives, shards(): lax.all_to_all(values, 'z', split_axis=0, concat_axis=0, tiled=True)  18.2 us
    ppermute x3, starting transfers between devices, shards(): lax.ppermute(payload, 'x', [(i, i ^ delta) for i in range(NX)])  10.2 us
    pallas_call x1, Pallas kernels, shards(): pl.pallas_call(main_kernel, out_shape=jax.ShapeDtypeStruct((TILES, NX, 2,...  9.37 us
    all_to_all x1, starting transfers between devices, shards(): lax.all_to_all(sent, ex + ('x',), split_axis=0, concat_axis=0, tiled=True)  8.79 us
    all_to_all x1, waiting for transfers between devices, shards(): lax.all_to_all(sent, ex + ('x',), split_axis=0, concat_axis=0, tiled=True)  7.21 us
  transfers between devices with their start and end apart: 4, of which 1 were waited for; matrix products, arithmetic and copies ran while one was open for 2% of the time, Pallas kernels for 0%

profile of v4, /device:TPU:1, one launch (start us, length us, event | category | flops | bytes accessed | tf_op | source)
XLA Modules:
  0.0 175.7 jit_solution(11903114438784754355)
XLA Ops:
  0.0 64.8 %pack_columns_and_words.1 = (bf16[1152,256]{1,0:T(8,128)(2,1)}, bf16[1152,256]{1,0:T(8,128)(2,1)}, bf16[1152,256]{1,0:T(8,128)(2,1)}, bf16[1152,256]{1,0:T(8,128)(2,1)}) custom-call(bf16[2,512,256]{2,1,0:T(8,128)(2,1)} %acts_in.1, s32[16,4096]{1,0:T(8,128)} %bitcast.18), custom_call_target="tpu_custom_call" | custom-call | tf_op jit(solution)/shard_map/pack_columns_and_words/pallas_call | solution.py:134
  64.8 3.9 %collective-permute-start = (bf16[1152,256]{1,0:T(8,128)(2,1)}, bf16[1152,256]{1,0:T(8,128)(2,1)S(1)}, u32[]{:S(2)}, u32[]{:S(2)}) collective-permute-start(bf16[1152,256]{1,0:T(8,128)(2,1)} %get-tuple-element.10), channel_id=1, source_target_pairs={{0,16},{16,0},{32,48},{48,32},{1,17},{17,1},{33,49},{49,33},{2,18}... | collective-permute-start | bytes 1769480 | tf_op jit(solution)/shard_map/ppermute | solution.py:150
  68.7 4.4 %collective-permute-start.1 = (bf16[1152,256]{1,0:T(8,128)(2,1)}, bf16[1152,256]{1,0:T(8,128)(2,1)S(1)}, u32[]{:S(2)}, u32[]{:S(2)}) collective-permute-start(bf16[1152,256]{1,0:T(8,128)(2,1)} %get-tuple-element.11), channel_id=1, source_target_pairs={{0,32},{16,48},{32,0},{48,16},{1,33},{17,49},{33,1},{49,17},{2,34}... | collective-permute-start | bytes 1769480 | tf_op jit(solution)/shard_map/ppermute | solution.py:150
  73.1 1.9 %collective-permute-start.2 = (bf16[1152,256]{1,0:T(8,128)(2,1)}, bf16[1152,256]{1,0:T(8,128)(2,1)S(1)}, u32[]{:S(2)}, u32[]{:S(2)}) collective-permute-start(bf16[1152,256]{1,0:T(8,128)(2,1)} %get-tuple-element.12), channel_id=1, source_target_pairs={{0,48},{16,32},{32,16},{48,0},{1,49},{17,33},{33,17},{49,1},{2,50}... | collective-permute-start | bytes 1769480 | tf_op jit(solution)/shard_map/ppermute | solution.py:150
  75.0 0.9 fusion
  76.0 0.0 copy-start
  76.0 0.0 copy-start.1
  76.0 52.6 %all-gather.1 = f16[2,2048,512]{2,1,0:T(8,128)(2,1)} all-gather(f16[2,64,512]{2,1,0:T(8,128)(2,1)S(1)} %fusion), channel_id=1, replica_groups=mesh['y'=4,'core'=2,'x'=4,'z'=16] {'z','core'}, dimensions={1}, use_global_device_ids=true | all-gather | bytes 4325376 | tf_op jit(solution)/shard_map/all_gather | solution.py:155
  128.6 2.1 %convert_convert_fusion = bf16[2,16,1,64,512]{4,3,1,0,2:T(8,128)(2,1)S(1)} fusion(f16[2,16,2,64,512]{4,3,2,1,0:T(8,128)(2,1)} %bitcast.17, s32[]{:T(128)S(6)} %select_n.8), kind=kLoop, calls=%fused_computation | loop fusion | flops 2097152 | bytes 4194308 | tf_op jit(solution)/shard_map/convert_element_type | solution.py:159
  130.7 0.0 collective-permute-done.p1
  130.7 0.0 collective-permute-done.1.p2
  130.7 0.0 collective-permute-done.2.p3
  130.7 0.0 copy-done
  130.7 0.0 copy-done.1
  130.7 9.4 %gradient_transform_sample.1 = f32[16,4,2,128]{3,2,1,0:T(2,128)S(1)} custom-call(s32[64,128]{1,0:T(8,128)S(1)} %bitcast.16, bf16[2,1024,512]{2,1,0:T(8,128)(2,1)S(1)} %bitcast.15, bf16[1152,256]{1,0:T(8,128)(2,1)S(1)} %copy-done, bf16[1152,256]{1,0:T(8,128)(2,1)S(1)} %collective-permute-done.p1, bf16[1152,256]{1,0:T(8,128)(2,1)S(1)} %collective-permute-done.1.p2, ...), custom_call_target="tpu_custom_call" | custom-call | flops 7000000000 | bytes 8388608 | tf_op jit(solution)/shard_map/gradient_transform_sample/pallas_call | solution.py:161
  140.1 18.2 %all_to_all.10 = f32[16,4,2,128]{3,2,1,0:T(2,128)S(1)} all-to-all(f32[16,4,2,128]{3,2,1,0:T(2,128)S(1)} %gradient_transform_sample.1), channel_id=1, replica_groups=mesh['y'=4,'core'=2,'x'=4,'z'=16] {'z'}, dimensions={0} | all-to-all | bytes 131072 | tf_op jit(solution)/shard_map/all_to_all | solution.py:177
  158.4 0.6 broadcast_in_dim.2
  159.0 8.8 %all-to-all-start.1 = ((f32[32,2,128]{2,1,0:T(2,128)}), f32[32,2,128]{2,1,0:T(2,128)S(1)}, u32[]{:S(2)}, u32[]{:S(2)}) async-start(f32[32,2,128]{2,1,0:T(2,128)} %bitcast.5), calls=%async_computation.1 | async-start | bytes 65536 | tf_op jit(solution)/shard_map/all_to_all | solution.py:180
  167.8 7.2 %all-to-all-done.1 = f32[32,2,128]{2,1,0:T(2,128)S(1)} async-done(((f32[32,2,128]{2,1,0:T(2,128)}), f32[32,2,128]{2,1,0:T(2,128)S(1)}, u32[]{:S(2)}, u32[]{:S(2)}) %all-to-all-start.1) | async-done | bytes 32800 | tf_op jit(solution)/shard_map/all_to_all | solution.py:180
  175.0 0.1 reduce_sum.29
  175.1 0.6 bitcast_subtract_fusion
  (4 shorter events, 0.1 us)
Async XLA Ops:
  64.8 65.9 %collective-permute-start = (bf16[1152,256]{1,0:T(8,128)(2,1)}, bf16[1152,256]{1,0:T(8,128)(2,1)S(1)}, u32[]{:S(2)}, u32[]{:S(2)}) collective-permute-start(bf16[1152,256]{1,0:T(8,128)(2,1)} %get-tuple-element.10), channel_id=1, source_target_pairs={{0,16},{16,0},{32,48},{48,32},{1,17},{17,1},{33,49},{49,33},{2,18}... | collective-permute-start | bytes 1769480 | tf_op jit(solution)/shard_map/ppermute | solution.py:150
  68.7 62.0 %collective-permute-start.1 = (bf16[1152,256]{1,0:T(8,128)(2,1)}, bf16[1152,256]{1,0:T(8,128)(2,1)S(1)}, u32[]{:S(2)}, u32[]{:S(2)}) collective-permute-start(bf16[1152,256]{1,0:T(8,128)(2,1)} %get-tuple-element.11), channel_id=1, source_target_pairs={{0,32},{16,48},{32,0},{48,16},{1,33},{17,49},{33,1},{49,17},{2,34}... | collective-permute-start | bytes 1769480 | tf_op jit(solution)/shard_map/ppermute | solution.py:150
  73.1 57.6 %collective-permute-start.2 = (bf16[1152,256]{1,0:T(8,128)(2,1)}, bf16[1152,256]{1,0:T(8,128)(2,1)S(1)}, u32[]{:S(2)}, u32[]{:S(2)}) collective-permute-start(bf16[1152,256]{1,0:T(8,128)(2,1)} %get-tuple-element.12), channel_id=1, source_target_pairs={{0,48},{16,32},{32,16},{48,0},{1,49},{17,33},{33,17},{49,1},{2,50}... | collective-permute-start | bytes 1769480 | tf_op jit(solution)/shard_map/ppermute | solution.py:150
  76.0 54.7 %copy-start = (bf16[1152,256]{1,0:T(8,128)(2,1)S(1)}, bf16[1152,256]{1,0:T(8,128)(2,1)}, u32[]{:S(2)}) copy-start(bf16[1152,256]{1,0:T(8,128)(2,1)} %get-tuple-element.9.p0) | copy-start | bytes 1769476
  76.0 54.7 %copy-start.1 = (s32[8192]{0:T(1024)S(1)}, s32[8192]{0:T(1024)}, u32[]{:S(2)}) copy-start(s32[8192]{0:T(1024)} %param.7) | copy-start | bytes 98308
  159.0 16.0 %all-to-all-start.1 = ((f32[32,2,128]{2,1,0:T(2,128)}), f32[32,2,128]{2,1,0:T(2,128)S(1)}, u32[]{:S(2)}, u32[]{:S(2)}) async-start(f32[32,2,128]{2,1,0:T(2,128)} %bitcast.5), calls=%async_computation.1 | async-start | bytes 65536 | tf_op jit(solution)/shard_map/all_to_all | solution.py:180

commit v5 on v4

--- a/solution.py
+++ b/solution.py
@@ -33,36 +33,19 @@
     return high, (values - high.astype(jnp.float32)).astype(jnp.bfloat16)
 
 
-def pack_kernel(acts_in, words_in, *refs):
-    payloads, (words, packed, word_sem, act_sem, out_sem) = refs[:NX], refs[NX:]
-    x = lax.axis_index("x")
-    copies = []
-    for delta in range(NX):
-        start = pl.multiple_of((x ^ delta) * ROWS, ROWS)
-        source = words_in.at[:, pl.ds(start, ROWS)]
-        copies.append(pltpu.make_async_copy(source, words.at[delta], word_sem.at[delta]))
-    for delta in range(NX):
+def pack_kernel(acts_ref, words_ref, out_ref):
+    for target in range(NX):
         for example in range(2):
-            target = payloads[delta].at[pl.ds(example * TOK, TOK)]
-            sem = act_sem.at[delta, example]
-            copies.append(pltpu.make_async_copy(acts_in.at[example], target, sem))
-    for copy in copies:
-        copy.start()
-    for delta in range(NX):
-        copies[delta].wait()
-        word = words[delta]
+            out_ref[target, pl.ds(example * TOK, TOK), :] = acts_ref[example]
+        word = words_ref[:, target * ROWS : (target + 1) * ROWS]
         two = jnp.concatenate([word & 255, (word >> 8) & 255], axis=0)
         two = two.astype(jnp.float32).astype(jnp.bfloat16)
         for q in range(4):
-            packed[delta, pl.ds(32 * q, 32), :] = two[:, q * COLS : (q + 1) * COLS]
-        target = payloads[delta].at[pl.ds(2 * TOK, 128)]
-        copies.append(pltpu.make_async_copy(packed.at[delta], target, out_sem.at[delta]))
-        copies[-1].start()
-    for copy in copies[NX:]:
-        copy.wait()
+            part = two[:, q * COLS : (q + 1) * COLS]
+            out_ref[target, pl.ds(2 * TOK + 32 * q, 32), :] = part
 
 
-def main_kernel(idx_ref, grads, p0, p1, p2, p3, out_ref, signs, tiles):
+def main_kernel(idx_ref, grads, columns, out_ref, signs, tiles):
     x, z = lax.axis_index("x"), lax.axis_index("z")
 
     row = lax.broadcasted_iota(jnp.int32, (COLS, COLS), 0)
@@ -75,19 +58,18 @@
     spread = spread.astype(jnp.bfloat16)
     shift = lax.broadcasted_iota(jnp.int32, (COLS, COLS), 1) & 7
 
-    for delta, payload in enumerate((p0, p1, p2, p3)):
-        block = x ^ delta
+    for block in range(NX):
         for q in range(4):
-            two = payload[pl.ds(2 * TOK + 32 * q, 32), :]
+            two = columns[block, pl.ds(2 * TOK + 32 * q, 32), :]
             value = lax.dot_general(
                 two, spread, (((0,), (0,)), ((), ())), preferred_element_type=jnp.float32
             )
             bit = (value.astype(jnp.int32) >> shift) & 1
-            signs[delta, pl.ds(q * COLS, COLS), :] = (1 - 2 * bit).astype(jnp.float32)
+            signs[block, pl.ds(q * COLS, COLS), :] = (1 - 2 * bit).astype(jnp.float32)
         for example in range(2):
-            act = payload[pl.ds(example * TOK, TOK), :]
+            act = columns[block, pl.ds(example * TOK, TOK), :]
             grad = jnp.dot(grads[example], act, preferred_element_type=jnp.float32)
-            signed = grad * signs[delta]
+            signed = grad * signs[block]
             parts = []
             for b in range(4):
                 both = jnp.concatenate(split(signed[b * COLS : (b + 1) * COLS]), axis=0)
@@ -130,38 +112,24 @@
     ex = ("y", "core")
     ex_size = lax.axis_size(ex)
     vmem = pl.BlockSpec(memory_space=pltpu.VMEM)
-    hbm = pl.BlockSpec(memory_space=pltpu.HBM)
-    payloads = pl.pallas_call(
+    packed = pl.pallas_call(
         pack_kernel,
-        out_shape=[jax.ShapeDtypeStruct((2 * TOK + 128, COLS), jnp.bfloat16)] * NX,
-        in_specs=[hbm] * 2,
-        out_specs=[hbm] * NX,
-        scratch_shapes=[
-            pltpu.VMEM((NX, FF // 1024, ROWS), jnp.int32),
-            pltpu.VMEM((NX, 128, COLS), jnp.bfloat16),
-            pltpu.SemaphoreType.DMA((NX,)),
-            pltpu.SemaphoreType.DMA((NX, 2)),
-            pltpu.SemaphoreType.DMA((NX,)),
-        ],
-        compiler_params=pltpu.CompilerParams(vmem_limit_bytes=60 * 1024 * 1024),
+        out_shape=jax.ShapeDtypeStruct((NX, 2 * TOK + 128, COLS), jnp.bfloat16),
+        in_specs=[vmem] * 2,
+        out_specs=vmem,
+        compiler_params=pltpu.CompilerParams(vmem_limit_bytes=16 * 1024 * 1024),
         name="pack_columns_and_words",
     )(activations, jnp.transpose(sign_words, (1, 0)))
-    payloads = [
-        lax.ppermute(payload, "x", [(i, i ^ delta) for i in range(NX)]) if delta else payload
-        for delta, payload in enumerate(payloads)
-    ]
+    columns = lax.all_to_all(packed, "x", split_axis=0, concat_axis=0, tiled=True)
 
     wire = jnp.transpose(out_grads, (0, 2, 1)).astype(jnp.float32) * WIRE
-    wire = lax.all_gather(wire.astype(jnp.float16), ("z", "core"), axis=1, tiled=True)
-    wire = lax.dynamic_index_in_dim(
-        wire.reshape(2, NZ, 2, LOW, TOK), lax.axis_index("core"), axis=2, keepdims=False
-    )
-    grads = wire.reshape(2, ROWS, TOK).astype(jnp.float32).astype(jnp.bfloat16)
+    wire = lax.all_gather(wire.astype(jnp.float16), "z", axis=1, tiled=True)
+    grads = wire.astype(jnp.float32).astype(jnp.bfloat16)
 
     values = pl.pallas_call(
         main_kernel,
         out_shape=jax.ShapeDtypeStruct((TILES, NX, 2, KDEV), jnp.float32),
-        in_specs=[vmem] * 6,
+        in_specs=[vmem] * 3,
         out_specs=vmem,
         scratch_shapes=[
             pltpu.VMEM((NX, ROWS, COLS), jnp.float32),
@@ -172,7 +140,7 @@
             flops=7 * 10**9, bytes_accessed=8 * 1024 * 1024, transcendentals=0
         ),
         name="gradient_transform_sample",
-    )(indices.reshape(NX * NZ, KDEV), grads, *payloads)
+    )(indices.reshape(NX * NZ, KDEV), grads, columns)
 
     along_z = lax.all_to_all(values, "z", split_axis=0, concat_axis=0, tiled=True)
     half = jnp.sum(along_z, axis=0) * SCALE

time: 176 us -> 108 us (0.61)
  Pallas kernels: 74.2 us -> 10.9 us
  blocking collectives: 70.8 us -> 62.7 us
  local copies, waits for them, and re-layouts: 0.62 us -> 4.22 us
    pallas_call x1, Pallas kernels: 64.8 us -> 1.57 us  [shards(): pl.pallas_call(pack_kernel, out_shape=jax.ShapeDtypeStruct((NX, 2 * TOK +...]
    ppermute x3 -> x0, starting transfers between devices: 10.2 us -> none  [shards(): lax.ppermute(payload, 'x', [(i, i ^ delta) for i in range(NX)])]
    all_gather x1, blocking collectives: 52.6 us -> 44.3 us  [shards(): wire = lax.all_gather(wire.astype(jnp.float16), 'z', axis=1, tiled=True)]
    all_to_all x1, starting transfers between devices: 8.79 us -> 14.8 us  [shards(): lax.all_to_all(sent, ex + ('x',), split_axis=0, concat_axis=0, tiled=True)]
    all_to_all x0 -> x1, starting transfers between devices: none -> 4.97 us  [shards(): lax.all_to_all(packed, 'x', split_axis=0, concat_axis=0, tiled=True)]
    unnamed x4 -> x10, local copies, waits for them, and re-layouts: 0.01 us -> 3.59 us
  transfers between devices with their start and end apart: 4 -> 2, of which waited for: 1 -> 1; matrix products, arithmetic and copies ran while one was open for 2% -> 2% of each run, Pallas kernels for 0% -> 0%
where the time goes in v5:
time: 108 us; the launch traced here: 107 us
  blocking collectives  62.7 us (58%)
  starting transfers between devices  19.7 us (18%)
  Pallas kernels  10.9 us (10%)
  waiting for transfers between devices  7.21 us (7%)
  local copies, waits for them, and re-layouts  4.22 us (4%)
  other arithmetic  2.44 us (2%)
    all_gather x1, blocking collectives, shards(): wire = lax.all_gather(wire.astype(jnp.float16), 'z', axis=1, tiled=True)  44.3 us
    all_to_all x1, blocking collectives, shards(): lax.all_to_all(values, 'z', split_axis=0, concat_axis=0, tiled=True)  18.5 us
    all_to_all x1, starting transfers between devices, shards(): lax.all_to_all(sent, ex + ('x',), split_axis=0, concat_axis=0, tiled=True)  14.8 us
    pallas_call x1, Pallas kernels, shards(): pl.pallas_call(main_kernel, out_shape=jax.ShapeDtypeStruct((TILES, NX, 2,...  9.36 us
    all_to_all x1, waiting for transfers between devices, shards(): lax.all_to_all(sent, ex + ('x',), split_axis=0, concat_axis=0, tiled=True)  7.21 us
    all_to_all x1, starting transfers between devices, shards(): lax.all_to_all(packed, 'x', split_axis=0, concat_axis=0, tiled=True)  4.97 us
    unnamed x10, local copies, waits for them, and re-layouts  3.59 us
  transfers between devices with their start and end apart: 2, of which 1 were waited for; matrix products, arithmetic and copies ran while one was open for 2% of the time, Pallas kernels for 0%

profile of v5, /device:TPU:1, one launch (start us, length us, event | category | flops | bytes accessed | tf_op | source)
XLA Modules:
  0.0 107.3 jit_solution(12121489063214552794)
XLA Ops:
  0.0 0.0 copy-start.1
  0.0 1.0 copy-done.1
  1.0 0.0 copy-start.2
  1.0 0.9 copy-done.2
  2.0 1.6 %pack_columns_and_words.1 = bf16[4,1152,256]{2,1,0:T(8,128)(2,1)} custom-call(bf16[2,512,256]{2,1,0:T(8,128)(2,1)S(1)} %copy-done.1, s32[16,4096]{1,0:T(8,128)S(1)} %bitcast.11), custom_call_target="tpu_custom_call" | custom-call | tf_op jit(solution)/shard_map/pack_columns_and_words/pallas_call | solution.py:115
  3.6 0.0 copy-start.4
  3.6 5.0 %all-to-all-start = ((bf16[4,1152,256]{2,1,0:T(8,128)(2,1)}), bf16[4,1152,256]{2,1,0:T(8,128)(2,1)S(1)}, u32[]{:S(2)}, u32[]{:S(2)}) async-start(bf16[4,1152,256]{2,1,0:T(8,128)(2,1)} %pack_columns_and_words.1), calls=%async_computation | async-start | bytes 4718592 | tf_op jit(solution)/shard_map/all_to_all | solution.py:123
  8.5 0.0 copy-done.4
  8.6 44.3 %all-gather.1 = f16[2,1024,512]{2,1,0:T(8,128)(2,1)S(1)} all-gather(f16[2,64,512]{2,1,0:T(8,128)(2,1)S(1)} %fusion), channel_id=1, replica_groups=mesh['y'=4,'core'=2,'x'=4,'z'=16] {'z'}, dimensions={1}, use_global_device_ids=true | all-gather | bytes 2228224 | tf_op jit(solution)/shard_map/all_gather | solution.py:126
  52.8 0.0 copy-start.3
  52.8 1.7 %convert_convert_fusion.grads = bf16[2,1024,512]{2,1,0:T(8,128)(2,1)} fusion(f16[2,1024,512]{2,1,0:T(8,128)(2,1)S(1)} %all-gather.1), kind=kLoop, calls=%fused_computation | loop fusion | flops 2097152 | bytes 4194304 | tf_op jit(solution)/shard_map/convert_element_type | solution.py:127
  54.6 0.0 all-to-all-done.columns
  54.6 0.0 copy-done.3
  54.6 0.0 copy-start
  54.6 1.6 %copy-done = bf16[2,1024,512]{2,1,0:T(8,128)(2,1)S(1)} copy-done((bf16[2,1024,512]{2,1,0:T(8,128)(2,1)S(1)}, bf16[2,1024,512]{2,1,0:T(8,128)(2,1)}, u32[]{:S(2)}) %copy-start) | copy-done | bytes 2097176
  56.2 9.4 %gradient_transform_sample.1 = f32[16,4,2,128]{3,2,1,0:T(2,128)S(1)} custom-call(s32[64,128]{1,0:T(8,128)S(1)} %bitcast.12, bf16[2,1024,512]{2,1,0:T(8,128)(2,1)S(1)} %copy-done, bf16[4,1152,256]{2,1,0:T(8,128)(2,1)S(1)} %all-to-all-done.columns), custom_call_target="tpu_custom_call" | custom-call | flops 7000000000 | bytes 8388608 | tf_op jit(solution)/shard_map/gradient_transform_sample/pallas_call | solution.py:129
  65.5 18.5 %all_to_all.15 = f32[16,4,2,128]{3,2,1,0:T(2,128)S(1)} all-to-all(f32[16,4,2,128]{3,2,1,0:T(2,128)S(1)} %gradient_transform_sample.1), channel_id=1, replica_groups=mesh['y'=4,'core'=2,'x'=4,'z'=16] {'z'}, dimensions={0} | all-to-all | bytes 131072 | tf_op jit(solution)/shard_map/all_to_all | solution.py:145
  84.1 0.6 broadcast_in_dim.2
  84.7 14.8 %all-to-all-start.2 = ((f32[32,2,128]{2,1,0:T(2,128)}), f32[32,2,128]{2,1,0:T(2,128)S(1)}, u32[]{:S(2)}, u32[]{:S(2)}) async-start(f32[32,2,128]{2,1,0:T(2,128)} %bitcast.3), calls=%async_computation.2 | async-start | bytes 65536 | tf_op jit(solution)/shard_map/all_to_all | solution.py:148
  99.5 7.2 %all-to-all-done.2 = f32[32,2,128]{2,1,0:T(2,128)S(1)} async-done(((f32[32,2,128]{2,1,0:T(2,128)}), f32[32,2,128]{2,1,0:T(2,128)S(1)}, u32[]{:S(2)}, u32[]{:S(2)}) %all-to-all-start.2) | async-done | bytes 32800 | tf_op jit(solution)/shard_map/all_to_all | solution.py:148
  106.7 0.1 reduce_sum.29
  106.8 0.6 bitcast_subtract_fusion
  (5 shorter events, 0.1 us)
Async XLA Ops:
  0.0 1.0 copy-start.1
  1.0 0.9 copy-start.2
  3.6 5.0 %copy-start.4 = (bf16[2,512,64]{1,2,0:T(8,128)(2,1)S(1)}, bf16[2,512,64]{1,2,0:T(8,128)(2,1)}, u32[]{:S(2)}) copy-start(bf16[2,512,64]{1,2,0:T(8,128)(2,1)} %param.5) | copy-start | bytes 393220
  3.6 51.0 %all-to-all-start = ((bf16[4,1152,256]{2,1,0:T(8,128)(2,1)}), bf16[4,1152,256]{2,1,0:T(8,128)(2,1)S(1)}, u32[]{:S(2)}, u32[]{:S(2)}) async-start(bf16[4,1152,256]{2,1,0:T(8,128)(2,1)} %pack_columns_and_words.1), calls=%async_computation | async-start | bytes 4718592 | tf_op jit(solution)/shard_map/all_to_all | solution.py:123
  52.8 1.7 %copy-start.3 = (s32[8192]{0:T(1024)S(1)}, s32[8192]{0:T(1024)}, u32[]{:S(2)}) copy-start(s32[8192]{0:T(1024)} %param.7) | copy-start | bytes 98308
  54.6 1.6 %copy-start = (bf16[2,1024,512]{2,1,0:T(8,128)(2,1)S(1)}, bf16[2,1024,512]{2,1,0:T(8,128)(2,1)}, u32[]{:S(2)}) copy-start(bf16[2,1024,512]{2,1,0:T(8,128)(2,1)} %convert_convert_fusion.grads) | copy-start | bytes 6291460
  84.7 22.0 %all-to-all-start.2 = ((f32[32,2,128]{2,1,0:T(2,128)}), f32[32,2,128]{2,1,0:T(2,128)S(1)}, u32[]{:S(2)}, u32[]{:S(2)}) async-start(f32[32,2,128]{2,1,0:T(2,128)} %bitcast.3), calls=%async_computation.2 | async-start | bytes 65536 | tf_op jit(solution)/shard_map/all_to_all | solution.py:148

commit v6 on v5

--- a/solution.py
+++ b/solution.py
@@ -18,7 +18,7 @@
 SAMPLES = NX * KDEV
 WIRE = 131072.0
 SCALE = 1.0 / 8192.0 / WIRE
-VMEM_BYTES = 36 * 1024 * 1024
+VMEM_BYTES = 20 * 1024 * 1024
 
 
 def sign_of(bits):
@@ -33,16 +33,32 @@
     return high, (values - high.astype(jnp.float32)).astype(jnp.bfloat16)
 
 
-def pack_kernel(acts_ref, words_ref, out_ref):
+def pack_kernel(acts_in, words_in, out, acts, words, packed, in_sem, act_sem, byte_sem):
+    word_copy = pltpu.make_async_copy(words_in, words, in_sem.at[2])
+    word_copy.start()
+    act_copies = []
+    for example in range(2):
+        target = acts.at[pl.ds(example * TOK, TOK)]
+        act_copies.append(pltpu.make_async_copy(acts_in.at[example], target, in_sem.at[example]))
+        act_copies[-1].start()
+    copies = []
+    word_copy.wait()
     for target in range(NX):
-        for example in range(2):
-            out_ref[target, pl.ds(example * TOK, TOK), :] = acts_ref[example]
-        word = words_ref[:, target * ROWS : (target + 1) * ROWS]
+        word = words[:, target * ROWS : (target + 1) * ROWS]
         two = jnp.concatenate([word & 255, (word >> 8) & 255], axis=0)
         two = two.astype(jnp.float32).astype(jnp.bfloat16)
         for q in range(4):
-            part = two[:, q * COLS : (q + 1) * COLS]
-            out_ref[target, pl.ds(2 * TOK + 32 * q, 32), :] = part
+            packed[target, pl.ds(32 * q, 32), :] = two[:, q * COLS : (q + 1) * COLS]
+    for copy in act_copies:
+        copy.wait()
+    for target in range(NX):
+        head, tail = out.at[target, pl.ds(0, 2 * TOK)], out.at[target, pl.ds(2 * TOK, 128)]
+        copies.append(pltpu.make_async_copy(acts, head, act_sem.at[target]))
+        copies.append(pltpu.make_async_copy(packed.at[target], tail, byte_sem.at[target]))
+    for copy in copies:
+        copy.start()
+    for copy in copies:
+        copy.wait()
 
 
 def main_kernel(idx_ref, grads, columns, out_ref, signs, tiles):
@@ -105,19 +121,28 @@
                 out_ref[tile, tx, pl.ds(example, 1), :] = picked[:, tx * KDEV : (tx + 1) * KDEV]
         return carry
 
-    lax.fori_loop(0, TILES, tile_body, 0, unroll=4)
+    lax.fori_loop(0, TILES, tile_body, 0, unroll=8)
 
 
 def shards(activations, out_grads, sign_words, indices):
     ex = ("y", "core")
     ex_size = lax.axis_size(ex)
     vmem = pl.BlockSpec(memory_space=pltpu.VMEM)
+    hbm = pl.BlockSpec(memory_space=pltpu.HBM)
     packed = pl.pallas_call(
         pack_kernel,
         out_shape=jax.ShapeDtypeStruct((NX, 2 * TOK + 128, COLS), jnp.bfloat16),
-        in_specs=[vmem] * 2,
-        out_specs=vmem,
-        compiler_params=pltpu.CompilerParams(vmem_limit_bytes=16 * 1024 * 1024),
+        in_specs=[hbm] * 2,
+        out_specs=hbm,
+        scratch_shapes=[
+            pltpu.VMEM((2 * TOK, COLS), jnp.bfloat16),
+            pltpu.VMEM((FF // 1024, D), jnp.int32),
+            pltpu.VMEM((NX, 128, COLS), jnp.bfloat16),
+            pltpu.SemaphoreType.DMA((3,)),
+            pltpu.SemaphoreType.DMA((NX,)),
+            pltpu.SemaphoreType.DMA((NX,)),
+        ],
+        compiler_params=pltpu.CompilerParams(vmem_limit_bytes=60 * 1024 * 1024),
         name="pack_columns_and_words",
     )(activations, jnp.transpose(sign_words, (1, 0)))
     columns = lax.all_to_all(packed, "x", split_axis=0, concat_axis=0, tiled=True)
@@ -135,7 +160,9 @@
             pltpu.VMEM((NX, ROWS, COLS), jnp.float32),
             pltpu.VMEM((TILES, 2, NX, LOW, COLS), jnp.bfloat16),
         ],
-        compiler_params=pltpu.CompilerParams(vmem_limit_bytes=VMEM_BYTES),
+        compiler_params=pltpu.CompilerParams(
+            vmem_limit_bytes=VMEM_BYTES, allow_input_fusion=[False, True, False]
+        ),
         cost_estimate=pl.CostEstimate(
             flops=7 * 10**9, bytes_accessed=8 * 1024 * 1024, transcendentals=0
         ),

time: 108 us -> 107 us (level)
  local copies, waits for them, and re-layouts: 4.22 us -> 2.21 us
    unnamed x10 -> x6, local copies, waits for them, and re-layouts: 3.59 us -> 1.6 us
where the time goes in v6:
time: 107 us; the launch traced here: 106 us
  blocking collectives  62.8 us (59%)
  starting transfers between devices  19.7 us (18%)
  Pallas kernels  11.9 us (11%)
  waiting for transfers between devices  7.21 us (7%)
  other arithmetic  2.43 us (2%)
  local copies, waits for them, and re-layouts  2.21 us (2%)
    all_gather x1, blocking collectives, shards(): wire = lax.all_gather(wire.astype(jnp.float16), 'z', axis=1, tiled=True)  44.3 us
    all_to_all x1, blocking collectives, shards(): lax.all_to_all(values, 'z', split_axis=0, concat_axis=0, tiled=True)  18.5 us
    all_to_all x1, starting transfers between devices, shards(): lax.all_to_all(sent, ex + ('x',), split_axis=0, concat_axis=0, tiled=True)  14.8 us
    pallas_call x1, Pallas kernels, shards(): pl.pallas_call(main_kernel, out_shape=jax.ShapeDtypeStruct((TILES, NX, 2,...  9.33 us
    all_to_all x1, waiting for transfers between devices, shards(): lax.all_to_all(sent, ex + ('x',), split_axis=0, concat_axis=0, tiled=True)  7.21 us
    all_to_all x1, starting transfers between devices, shards(): lax.all_to_all(packed, 'x', split_axis=0, concat_axis=0, tiled=True)  4.99 us
    pallas_call x1, Pallas kernels, shards(): pl.pallas_call(pack_kernel, out_shape=jax.ShapeDtypeStruct((NX, 2 * TOK +...  2.61 us
  transfers between devices with their start and end apart: 2, of which 1 were waited for; matrix products, arithmetic and copies ran while one was open for 2% of the time, Pallas kernels for 0%

profile of v6, /device:TPU:1, one launch (start us, length us, event | category | flops | bytes accessed | tf_op | source)
XLA Modules:
  0.0 106.4 jit_solution(8045487630799418912)
XLA Ops:
  0.0 2.6 %pack_columns_and_words.1 = bf16[4,1152,256]{2,1,0:T(8,128)(2,1)} custom-call(bf16[2,512,256]{2,1,0:T(8,128)(2,1)} %acts_in.1, s32[16,4096]{1,0:T(8,128)} %bitcast.12), custom_call_target="tpu_custom_call" | custom-call | tf_op jit(solution)/shard_map/pack_columns_and_words/pallas_call | solution.py:132
  2.6 0.0 copy-start.2
  2.6 5.0 %all-to-all-start = ((bf16[4,1152,256]{2,1,0:T(8,128)(2,1)}), bf16[4,1152,256]{2,1,0:T(8,128)(2,1)S(1)}, u32[]{:S(2)}, u32[]{:S(2)}) async-start(bf16[4,1152,256]{2,1,0:T(8,128)(2,1)} %pack_columns_and_words.1), calls=%async_computation | async-start | bytes 4718592 | tf_op jit(solution)/shard_map/all_to_all | solution.py:148
  7.6 0.0 copy-done.2
  7.7 44.3 %all-gather.1 = f16[2,1024,512]{2,1,0:T(8,128)(2,1)S(1)} all-gather(f16[2,64,512]{2,1,0:T(8,128)(2,1)S(1)} %fusion), channel_id=1, replica_groups=mesh['y'=4,'core'=2,'x'=4,'z'=16] {'z'}, dimensions={1}, use_global_device_ids=true | all-gather | bytes 2228224 | tf_op jit(solution)/shard_map/all_gather | solution.py:151
  51.9 0.0 copy-start.1
  51.9 1.7 %convert_convert_fusion.grads = bf16[2,1024,512]{2,1,0:T(8,128)(2,1)} fusion(f16[2,1024,512]{2,1,0:T(8,128)(2,1)S(1)} %all-gather.1), kind=kLoop, calls=%fused_computation | loop fusion | flops 2097152 | bytes 4194304 | tf_op jit(solution)/shard_map/convert_element_type | solution.py:152
  53.6 0.0 all-to-all-done.columns
  53.6 0.0 copy-done.1
  53.6 0.0 copy-start
  53.6 1.6 %copy-done = bf16[2,1024,512]{2,1,0:T(8,128)(2,1)S(1)} copy-done((bf16[2,1024,512]{2,1,0:T(8,128)(2,1)S(1)}, bf16[2,1024,512]{2,1,0:T(8,128)(2,1)}, u32[]{:S(2)}) %copy-start) | copy-done | bytes 2097176
  55.2 9.3 %gradient_transform_sample.1 = f32[16,4,2,128]{3,2,1,0:T(2,128)S(1)} custom-call(s32[64,128]{1,0:T(8,128)S(1)} %bitcast.11, bf16[2,1024,512]{2,1,0:T(8,128)(2,1)S(1)} %copy-done, bf16[4,1152,256]{2,1,0:T(8,128)(2,1)S(1)} %all-to-all-done.columns), custom_call_target="tpu_custom_call" | custom-call | flops 7000000000 | bytes 8388608 | tf_op jit(solution)/shard_map/gradient_transform_sample/pallas_call | solution.py:154
  64.6 18.5 %all_to_all.15 = f32[16,4,2,128]{3,2,1,0:T(2,128)S(1)} all-to-all(f32[16,4,2,128]{3,2,1,0:T(2,128)S(1)} %gradient_transform_sample.1), channel_id=1, replica_groups=mesh['y'=4,'core'=2,'x'=4,'z'=16] {'z'}, dimensions={0} | all-to-all | bytes 131072 | tf_op jit(solution)/shard_map/all_to_all | solution.py:172
  83.1 0.6 broadcast_in_dim.2
  83.7 14.8 %all-to-all-start.2 = ((f32[32,2,128]{2,1,0:T(2,128)}), f32[32,2,128]{2,1,0:T(2,128)S(1)}, u32[]{:S(2)}, u32[]{:S(2)}) async-start(f32[32,2,128]{2,1,0:T(2,128)} %bitcast.3), calls=%async_computation.2 | async-start | bytes 65536 | tf_op jit(solution)/shard_map/all_to_all | solution.py:175
  98.5 7.2 %all-to-all-done.2 = f32[32,2,128]{2,1,0:T(2,128)S(1)} async-done(((f32[32,2,128]{2,1,0:T(2,128)}), f32[32,2,128]{2,1,0:T(2,128)S(1)}, u32[]{:S(2)}, u32[]{:S(2)}) %all-to-all-start.2) | async-done | bytes 32800 | tf_op jit(solution)/shard_map/all_to_all | solution.py:175
  105.7 0.1 reduce_sum.29
  105.8 0.6 bitcast_subtract_fusion
  (5 shorter events, 0.1 us)
Async XLA Ops:
  2.6 5.0 %copy-start.2 = (bf16[2,512,64]{1,2,0:T(8,128)(2,1)S(1)}, bf16[2,512,64]{1,2,0:T(8,128)(2,1)}, u32[]{:S(2)}) copy-start(bf16[2,512,64]{1,2,0:T(8,128)(2,1)} %param.5) | copy-start | bytes 393220
  2.6 51.0 %all-to-all-start = ((bf16[4,1152,256]{2,1,0:T(8,128)(2,1)}), bf16[4,1152,256]{2,1,0:T(8,128)(2,1)S(1)}, u32[]{:S(2)}, u32[]{:S(2)}) async-start(bf16[4,1152,256]{2,1,0:T(8,128)(2,1)} %pack_columns_and_words.1), calls=%async_computation | async-start | bytes 4718592 | tf_op jit(solution)/shard_map/all_to_all | solution.py:148
  51.9 1.7 %copy-start.1 = (s32[8192]{0:T(1024)S(1)}, s32[8192]{0:T(1024)}, u32[]{:S(2)}) copy-start(s32[8192]{0:T(1024)} %param.7) | copy-start | bytes 98308
  53.6 1.6 %copy-start = (bf16[2,1024,512]{2,1,0:T(8,128)(2,1)S(1)}, bf16[2,1024,512]{2,1,0:T(8,128)(2,1)}, u32[]{:S(2)}) copy-start(bf16[2,1024,512]{2,1,0:T(8,128)(2,1)} %convert_convert_fusion.grads) | copy-start | bytes 6291460
  83.7 22.0 %all-to-all-start.2 = ((f32[32,2,128]{2,1,0:T(2,128)}), f32[32,2,128]{2,1,0:T(2,128)S(1)}, u32[]{:S(2)}, u32[]{:S(2)}) async-start(f32[32,2,128]{2,1,0:T(2,128)} %bitcast.3), calls=%async_computation.2 | async-start | bytes 65536 | tf_op jit(solution)/shard_map/all_to_all | solution.py:175

commit v7 on v6

--- a/solution.py
+++ b/solution.py
@@ -70,9 +70,9 @@
     had = jnp.concatenate([had, had], axis=1)
     byte_row = lax.broadcasted_iota(jnp.int32, (32, COLS), 0)
     byte_col = lax.broadcasted_iota(jnp.int32, (32, COLS), 1)
-    spread = (byte_row == (byte_col >> 4) + 16 * ((byte_col >> 3) & 1)).astype(jnp.float32)
+    chosen_byte = byte_row == (byte_col >> 4) + 16 * ((byte_col >> 3) & 1)
+    spread = jnp.where(chosen_byte, 128 >> (byte_col & 7), 0).astype(jnp.float32)
     spread = spread.astype(jnp.bfloat16)
-    shift = lax.broadcasted_iota(jnp.int32, (COLS, COLS), 1) & 7
 
     for block in range(NX):
         for q in range(4):
@@ -80,8 +80,8 @@
             value = lax.dot_general(
                 two, spread, (((0,), (0,)), ((), ())), preferred_element_type=jnp.float32
             )
-            bit = (value.astype(jnp.int32) >> shift) & 1
-            signs[block, pl.ds(q * COLS, COLS), :] = (1 - 2 * bit).astype(jnp.float32)
+            bit = (value.astype(jnp.int32) & 128).astype(jnp.float32)
+            signs[block, pl.ds(q * COLS, COLS), :] = 1.0 - bit * (1.0 / 64.0)
         for example in range(2):
             act = columns[block, pl.ds(example * TOK, TOK), :]
             grad = jnp.dot(grads[example], act, preferred_element_type=jnp.float32)
@@ -100,10 +100,10 @@
     def tile_body(tile, carry):
         idx = jnp.concatenate([idx_ref[pl.ds(tx * NZ + tile, 1), :] for tx in range(NX)], axis=1)
         line = lax.broadcasted_iota(jnp.int32, (16, SAMPLES), 0)
-        low_signs = sign_of(line & idx)
-        high_signs = sign_of(line & (idx >> 4))
+        low_signs = sign_of(line & idx).astype(jnp.bfloat16)
+        high_signs = sign_of(line & (idx >> 4)).astype(jnp.bfloat16)
         weights = jnp.concatenate(
-            [(low_signs * high_signs[a : a + 1]).astype(jnp.bfloat16) for a in range(16)], axis=0
+            [low_signs * high_signs[a : a + 1] for a in range(16)], axis=0
         )
         sign_xz = sign_of(((idx >> 8) & 15 & z) | (((idx >> 24) & 3 & x) << 4))
         sign_1 = sign_of((idx >> 12) & 1)
@@ -149,6 +149,7 @@
 
     wire = jnp.transpose(out_grads, (0, 2, 1)).astype(jnp.float32) * WIRE
     wire = lax.all_gather(wire.astype(jnp.float16), "z", axis=1, tiled=True)
+    wire, columns = lax.optimization_barrier((wire, columns))
     grads = wire.astype(jnp.float32).astype(jnp.bfloat16)
 
     values = pl.pallas_call(

time: 107 us -> 107 us (level)
  local copies, waits for them, and re-layouts: 2.21 us -> 0.62 us
  blocking collectives: 62.8 us -> 64.3 us
    all_gather x1, blocking collectives: 44.3 us -> 45.9 us  [shards(): wire = lax.all_gather(wire.astype(jnp.float16), 'z', axis=1, tiled=True)]
    unnamed x6 -> x4, local copies, waits for them, and re-layouts: 1.6 us -> 0.01 us
  transfers between devices with their start and end apart: 2 -> 2, of which waited for: 1 -> 1; matrix products, arithmetic and copies ran while one was open for 2% -> 0% of each run, Pallas kernels for 0% -> 0%
where the time goes in v7:
time: 107 us
  blocking collectives  64.3 us (60%)
  starting transfers between devices  20.2 us (19%)
  Pallas kernels  11.6 us (11%)
  waiting for transfers between devices  7.21 us (7%)
  other arithmetic  2.66 us (2%)
    all_gather x1, blocking collectives, shards(): wire = lax.all_gather(wire.astype(jnp.float16), 'z', axis=1, tiled=True)  45.9 us
    all_to_all x1, blocking collectives, shards(): lax.all_to_all(values, 'z', split_axis=0, concat_axis=0, tiled=True)  18.4 us
    all_to_all x1, starting transfers between devices, shards(): lax.all_to_all(sent, ex + ('x',), split_axis=0, concat_axis=0, tiled=True)  15.2 us
    pallas_call x1, Pallas kernels, shards(): pl.pallas_call(main_kernel, out_shape=jax.ShapeDtypeStruct((TILES, NX, 2,...  8.96 us
    all_to_all x1, waiting for transfers between devices, shards(): lax.all_to_all(sent, ex + ('x',), split_axis=0, concat_axis=0, tiled=True)  7.21 us
    all_to_all x1, starting transfers between devices, shards(): lax.all_to_all(packed, 'x', split_axis=0, concat_axis=0, tiled=True)  4.99 us
    pallas_call x1, Pallas kernels, shards(): pl.pallas_call(pack_kernel, out_shape=jax.ShapeDtypeStruct((NX, 2 * TOK +...  2.61 us
  transfers between devices with their start and end apart: 2, of which 1 were waited for; matrix products, arithmetic and copies ran while one was open for 0% of the time, Pallas kernels for 0%

profile of v7, /device:TPU:1, one launch (start us, length us, event | category | flops | bytes accessed | tf_op | source)
XLA Modules:
  0.0 106.6 jit_solution(15937586286208351260)
XLA Ops:
  0.0 2.6 %pack_columns_and_words.1 = bf16[4,1152,256]{2,1,0:T(8,128)(2,1)} custom-call(bf16[2,512,256]{2,1,0:T(8,128)(2,1)} %acts_in.1, s32[16,4096]{1,0:T(8,128)} %bitcast.12), custom_call_target="tpu_custom_call" | custom-call | tf_op jit(solution)/shard_map/pack_columns_and_words/pallas_call | solution.py:132
  2.6 0.0 copy-start.1
  2.6 5.0 %all-to-all-start = ((bf16[4,1152,256]{2,1,0:T(8,128)(2,1)}), bf16[4,1152,256]{2,1,0:T(8,128)(2,1)S(1)}, u32[]{:S(2)}, u32[]{:S(2)}) async-start(bf16[4,1152,256]{2,1,0:T(8,128)(2,1)} %pack_columns_and_words.1), calls=%async_computation | async-start | bytes 4718592 | tf_op jit(solution)/shard_map/all_to_all | solution.py:148
  7.6 0.0 copy-done.1
  7.7 45.9 %all-gather.1 = f16[2,1024,512]{2,1,0:T(8,128)(2,1)} all-gather(f16[2,64,512]{2,1,0:T(8,128)(2,1)S(1)} %fusion), channel_id=1, replica_groups=mesh['y'=4,'core'=2,'x'=4,'z'=16] {'z'}, dimensions={1}, use_global_device_ids=true | all-gather | bytes 2228224 | tf_op jit(solution)/shard_map/all_gather | solution.py:151
  53.5 0.0 copy-start
  53.5 0.0 all-to-all-done.columns
  53.5 1.9 %convert_convert_fusion.grads = bf16[2,1024,512]{2,1,0:T(8,128)(2,1)S(1)} fusion(f16[2,1024,512]{2,1,0:T(8,128)(2,1)} %all-gather.1), kind=kLoop, calls=%fused_computation | loop fusion | flops 2097152 | bytes 4194304 | tf_op jit(solution)/shard_map/convert_element_type | solution.py:153
  55.5 0.0 copy-done
  55.5 9.0 %gradient_transform_sample.1 = f32[16,4,2,128]{3,2,1,0:T(2,128)S(1)} custom-call(s32[64,128]{1,0:T(8,128)S(1)} %bitcast.11, bf16[2,1024,512]{2,1,0:T(8,128)(2,1)S(1)} %convert_convert_fusion.grads, bf16[4,1152,256]{2,1,0:T(8,128)(2,1)S(1)} %all-to-all-done.columns), custom_call_target="tpu_custom_call" | custom-call | flops 7000000000 | bytes 8388608 | tf_op jit(solution)/shard_map/gradient_transform_sample/pallas_call | solution.py:155
  64.5 18.4 %all_to_all.15 = f32[16,4,2,128]{3,2,1,0:T(2,128)S(1)} all-to-all(f32[16,4,2,128]{3,2,1,0:T(2,128)S(1)} %gradient_transform_sample.1), channel_id=1, replica_groups=mesh['y'=4,'core'=2,'x'=4,'z'=16] {'z'}, dimensions={0} | all-to-all | bytes 131072 | tf_op jit(solution)/shard_map/all_to_all | solution.py:173
  82.9 0.6 broadcast_in_dim.2
  83.5 15.2 %all-to-all-start.2 = ((f32[32,2,128]{2,1,0:T(2,128)}), f32[32,2,128]{2,1,0:T(2,128)S(1)}, u32[]{:S(2)}, u32[]{:S(2)}) async-start(f32[32,2,128]{2,1,0:T(2,128)} %bitcast.3), calls=%async_computation.2 | async-start | bytes 65536 | tf_op jit(solution)/shard_map/all_to_all | solution.py:176
  98.7 7.2 %all-to-all-done.2 = f32[32,2,128]{2,1,0:T(2,128)S(1)} async-done(((f32[32,2,128]{2,1,0:T(2,128)}), f32[32,2,128]{2,1,0:T(2,128)S(1)}, u32[]{:S(2)}, u32[]{:S(2)}) %all-to-all-start.2) | async-done | bytes 32800 | tf_op jit(solution)/shard_map/all_to_all | solution.py:176
  105.9 0.1 reduce_sum.29
  106.0 0.6 bitcast_subtract_fusion
  (5 shorter events, 0.1 us)
Async XLA Ops:
  2.6 5.0 %copy-start.1 = (bf16[2,512,64]{1,2,0:T(8,128)(2,1)S(1)}, bf16[2,512,64]{1,2,0:T(8,128)(2,1)}, u32[]{:S(2)}) copy-start(bf16[2,512,64]{1,2,0:T(8,128)(2,1)} %param.5) | copy-start | bytes 393220
  2.6 50.9 %all-to-all-start = ((bf16[4,1152,256]{2,1,0:T(8,128)(2,1)}), bf16[4,1152,256]{2,1,0:T(8,128)(2,1)S(1)}, u32[]{:S(2)}, u32[]{:S(2)}) async-start(bf16[4,1152,256]{2,1,0:T(8,128)(2,1)} %pack_columns_and_words.1), calls=%async_computation | async-start | bytes 4718592 | tf_op jit(solution)/shard_map/all_to_all | solution.py:148
  53.5 2.0 %copy-start = (s32[8192]{0:T(1024)S(1)}, s32[8192]{0:T(1024)}, u32[]{:S(2)}) copy-start(s32[8192]{0:T(1024)} %param.7) | copy-start | bytes 98308
  83.5 22.4 %all-to-all-start.2 = ((f32[32,2,128]{2,1,0:T(2,128)}), f32[32,2,128]{2,1,0:T(2,128)S(1)}, u32[]{:S(2)}, u32[]{:S(2)}) async-start(f32[32,2,128]{2,1,0:T(2,128)} %bitcast.3), calls=%async_computation.2 | async-start | bytes 65536 | tf_op jit(solution)/shard_map/all_to_all | solution.py:176

commit v8 on v7

--- a/solution.py
+++ b/solution.py
@@ -42,6 +42,12 @@
         act_copies.append(pltpu.make_async_copy(acts_in.at[example], target, in_sem.at[example]))
         act_copies[-1].start()
     copies = []
+    for copy in act_copies:
+        copy.wait()
+    for target in range(NX):
+        head = out.at[target, pl.ds(0, 2 * TOK)]
+        copies.append(pltpu.make_async_copy(acts, head, act_sem.at[target]))
+        copies[-1].start()
     word_copy.wait()
     for target in range(NX):
         word = words[:, target * ROWS : (target + 1) * ROWS]
@@ -49,19 +55,14 @@
         two = two.astype(jnp.float32).astype(jnp.bfloat16)
         for q in range(4):
             packed[target, pl.ds(32 * q, 32), :] = two[:, q * COLS : (q + 1) * COLS]
-    for copy in act_copies:
-        copy.wait()
-    for target in range(NX):
-        head, tail = out.at[target, pl.ds(0, 2 * TOK)], out.at[target, pl.ds(2 * TOK, 128)]
-        copies.append(pltpu.make_async_copy(acts, head, act_sem.at[target]))
+        tail = out.at[target, pl.ds(2 * TOK, 128)]
         copies.append(pltpu.make_async_copy(packed.at[target], tail, byte_sem.at[target]))
-    for copy in copies:
-        copy.start()
+        copies[-1].start()
     for copy in copies:
         copy.wait()
 
 
-def main_kernel(idx_ref, grads, columns, out_ref, signs, tiles):
+def main_kernel(idx_ref, grads_0, grads_1, columns, out_ref, signs, tiles):
     x, z = lax.axis_index("x"), lax.axis_index("z")
 
     row = lax.broadcasted_iota(jnp.int32, (COLS, COLS), 0)
@@ -82,9 +83,9 @@
             )
             bit = (value.astype(jnp.int32) & 128).astype(jnp.float32)
             signs[block, pl.ds(q * COLS, COLS), :] = 1.0 - bit * (1.0 / 64.0)
-        for example in range(2):
+        for example, grads in enumerate((grads_0, grads_1)):
             act = columns[block, pl.ds(example * TOK, TOK), :]
-            grad = jnp.dot(grads[example], act, preferred_element_type=jnp.float32)
+            grad = jnp.dot(grads[...], act, preferred_element_type=jnp.float32)
             signed = grad * signs[block]
             parts = []
             for b in range(4):
@@ -149,26 +150,25 @@
 
     wire = jnp.transpose(out_grads, (0, 2, 1)).astype(jnp.float32) * WIRE
     wire = lax.all_gather(wire.astype(jnp.float16), "z", axis=1, tiled=True)
-    wire, columns = lax.optimization_barrier((wire, columns))
-    grads = wire.astype(jnp.float32).astype(jnp.bfloat16)
+    grads = [wire[example].astype(jnp.float32).astype(jnp.bfloat16) for example in range(2)]
 
     values = pl.pallas_call(
         main_kernel,
         out_shape=jax.ShapeDtypeStruct((TILES, NX, 2, KDEV), jnp.float32),
-        in_specs=[vmem] * 3,
+        in_specs=[vmem] * 4,
         out_specs=vmem,
         scratch_shapes=[
             pltpu.VMEM((NX, ROWS, COLS), jnp.float32),
             pltpu.VMEM((TILES, 2, NX, LOW, COLS), jnp.bfloat16),
         ],
         compiler_params=pltpu.CompilerParams(
-            vmem_limit_bytes=VMEM_BYTES, allow_input_fusion=[False, True, False]
+            vmem_limit_bytes=VMEM_BYTES, allow_input_fusion=[False, True, True, False]
         ),
         cost_estimate=pl.CostEstimate(
             flops=7 * 10**9, bytes_accessed=8 * 1024 * 1024, transcendentals=0
         ),
         name="gradient_transform_sample",
-    )(indices.reshape(NX * NZ, KDEV), grads, columns)
+    )(indices.reshape(NX * NZ, KDEV), *grads, columns)
 
     along_z = lax.all_to_all(values, "z", split_axis=0, concat_axis=0, tiled=True)
     half = jnp.sum(along_z, axis=0) * SCALE

time: 107 us -> 106 us (level)
  blocking collectives: 64.3 us -> 62.7 us
  local copies, waits for them, and re-layouts: 0.62 us -> 1.85 us
    all_gather x1, blocking collectives: 45.9 us -> 44.3 us  [shards(): wire = lax.all_gather(wire.astype(jnp.float16), 'z', axis=1, tiled=True)]
    unnamed x4 -> x6, local copies, waits for them, and re-layouts: 0.01 us -> 1.24 us
  transfers between devices with their start and end apart: 2 -> 2, of which waited for: 1 -> 1; matrix products, arithmetic and copies ran while one was open for 0% -> 1% of each run, Pallas kernels for 0% -> 0%
where the time goes in v8:
time: 106 us; the launch traced here: 105 us
  blocking collectives  62.7 us (59%)
  starting transfers between devices  19.8 us (19%)
  Pallas kernels  11.6 us (11%)
  waiting for transfers between devices  7.21 us (7%)
  other arithmetic  2.09 us (2%)
  local copies, waits for them, and re-layouts  1.85 us (2%)
    all_gather x1, blocking collectives, shards(): wire = lax.all_gather(wire.astype(jnp.float16), 'z', axis=1, tiled=True)  44.3 us
    all_to_all x1, blocking collectives, shards(): lax.all_to_all(values, 'z', split_axis=0, concat_axis=0, tiled=True)  18.5 us
    all_to_all x1, starting transfers between devices, shards(): lax.all_to_all(sent, ex + ('x',), split_axis=0, concat_axis=0, tiled=True)  14.8 us
    pallas_call x1, Pallas kernels, shards(): pl.pallas_call(main_kernel, out_shape=jax.ShapeDtypeStruct((TILES, NX, 2,...  8.94 us
    all_to_all x1, waiting for transfers between devices, shards(): lax.all_to_all(sent, ex + ('x',), split_axis=0, concat_axis=0, tiled=True)  7.21 us
    all_to_all x1, starting transfers between devices, shards(): lax.all_to_all(packed, 'x', split_axis=0, concat_axis=0, tiled=True)  4.99 us
    pallas_call x1, Pallas kernels, shards(): pl.pallas_call(pack_kernel, out_shape=jax.ShapeDtypeStruct((NX, 2 * TOK +...  2.61 us
  transfers between devices with their start and end apart: 2, of which 1 were waited for; matrix products, arithmetic and copies ran while one was open for 1% of the time, Pallas kernels for 0%

profile of v8, /device:TPU:1, one launch (start us, length us, event | category | flops | bytes accessed | tf_op | source)
XLA Modules:
  0.0 105.3 jit_solution(6088274683000171112)
XLA Ops:
  0.0 2.6 %pack_columns_and_words.1 = bf16[4,1152,256]{2,1,0:T(8,128)(2,1)} custom-call(bf16[2,512,256]{2,1,0:T(8,128)(2,1)} %acts_in.1, s32[16,4096]{1,0:T(8,128)} %bitcast.16), custom_call_target="tpu_custom_call" | custom-call | tf_op jit(solution)/shard_map/pack_columns_and_words/pallas_call | solution.py:133
  2.6 0.0 copy-start.2
  2.6 5.0 %all-to-all-start = ((bf16[4,1152,256]{2,1,0:T(8,128)(2,1)}), bf16[4,1152,256]{2,1,0:T(8,128)(2,1)S(1)}, u32[]{:S(2)}, u32[]{:S(2)}) async-start(bf16[4,1152,256]{2,1,0:T(8,128)(2,1)} %pack_columns_and_words.1), calls=%async_computation | async-start | bytes 4718592 | tf_op jit(solution)/shard_map/all_to_all | solution.py:149
  7.6 0.0 copy-done.2
  7.7 44.3 %all-gather.1 = f16[2,1024,512]{2,1,0:T(8,128)(2,1)S(1)} all-gather(f16[2,64,512]{2,1,0:T(8,128)(2,1)S(1)} %fusion.2), channel_id=1, replica_groups=mesh['y'=4,'core'=2,'x'=4,'z'=16] {'z'}, dimensions={1}, use_global_device_ids=true | all-gather | bytes 2228224 | tf_op jit(solution)/shard_map/all_gather | solution.py:152
  51.9 0.0 copy-start.1
  51.9 1.4 %fusion.1 = (bf16[1024,512]{1,0:T(8,128)(2,1)S(1)}, bf16[1024,512]{1,0:T(8,128)(2,1)}) fusion(f16[2,1024,512]{2,1,0:T(8,128)(2,1)S(1)} %all-gather.1), kind=kLoop, calls=%fused_computation.3 | loop fusion | flops 2097152 | bytes 4194304 | tf_op jit(solution)/shard_map/convert_element_type | solution.py:153
  53.3 0.0 all-to-all-done.columns
  53.3 0.0 copy-done.1
  53.3 0.0 copy-start
  53.3 1.2 %copy-done = bf16[1024,512]{1,0:T(8,128)(2,1)S(1)} copy-done((bf16[1024,512]{1,0:T(8,128)(2,1)S(1)}, bf16[1024,512]{1,0:T(8,128)(2,1)}, u32[]{:S(2)}) %copy-start) | copy-done | bytes 1048600
  54.5 8.9 %gradient_transform_sample.1 = f32[16,4,2,128]{3,2,1,0:T(2,128)S(1)} custom-call(s32[64,128]{1,0:T(8,128)S(1)} %bitcast.15, bf16[1024,512]{1,0:T(8,128)(2,1)S(1)} %copy-done, bf16[1024,512]{1,0:T(8,128)(2,1)S(1)} %get-tuple-element.5.grads_1, bf16[4,1152,256]{2,1,0:T(8,128)(2,1)S(1)} %all-to-all-done.columns), custom_call_target="tpu_custom_call" | custom-call | flops 7000000000 | bytes 8388608 | tf_op jit(solution)/shard_map/gradient_transform_sample/pallas_call | solution.py:155
  63.5 18.5 %all_to_all.15 = f32[16,4,2,128]{3,2,1,0:T(2,128)S(1)} all-to-all(f32[16,4,2,128]{3,2,1,0:T(2,128)S(1)} %gradient_transform_sample.1), channel_id=1, replica_groups=mesh['y'=4,'core'=2,'x'=4,'z'=16] {'z'}, dimensions={0} | all-to-all | bytes 131072 | tf_op jit(solution)/shard_map/all_to_all | solution.py:173
  82.0 0.6 broadcast_in_dim.2
  82.6 14.8 %all-to-all-start.2 = ((f32[32,2,128]{2,1,0:T(2,128)}), f32[32,2,128]{2,1,0:T(2,128)S(1)}, u32[]{:S(2)}, u32[]{:S(2)}) async-start(f32[32,2,128]{2,1,0:T(2,128)} %bitcast.5), calls=%async_computation.2 | async-start | bytes 65536 | tf_op jit(solution)/shard_map/all_to_all | solution.py:176
  97.4 7.2 %all-to-all-done.2 = f32[32,2,128]{2,1,0:T(2,128)S(1)} async-done(((f32[32,2,128]{2,1,0:T(2,128)}), f32[32,2,128]{2,1,0:T(2,128)S(1)}, u32[]{:S(2)}, u32[]{:S(2)}) %all-to-all-start.2) | async-done | bytes 32800 | tf_op jit(solution)/shard_map/all_to_all | solution.py:176
  104.6 0.1 reduce_sum.29
  104.7 0.6 bitcast_subtract_fusion
  (5 shorter events, 0.1 us)
Async XLA Ops:
  2.6 5.0 %copy-start.2 = (bf16[2,512,64]{1,2,0:T(8,128)(2,1)S(1)}, bf16[2,512,64]{1,2,0:T(8,128)(2,1)}, u32[]{:S(2)}) copy-start(bf16[2,512,64]{1,2,0:T(8,128)(2,1)} %param.5) | copy-start | bytes 393220
  2.6 50.6 %all-to-all-start = ((bf16[4,1152,256]{2,1,0:T(8,128)(2,1)}), bf16[4,1152,256]{2,1,0:T(8,128)(2,1)S(1)}, u32[]{:S(2)}, u32[]{:S(2)}) async-start(bf16[4,1152,256]{2,1,0:T(8,128)(2,1)} %pack_columns_and_words.1), calls=%async_computation | async-start | bytes 4718592 | tf_op jit(solution)/shard_map/all_to_all | solution.py:149
  51.9 1.4 %copy-start.1 = (s32[8192]{0:T(1024)S(1)}, s32[8192]{0:T(1024)}, u32[]{:S(2)}) copy-start(s32[8192]{0:T(1024)} %param.7) | copy-start | bytes 98308
  53.3 1.2 %copy-start = (bf16[1024,512]{1,0:T(8,128)(2,1)S(1)}, bf16[1024,512]{1,0:T(8,128)(2,1)}, u32[]{:S(2)}) copy-start(bf16[1024,512]{1,0:T(8,128)(2,1)} %get-tuple-element.6.grads_0) | copy-start | bytes 3145732
  82.6 22.0 %all-to-all-start.2 = ((f32[32,2,128]{2,1,0:T(2,128)}), f32[32,2,128]{2,1,0:T(2,128)S(1)}, u32[]{:S(2)}, u32[]{:S(2)}) async-start(f32[32,2,128]{2,1,0:T(2,128)} %bitcast.5), calls=%async_computation.2 | async-start | bytes 65536 | tf_op jit(solution)/shard_map/all_to_all | solution.py:176

commit v9 on v8

--- a/solution.py
+++ b/solution.py
@@ -85,12 +85,18 @@
             signs[block, pl.ds(q * COLS, COLS), :] = 1.0 - bit * (1.0 / 64.0)
         for example, grads in enumerate((grads_0, grads_1)):
             act = columns[block, pl.ds(example * TOK, TOK), :]
-            grad = jnp.dot(grads[...], act, preferred_element_type=jnp.float32)
+            rows = jnp.concatenate([grads[piece] for piece in range(4)], axis=1)
+            grad = jnp.dot(rows, act, preferred_element_type=jnp.float32)
             signed = grad * signs[block]
-            parts = []
-            for b in range(4):
-                both = jnp.concatenate(split(signed[b * COLS : (b + 1) * COLS]), axis=0)
-                parts.append(jnp.dot(had, both, preferred_element_type=jnp.float32))
+            both = jnp.concatenate(
+                [
+                    jnp.concatenate(split(signed[b * COLS : (b + 1) * COLS]), axis=0)
+                    for b in range(4)
+                ],
+                axis=1,
+            )
+            product = jnp.dot(had, both, preferred_element_type=jnp.float32)
+            parts = [product[:, b * COLS : (b + 1) * COLS] for b in range(4)]
             p0_, p1_ = parts[0] + parts[1], parts[0] - parts[1]
             p2_, p3_ = parts[2] + parts[3], parts[2] - parts[3]
             for a, value in enumerate((p0_ + p2_, p1_ + p3_, p0_ - p2_, p1_ - p3_)):
@@ -148,8 +154,9 @@
     )(activations, jnp.transpose(sign_words, (1, 0)))
     columns = lax.all_to_all(packed, "x", split_axis=0, concat_axis=0, tiled=True)
 
-    wire = jnp.transpose(out_grads, (0, 2, 1)).astype(jnp.float32) * WIRE
-    wire = lax.all_gather(wire.astype(jnp.float16), "z", axis=1, tiled=True)
+    wire = jnp.transpose(out_grads, (0, 2, 1)).reshape(2, LOW, 4, KDEV).transpose(0, 2, 1, 3)
+    wire = (wire.astype(jnp.float32) * WIRE).astype(jnp.float16)
+    wire = lax.all_gather(wire, "z", axis=2, tiled=True)
     grads = [wire[example].astype(jnp.float32).astype(jnp.bfloat16) for example in range(2)]
 
     values = pl.pallas_call(

time: 106 us -> 106 us (level)
  no operation moved by 1% of the time
where the time goes in v9:
time: 106 us; the launch traced here: 105 us
  blocking collectives  62.7 us (59%)
  starting transfers between devices  19.8 us (19%)
  Pallas kernels  11.6 us (11%)
  waiting for transfers between devices  7.21 us (7%)
  other arithmetic  2.06 us (2%)
  local copies, waits for them, and re-layouts  1.85 us (2%)
    all_gather x1, blocking collectives, shards(): wire = lax.all_gather(wire, 'z', axis=2, tiled=True)  44.3 us
    all_to_all x1, blocking collectives, shards(): lax.all_to_all(values, 'z', split_axis=0, concat_axis=0, tiled=True)  18.5 us
    all_to_all x1, starting transfers between devices, shards(): lax.all_to_all(sent, ex + ('x',), split_axis=0, concat_axis=0, tiled=True)  14.8 us
    pallas_call x1, Pallas kernels, shards(): pl.pallas_call(main_kernel, out_shape=jax.ShapeDtypeStruct((TILES, NX, 2,...  8.94 us
    all_to_all x1, waiting for transfers between devices, shards(): lax.all_to_all(sent, ex + ('x',), split_axis=0, concat_axis=0, tiled=True)  7.21 us
    all_to_all x1, starting transfers between devices, shards(): lax.all_to_all(packed, 'x', split_axis=0, concat_axis=0, tiled=True)  4.99 us
    pallas_call x1, Pallas kernels, shards(): pl.pallas_call(pack_kernel, out_shape=jax.ShapeDtypeStruct((NX, 2 * TOK +...  2.61 us
  transfers between devices with their start and end apart: 2, of which 1 were waited for; matrix products, arithmetic and copies ran while one was open for 1% of the time, Pallas kernels for 0%

profile of v9, /device:TPU:1, one launch (start us, length us, event | category | flops | bytes accessed | tf_op | source)
XLA Modules:
  0.0 105.2 jit_solution(8443475654473513111)
XLA Ops:
  0.0 2.6 %pack_columns_and_words.1 = bf16[4,1152,256]{2,1,0:T(8,128)(2,1)} custom-call(bf16[2,512,256]{2,1,0:T(8,128)(2,1)} %acts_in.1, s32[16,4096]{1,0:T(8,128)} %bitcast.22), custom_call_target="tpu_custom_call" | custom-call | tf_op jit(solution)/shard_map/pack_columns_and_words/pallas_call | solution.py:139
  2.6 0.0 copy-start.2
  2.6 5.0 %all-to-all-start = ((bf16[4,1152,256]{2,1,0:T(8,128)(2,1)}), bf16[4,1152,256]{2,1,0:T(8,128)(2,1)S(1)}, u32[]{:S(2)}, u32[]{:S(2)}) async-start(bf16[4,1152,256]{2,1,0:T(8,128)(2,1)} %pack_columns_and_words.1), calls=%async_computation | async-start | bytes 4718592 | tf_op jit(solution)/shard_map/all_to_all | solution.py:155
  7.6 0.0 copy-done.2
  7.7 44.3 %all-gather.1 = f16[2,4,1024,128]{3,2,1,0:T(8,128)(2,1)S(1)} all-gather(f16[2,4,64,128]{3,2,1,0:T(8,128)(2,1)S(1)} %bitcast_bitcast_fusion), channel_id=1, replica_groups=mesh['y'=4,'core'=2,'x'=4,'z'=16] {'z'}, dimensions={2}, use_global_device_ids=true | all-gather | bytes 2228224 | tf_op jit(solution)/shard_map/all_gather | solution.py:159
  51.9 0.0 copy-start.1
  51.9 1.3 %fusion.1 = (bf16[4,1024,128]{2,1,0:T(8,128)(2,1)S(1)}, bf16[4,1024,128]{2,1,0:T(8,128)(2,1)}) fusion(f16[2,4,1024,128]{3,2,1,0:T(8,128)(2,1)S(1)} %all-gather.1), kind=kLoop, calls=%fused_computation.3 | loop fusion | flops 2097152 | bytes 4194304 | tf_op jit(solution)/shard_map/convert_element_type | solution.py:160
  53.2 0.0 all-to-all-done.columns
  53.3 0.0 copy-done.1
  53.3 0.0 copy-start
  53.3 1.2 %copy-done = bf16[4,1024,128]{2,1,0:T(8,128)(2,1)S(1)} copy-done((bf16[4,1024,128]{2,1,0:T(8,128)(2,1)S(1)}, bf16[4,1024,128]{2,1,0:T(8,128)(2,1)}, u32[]{:S(2)}) %copy-start) | copy-done | bytes 1048600
  54.5 8.9 %gradient_transform_sample.1 = f32[16,4,2,128]{3,2,1,0:T(2,128)S(1)} custom-call(s32[64,128]{1,0:T(8,128)S(1)} %bitcast.21, bf16[4,1024,128]{2,1,0:T(8,128)(2,1)S(1)} %copy-done, bf16[4,1024,128]{2,1,0:T(8,128)(2,1)S(1)} %get-tuple-element.5.grads_1, bf16[4,1152,256]{2,1,0:T(8,128)(2,1)S(1)} %all-to-all-done.columns), custom_call_target="tpu_custom_call" | custom-call | flops 7000000000 | bytes 8388608 | tf_op jit(solution)/shard_map/gradient_transform_sample/pallas_call | solution.py:162
  63.4 18.5 %all_to_all.15 = f32[16,4,2,128]{3,2,1,0:T(2,128)S(1)} all-to-all(f32[16,4,2,128]{3,2,1,0:T(2,128)S(1)} %gradient_transform_sample.1), channel_id=1, replica_groups=mesh['y'=4,'core'=2,'x'=4,'z'=16] {'z'}, dimensions={0} | all-to-all | bytes 131072 | tf_op jit(solution)/shard_map/all_to_all | solution.py:180
  82.0 0.6 broadcast_in_dim.2
  82.6 14.8 %all-to-all-start.2 = ((f32[32,2,128]{2,1,0:T(2,128)}), f32[32,2,128]{2,1,0:T(2,128)S(1)}, u32[]{:S(2)}, u32[]{:S(2)}) async-start(f32[32,2,128]{2,1,0:T(2,128)} %bitcast.6), calls=%async_computation.2 | async-start | bytes 65536 | tf_op jit(solution)/shard_map/all_to_all | solution.py:183
  97.4 7.2 %all-to-all-done.2 = f32[32,2,128]{2,1,0:T(2,128)S(1)} async-done(((f32[32,2,128]{2,1,0:T(2,128)}), f32[32,2,128]{2,1,0:T(2,128)S(1)}, u32[]{:S(2)}, u32[]{:S(2)}) %all-to-all-start.2) | async-done | bytes 32800 | tf_op jit(solution)/shard_map/all_to_all | solution.py:183
  104.6 0.1 reduce_sum.29
  104.7 0.6 bitcast_subtract_fusion
  (5 shorter events, 0.1 us)
Async XLA Ops:
  2.6 5.0 %copy-start.2 = (bf16[2,512,64]{1,2,0:T(8,128)(2,1)S(1)}, bf16[2,512,64]{1,2,0:T(8,128)(2,1)}, u32[]{:S(2)}) copy-start(bf16[2,512,64]{1,2,0:T(8,128)(2,1)} %param.5) | copy-start | bytes 393220
  2.6 50.6 %all-to-all-start = ((bf16[4,1152,256]{2,1,0:T(8,128)(2,1)}), bf16[4,1152,256]{2,1,0:T(8,128)(2,1)S(1)}, u32[]{:S(2)}, u32[]{:S(2)}) async-start(bf16[4,1152,256]{2,1,0:T(8,128)(2,1)} %pack_columns_and_words.1), calls=%async_computation | async-start | bytes 4718592 | tf_op jit(solution)/shard_map/all_to_all | solution.py:155
  51.9 1.3 %copy-start.1 = (s32[8192]{0:T(1024)S(1)}, s32[8192]{0:T(1024)}, u32[]{:S(2)}) copy-start(s32[8192]{0:T(1024)} %param.7) | copy-start | bytes 98308
  53.3 1.2 %copy-start = (bf16[4,1024,128]{2,1,0:T(8,128)(2,1)S(1)}, bf16[4,1024,128]{2,1,0:T(8,128)(2,1)}, u32[]{:S(2)}) copy-start(bf16[4,1024,128]{2,1,0:T(8,128)(2,1)} %get-tuple-element.6.grads_0) | copy-start | bytes 3145732
  82.6 22.0 %all-to-all-start.2 = ((f32[32,2,128]{2,1,0:T(2,128)}), f32[32,2,128]{2,1,0:T(2,128)S(1)}, u32[]{:S(2)}, u32[]{:S(2)}) async-start(f32[32,2,128]{2,1,0:T(2,128)} %bitcast.6), calls=%async_computation.2 | async-start | bytes 65536 | tf_op jit(solution)/shard_map/all_to_all | solution.py:183

commit v10 on v8

--- a/solution.py
+++ b/solution.py
@@ -64,6 +64,7 @@
 
 def main_kernel(idx_ref, grads_0, grads_1, columns, out_ref, signs, tiles):
     x, z = lax.axis_index("x"), lax.axis_index("z")
+    core = lax.axis_index("core")
 
     row = lax.broadcasted_iota(jnp.int32, (COLS, COLS), 0)
     col = lax.broadcasted_iota(jnp.int32, (COLS, COLS), 1)
@@ -77,7 +78,8 @@
 
     for block in range(NX):
         for q in range(4):
-            two = columns[block, pl.ds(2 * TOK + 32 * q, 32), :]
+            start = pl.multiple_of(2 * TOK + 32 * (q ^ (2 * core)), 32)
+            two = columns[block, pl.ds(start, 32), :]
             value = lax.dot_general(
                 two, spread, (((0,), (0,)), ((), ())), preferred_element_type=jnp.float32
             )
@@ -106,7 +108,8 @@
         weights = jnp.concatenate(
             [low_signs * high_signs[a : a + 1] for a in range(16)], axis=0
         )
-        sign_xz = sign_of(((idx >> 8) & 15 & z) | (((idx >> 24) & 3 & x) << 4))
+        swap = (tile >> 3) & core
+        sign_xz = sign_of(((idx >> 8) & 15 & z) | (((idx >> 24) & 3 & x) << 4) | (swap << 6))
         sign_1 = sign_of((idx >> 12) & 1)
         sign_2 = sign_of((idx >> 13) & 1)
         chosen = lax.broadcasted_iota(jnp.int32, (LOW, SAMPLES), 0) == ((idx >> 14) & (LOW - 1))
@@ -149,7 +152,10 @@
     columns = lax.all_to_all(packed, "x", split_axis=0, concat_axis=0, tiled=True)
 
     wire = jnp.transpose(out_grads, (0, 2, 1)).astype(jnp.float32) * WIRE
-    wire = lax.all_gather(wire.astype(jnp.float16), "z", axis=1, tiled=True)
+    wire = lax.all_gather(
+        wire.astype(jnp.float16), ("core", "z"), axis=1, tiled=True,
+        axis_index_groups=[list(range(NZ)), [NZ + (i ^ 8) for i in range(NZ)]],
+    )
     grads = [wire[example].astype(jnp.float32).astype(jnp.bfloat16) for example in range(2)]
 
     values = pl.pallas_call(

time: 106 us -> 106 us (level)
  no operation moved by 1% of the time
where the time goes in v10:
time: 106 us; the launch traced here: 105 us
  blocking collectives  62.7 us (59%)
  starting transfers between devices  19.8 us (19%)
  Pallas kernels  11.6 us (11%)
  waiting for transfers between devices  7.21 us (7%)
  other arithmetic  2.09 us (2%)
  local copies, waits for them, and re-layouts  1.85 us (2%)
    all_gather x1, blocking collectives, shards(): lax.all_gather(wire.astype(jnp.float16), ('core', 'z'), axis=1, tiled=Tru...  44.3 us
    all_to_all x1, blocking collectives, shards(): lax.all_to_all(values, 'z', split_axis=0, concat_axis=0, tiled=True)  18.5 us
    all_to_all x1, starting transfers between devices, shards(): lax.all_to_all(sent, ex + ('x',), split_axis=0, concat_axis=0, tiled=True)  14.8 us
    pallas_call x1, Pallas kernels, shards(): pl.pallas_call(main_kernel, out_shape=jax.ShapeDtypeStruct((TILES, NX, 2,...  8.98 us
    all_to_all x1, waiting for transfers between devices, shards(): lax.all_to_all(sent, ex + ('x',), split_axis=0, concat_axis=0, tiled=True)  7.21 us
    all_to_all x1, starting transfers between devices, shards(): lax.all_to_all(packed, 'x', split_axis=0, concat_axis=0, tiled=True)  4.99 us
    pallas_call x1, Pallas kernels, shards(): pl.pallas_call(pack_kernel, out_shape=jax.ShapeDtypeStruct((NX, 2 * TOK +...  2.61 us
  transfers between devices with their start and end apart: 2, of which 1 were waited for; matrix products, arithmetic and copies ran while one was open for 1% of the time, Pallas kernels for 0%

profile of v10, /device:TPU:1, one launch (start us, length us, event | category | flops | bytes accessed | tf_op | source)
XLA Modules:
  0.0 105.3 jit_solution(8083526862095099360)
XLA Ops:
  0.0 2.6 %pack_columns_and_words.1 = bf16[4,1152,256]{2,1,0:T(8,128)(2,1)} custom-call(bf16[2,512,256]{2,1,0:T(8,128)(2,1)} %acts_in.1, s32[16,4096]{1,0:T(8,128)} %bitcast.16), custom_call_target="tpu_custom_call" | custom-call | tf_op jit(solution)/shard_map/pack_columns_and_words/pallas_call | solution.py:136
  2.6 0.0 copy-start.2
  2.6 5.0 %all-to-all-start = ((bf16[4,1152,256]{2,1,0:T(8,128)(2,1)}), bf16[4,1152,256]{2,1,0:T(8,128)(2,1)S(1)}, u32[]{:S(2)}, u32[]{:S(2)}) async-start(bf16[4,1152,256]{2,1,0:T(8,128)(2,1)} %pack_columns_and_words.1), calls=%async_computation | async-start | bytes 4718592 | tf_op jit(solution)/shard_map/all_to_all | solution.py:152
  7.6 0.0 copy-done.2
  7.7 44.3 %all-gather.1 = f16[2,1024,512]{2,1,0:T(8,128)(2,1)S(1)} all-gather(f16[2,64,512]{2,1,0:T(8,128)(2,1)S(1)} %fusion.2), channel_id=1, replica_groups={{0,1,2,3,4,5,6,7,8,9,10,11,12,13,14,15},{72,73,74,75,76,77,78,79,64,65,..., dimensions={1}, use_global_device_ids=true | all-gather | bytes 2228224 | tf_op jit(solution)/shard_map/all_gather | solution.py:155
  51.9 0.0 copy-start.1
  51.9 1.4 %fusion.1 = (bf16[1024,512]{1,0:T(8,128)(2,1)S(1)}, bf16[1024,512]{1,0:T(8,128)(2,1)}) fusion(f16[2,1024,512]{2,1,0:T(8,128)(2,1)S(1)} %all-gather.1), kind=kLoop, calls=%fused_computation.3 | loop fusion | flops 2097152 | bytes 4194304 | tf_op jit(solution)/shard_map/convert_element_type | solution.py:159
  53.3 0.0 all-to-all-done.columns
  53.3 0.0 copy-done.1
  53.3 0.0 copy-start
  53.3 1.2 %copy-done = bf16[1024,512]{1,0:T(8,128)(2,1)S(1)} copy-done((bf16[1024,512]{1,0:T(8,128)(2,1)S(1)}, bf16[1024,512]{1,0:T(8,128)(2,1)}, u32[]{:S(2)}) %copy-start) | copy-done | bytes 1048600
  54.5 9.0 %gradient_transform_sample.1 = f32[16,4,2,128]{3,2,1,0:T(2,128)S(1)} custom-call(s32[64,128]{1,0:T(8,128)S(1)} %bitcast.15, bf16[1024,512]{1,0:T(8,128)(2,1)S(1)} %copy-done, bf16[1024,512]{1,0:T(8,128)(2,1)S(1)} %get-tuple-element.5.grads_1, bf16[4,1152,256]{2,1,0:T(8,128)(2,1)S(1)} %all-to-all-done.columns), custom_call_target="tpu_custom_call" | custom-call | flops 7000000000 | bytes 8388608 | tf_op jit(solution)/shard_map/gradient_transform_sample/pallas_call | solution.py:161
  63.5 18.5 %all_to_all.15 = f32[16,4,2,128]{3,2,1,0:T(2,128)S(1)} all-to-all(f32[16,4,2,128]{3,2,1,0:T(2,128)S(1)} %gradient_transform_sample.1), channel_id=1, replica_groups=mesh['y'=4,'core'=2,'x'=4,'z'=16] {'z'}, dimensions={0} | all-to-all | bytes 131072 | tf_op jit(solution)/shard_map/all_to_all | solution.py:179
  82.0 0.6 broadcast_in_dim.2
  82.7 14.8 %all-to-all-start.2 = ((f32[32,2,128]{2,1,0:T(2,128)}), f32[32,2,128]{2,1,0:T(2,128)S(1)}, u32[]{:S(2)}, u32[]{:S(2)}) async-start(f32[32,2,128]{2,1,0:T(2,128)} %bitcast.5), calls=%async_computation.2 | async-start | bytes 65536 | tf_op jit(solution)/shard_map/all_to_all | solution.py:182
  97.4 7.2 %all-to-all-done.2 = f32[32,2,128]{2,1,0:T(2,128)S(1)} async-done(((f32[32,2,128]{2,1,0:T(2,128)}), f32[32,2,128]{2,1,0:T(2,128)S(1)}, u32[]{:S(2)}, u32[]{:S(2)}) %all-to-all-start.2) | async-done | bytes 32800 | tf_op jit(solution)/shard_map/all_to_all | solution.py:182
  104.7 0.1 reduce_sum.29
  104.7 0.6 bitcast_subtract_fusion
  (5 shorter events, 0.1 us)
Async XLA Ops:
  2.6 5.0 %copy-start.2 = (bf16[2,512,64]{1,2,0:T(8,128)(2,1)S(1)}, bf16[2,512,64]{1,2,0:T(8,128)(2,1)}, u32[]{:S(2)}) copy-start(bf16[2,512,64]{1,2,0:T(8,128)(2,1)} %param.5) | copy-start | bytes 393220
  2.6 50.6 %all-to-all-start = ((bf16[4,1152,256]{2,1,0:T(8,128)(2,1)}), bf16[4,1152,256]{2,1,0:T(8,128)(2,1)S(1)}, u32[]{:S(2)}, u32[]{:S(2)}) async-start(bf16[4,1152,256]{2,1,0:T(8,128)(2,1)} %pack_columns_and_words.1), calls=%async_computation | async-start | bytes 4718592 | tf_op jit(solution)/shard_map/all_to_all | solution.py:152
  51.9 1.4 %copy-start.1 = (s32[8192]{0:T(1024)S(1)}, s32[8192]{0:T(1024)}, u32[]{:S(2)}) copy-start(s32[8192]{0:T(1024)} %param.7) | copy-start | bytes 98308
  53.3 1.2 %copy-start = (bf16[1024,512]{1,0:T(8,128)(2,1)S(1)}, bf16[1024,512]{1,0:T(8,128)(2,1)}, u32[]{:S(2)}) copy-start(bf16[1024,512]{1,0:T(8,128)(2,1)} %get-tuple-element.6.grads_0) | copy-start | bytes 3145732
  82.7 22.0 %all-to-all-start.2 = ((f32[32,2,128]{2,1,0:T(2,128)}), f32[32,2,128]{2,1,0:T(2,128)S(1)}, u32[]{:S(2)}, u32[]{:S(2)}) async-start(f32[32,2,128]{2,1,0:T(2,128)} %bitcast.5), calls=%async_computation.2 | async-start | bytes 65536 | tf_op jit(solution)/shard_map/all_to_all | solution.py:182

commit v11 on v8

--- a/solution.py
+++ b/solution.py
@@ -45,9 +45,13 @@
     for copy in act_copies:
         copy.wait()
     for target in range(NX):
-        head = out.at[target, pl.ds(0, 2 * TOK)]
-        copies.append(pltpu.make_async_copy(acts, head, act_sem.at[target]))
-        copies[-1].start()
+        for piece in range(4):
+            rows = pl.ds(piece * COLS, COLS)
+            copy = pltpu.make_async_copy(
+                acts.at[rows], out.at[target, rows], act_sem.at[target, piece]
+            )
+            copy.start()
+            copies.append(copy)
     word_copy.wait()
     for target in range(NX):
         word = words[:, target * ROWS : (target + 1) * ROWS]
@@ -63,7 +67,7 @@
 
 
 def main_kernel(idx_ref, grads_0, grads_1, columns, out_ref, signs, tiles):
-    x, z = lax.axis_index("x"), lax.axis_index("z")
+    z = lax.axis_index("z")
 
     row = lax.broadcasted_iota(jnp.int32, (COLS, COLS), 0)
     col = lax.broadcasted_iota(jnp.int32, (COLS, COLS), 1)
@@ -106,7 +110,7 @@
         weights = jnp.concatenate(
             [low_signs * high_signs[a : a + 1] for a in range(16)], axis=0
         )
-        sign_xz = sign_of(((idx >> 8) & 15 & z) | (((idx >> 24) & 3 & x) << 4))
+        sign_z = sign_of((idx >> 8) & 15 & z)
         sign_1 = sign_of((idx >> 12) & 1)
         sign_2 = sign_of((idx >> 13) & 1)
         chosen = lax.broadcasted_iota(jnp.int32, (LOW, SAMPLES), 0) == ((idx >> 14) & (LOW - 1))
@@ -117,7 +121,7 @@
                 both[(example * NX + j) * LOW : (example * NX + j + 1) * LOW] for j in range(NX)
             ]
             total = (b0 + b1 * sign_1) + (b2 + b3 * sign_1) * sign_2
-            picked = jnp.sum(jnp.where(chosen, total, 0.0), axis=0, keepdims=True) * sign_xz
+            picked = jnp.sum(jnp.where(chosen, total, 0.0), axis=0, keepdims=True) * sign_z
             for tx in range(NX):
                 out_ref[tile, tx, pl.ds(example, 1), :] = picked[:, tx * KDEV : (tx + 1) * KDEV]
         return carry
@@ -140,7 +144,7 @@
             pltpu.VMEM((FF // 1024, D), jnp.int32),
             pltpu.VMEM((NX, 128, COLS), jnp.bfloat16),
             pltpu.SemaphoreType.DMA((3,)),
-            pltpu.SemaphoreType.DMA((NX,)),
+            pltpu.SemaphoreType.DMA((NX, 4)),
             pltpu.SemaphoreType.DMA((NX,)),
         ],
         compiler_params=pltpu.CompilerParams(vmem_limit_bytes=60 * 1024 * 1024),
@@ -171,7 +175,11 @@
     )(indices.reshape(NX * NZ, KDEV), *grads, columns)
 
     along_z = lax.all_to_all(values, "z", split_axis=0, concat_axis=0, tiled=True)
-    half = jnp.sum(along_z, axis=0) * SCALE
+    own_indices = lax.dynamic_index_in_dim(
+        indices.reshape(NX, NZ, KDEV), lax.axis_index("z"), axis=1, keepdims=False
+    )
+    own_signs = sign_of((own_indices >> 24) & lax.axis_index("x")) * SCALE
+    half = jnp.sum(along_z, axis=0) * own_signs[:, None, :]
     sent = jnp.broadcast_to(half[None], (ex_size, NX, 2, KDEV)).reshape(ex_size * NX, 2, KDEV)
     received = lax.all_to_all(sent, ex + ("x",), split_axis=0, concat_axis=0, tiled=True)
     raw = jnp.sum(received.reshape(ex_size, NX, 2, KDEV), axis=1)

time: 106 us -> 106 us (level)
  blocking collectives: 62.7 us -> 44.3 us
  waiting for transfers between devices: 7.21 us -> 18.7 us
  starting transfers between devices: 19.8 us -> 26.9 us
    all_to_all x1 -> x0, blocking collectives: 18.5 us -> none  [shards(): lax.all_to_all(values, 'z', split_axis=0, concat_axis=0, tiled=True)]
    all_to_all x0 -> x1, waiting for transfers between devices: none -> 11.5 us  [shards(): lax.all_to_all(values, 'z', split_axis=0, concat_axis=0, tiled=True)]
    all_to_all x0 -> x1, starting transfers between devices: none -> 7.13 us  [shards(): lax.all_to_all(values, 'z', split_axis=0, concat_axis=0, tiled=True)]
  transfers between devices with their start and end apart: 2 -> 3, of which waited for: 1 -> 2; matrix products, arithmetic and copies ran while one was open for 1% -> 1% of each run, Pallas kernels for 0% -> 0%
where the time goes in v11:
time: 106 us
  blocking collectives  44.3 us (42%)
  starting transfers between devices  26.9 us (25%)
  waiting for transfers between devices  18.7 us (18%)
  Pallas kernels  12.2 us (12%)
  other arithmetic  2.09 us (2%)
  local copies, waits for them, and re-layouts  1.86 us (2%)
    all_gather x1, blocking collectives, shards(): wire = lax.all_gather(wire.astype(jnp.float16), 'z', axis=1, tiled=True)  44.3 us
    all_to_all x1, starting transfers between devices, shards(): lax.all_to_all(sent, ex + ('x',), split_axis=0, concat_axis=0, tiled=True)  14.8 us
    all_to_all x1, waiting for transfers between devices, shards(): lax.all_to_all(values, 'z', split_axis=0, concat_axis=0, tiled=True)  11.5 us
    pallas_call x1, Pallas kernels, shards(): pl.pallas_call(main_kernel, out_shape=jax.ShapeDtypeStruct((TILES, NX, 2,...  9.51 us
    all_to_all x1, waiting for transfers between devices, shards(): lax.all_to_all(sent, ex + ('x',), split_axis=0, concat_axis=0, tiled=True)  7.21 us
    all_to_all x1, starting transfers between devices, shards(): lax.all_to_all(values, 'z', split_axis=0, concat_axis=0, tiled=True)  7.13 us
    all_to_all x1, starting transfers between devices, shards(): lax.all_to_all(packed, 'x', split_axis=0, concat_axis=0, tiled=True)  4.99 us
    pallas_call x1, Pallas kernels, shards(): pl.pallas_call(pack_kernel, out_shape=jax.ShapeDtypeStruct((NX, 2 * TOK +...  2.73 us
  transfers between devices with their start and end apart: 3, of which 2 were waited for; matrix products, arithmetic and copies ran while one was open for 1% of the time, Pallas kernels for 0%

profile of v11, /device:TPU:1, one launch (start us, length us, event | category | flops | bytes accessed | tf_op | source)
XLA Modules:
  0.0 106.1 jit_solution(17848813193081393188)
XLA Ops:
  0.0 2.7 %pack_columns_and_words.1 = bf16[4,1152,256]{2,1,0:T(8,128)(2,1)} custom-call(bf16[2,512,256]{2,1,0:T(8,128)(2,1)} %acts_in.1, s32[16,4096]{1,0:T(8,128)} %bitcast.21), custom_call_target="tpu_custom_call" | custom-call | tf_op jit(solution)/shard_map/pack_columns_and_words/pallas_call | solution.py:137
  2.7 0.0 copy-start.2
  2.7 5.0 %all-to-all-start = ((bf16[4,1152,256]{2,1,0:T(8,128)(2,1)}), bf16[4,1152,256]{2,1,0:T(8,128)(2,1)S(1)}, u32[]{:S(2)}, u32[]{:S(2)}) async-start(bf16[4,1152,256]{2,1,0:T(8,128)(2,1)} %pack_columns_and_words.1), calls=%async_computation | async-start | bytes 4718592 | tf_op jit(solution)/shard_map/all_to_all | solution.py:153
  7.7 0.0 copy-done.2
  7.8 44.3 %all-gather.1 = f16[2,1024,512]{2,1,0:T(8,128)(2,1)S(1)} all-gather(f16[2,64,512]{2,1,0:T(8,128)(2,1)S(1)} %fusion.2), channel_id=1, replica_groups=mesh['y'=4,'core'=2,'x'=4,'z'=16] {'z'}, dimensions={1}, use_global_device_ids=true | all-gather | bytes 2228224 | tf_op jit(solution)/shard_map/all_gather | solution.py:156
  52.0 0.0 copy-start.1
  52.0 1.4 %fusion.1 = (bf16[1024,512]{1,0:T(8,128)(2,1)S(1)}, bf16[1024,512]{1,0:T(8,128)(2,1)}) fusion(f16[2,1024,512]{2,1,0:T(8,128)(2,1)S(1)} %all-gather.1), kind=kLoop, calls=%fused_computation.3 | loop fusion | flops 2097152 | bytes 4194304 | tf_op jit(solution)/shard_map/convert_element_type | solution.py:157
  53.4 0.0 all-to-all-done.columns
  53.4 0.0 copy-done.1
  53.4 0.0 copy-start
  53.4 1.2 %copy-done = bf16[1024,512]{1,0:T(8,128)(2,1)S(1)} copy-done((bf16[1024,512]{1,0:T(8,128)(2,1)S(1)}, bf16[1024,512]{1,0:T(8,128)(2,1)}, u32[]{:S(2)}) %copy-start) | copy-done | bytes 1048600
  54.6 9.5 %gradient_transform_sample.1 = f32[16,4,2,128]{3,2,1,0:T(2,128)} custom-call(s32[64,128]{1,0:T(8,128)S(1)} %bitcast.19, bf16[1024,512]{1,0:T(8,128)(2,1)S(1)} %copy-done, bf16[1024,512]{1,0:T(8,128)(2,1)S(1)} %get-tuple-element.5.grads_1, bf16[4,1152,256]{2,1,0:T(8,128)(2,1)S(1)} %all-to-all-done.columns), custom_call_target="tpu_custom_call" | custom-call | flops 7000000000 | bytes 8388608 | tf_op jit(solution)/shard_map/gradient_transform_sample/pallas_call | solution.py:159
  64.1 7.1 %all-to-all-start.1 = ((f32[16,4,2,128]{3,2,1,0:T(2,128)}), f32[16,4,2,128]{3,2,1,0:T(2,128)S(1)}, u32[]{:S(2)}, u32[]{:S(2)}) async-start(f32[16,4,2,128]{3,2,1,0:T(2,128)} %gradient_transform_sample.1), calls=%async_computation.1 | async-start | bytes 131072 | tf_op jit(solution)/shard_map/all_to_all | solution.py:177
  71.3 11.5 %all-to-all-done.1 = f32[16,4,2,128]{3,2,1,0:T(2,128)S(1)} async-done(((f32[16,4,2,128]{3,2,1,0:T(2,128)}), f32[16,4,2,128]{3,2,1,0:T(2,128)S(1)}, u32[]{:S(2)}, u32[]{:S(2)}) %all-to-all-start.1) | async-done | bytes 65568 | tf_op jit(solution)/shard_map/all_to_all | solution.py:177
  82.9 0.6 broadcast_in_dim.2
  83.5 14.8 %all-to-all-start.2 = ((f32[32,2,128]{2,1,0:T(2,128)}), f32[32,2,128]{2,1,0:T(2,128)S(1)}, u32[]{:S(2)}, u32[]{:S(2)}) async-start(f32[32,2,128]{2,1,0:T(2,128)} %bitcast.7), calls=%async_computation.2 | async-start | bytes 65536 | tf_op jit(solution)/shard_map/all_to_all | solution.py:184
  98.3 7.2 %all-to-all-done.2 = f32[32,2,128]{2,1,0:T(2,128)S(1)} async-done(((f32[32,2,128]{2,1,0:T(2,128)}), f32[32,2,128]{2,1,0:T(2,128)S(1)}, u32[]{:S(2)}, u32[]{:S(2)}) %all-to-all-start.2) | async-done | bytes 32800 | tf_op jit(solution)/shard_map/all_to_all | solution.py:184
  105.5 0.1 reduce_sum.29
  105.6 0.6 bitcast_subtract_fusion
  (7 shorter events, 0.1 us)
Async XLA Ops:
  2.7 5.0 %copy-start.2 = (bf16[2,512,64]{1,2,0:T(8,128)(2,1)S(1)}, bf16[2,512,64]{1,2,0:T(8,128)(2,1)}, u32[]{:S(2)}) copy-start(bf16[2,512,64]{1,2,0:T(8,128)(2,1)} %param.5) | copy-start | bytes 393220
  2.7 50.6 %all-to-all-start = ((bf16[4,1152,256]{2,1,0:T(8,128)(2,1)}), bf16[4,1152,256]{2,1,0:T(8,128)(2,1)S(1)}, u32[]{:S(2)}, u32[]{:S(2)}) async-start(bf16[4,1152,256]{2,1,0:T(8,128)(2,1)} %pack_columns_and_words.1), calls=%async_computation | async-start | bytes 4718592 | tf_op jit(solution)/shard_map/all_to_all | solution.py:153
  52.0 1.4 %copy-start.1 = (s32[8192]{0:T(1024)S(1)}, s32[8192]{0:T(1024)}, u32[]{:S(2)}) copy-start(s32[8192]{0:T(1024)} %param.7) | copy-start | bytes 98308
  53.4 1.2 %copy-start = (bf16[1024,512]{1,0:T(8,128)(2,1)S(1)}, bf16[1024,512]{1,0:T(8,128)(2,1)}, u32[]{:S(2)}) copy-start(bf16[1024,512]{1,0:T(8,128)(2,1)} %get-tuple-element.6.grads_0) | copy-start | bytes 3145732
  64.1 18.7 %all-to-all-start.1 = ((f32[16,4,2,128]{3,2,1,0:T(2,128)}), f32[16,4,2,128]{3,2,1,0:T(2,128)S(1)}, u32[]{:S(2)}, u32[]{:S(2)}) async-start(f32[16,4,2,128]{3,2,1,0:T(2,128)} %gradient_transform_sample.1), calls=%async_computation.1 | async-start | bytes 131072 | tf_op jit(solution)/shard_map/all_to_all | solution.py:177
  83.5 22.0 %all-to-all-start.2 = ((f32[32,2,128]{2,1,0:T(2,128)}), f32[32,2,128]{2,1,0:T(2,128)S(1)}, u32[]{:S(2)}, u32[]{:S(2)}) async-start(f32[32,2,128]{2,1,0:T(2,128)} %bitcast.7), calls=%async_computation.2 | async-start | bytes 65536 | tf_op jit(solution)/shard_map/all_to_all | solution.py:184

commit v12 on v8

--- a/solution.py
+++ b/solution.py
@@ -62,7 +62,7 @@
         copy.wait()
 
 
-def main_kernel(idx_ref, grads_0, grads_1, columns, out_ref, signs, tiles):
+def main_kernel(idx_ref, grads_0, grads_1, columns, out_ref, tiles):
     x, z = lax.axis_index("x"), lax.axis_index("z")
 
     row = lax.broadcasted_iota(jnp.int32, (COLS, COLS), 0)
@@ -76,17 +76,19 @@
     spread = spread.astype(jnp.bfloat16)
 
     for block in range(NX):
+        chunks = []
         for q in range(4):
             two = columns[block, pl.ds(2 * TOK + 32 * q, 32), :]
             value = lax.dot_general(
                 two, spread, (((0,), (0,)), ((), ())), preferred_element_type=jnp.float32
             )
             bit = (value.astype(jnp.int32) & 128).astype(jnp.float32)
-            signs[block, pl.ds(q * COLS, COLS), :] = 1.0 - bit * (1.0 / 64.0)
+            chunks.append(1.0 - bit * (1.0 / 64.0))
+        signs = jnp.concatenate(chunks, axis=0)
         for example, grads in enumerate((grads_0, grads_1)):
             act = columns[block, pl.ds(example * TOK, TOK), :]
             grad = jnp.dot(grads[...], act, preferred_element_type=jnp.float32)
-            signed = grad * signs[block]
+            signed = grad * signs
             parts = []
             for b in range(4):
                 both = jnp.concatenate(split(signed[b * COLS : (b + 1) * COLS]), axis=0)
@@ -158,7 +160,6 @@
         in_specs=[vmem] * 4,
         out_specs=vmem,
         scratch_shapes=[
-            pltpu.VMEM((NX, ROWS, COLS), jnp.float32),
             pltpu.VMEM((TILES, 2, NX, LOW, COLS), jnp.bfloat16),
         ],
         compiler_params=pltpu.CompilerParams(

time: 106 us -> 106 us (level)
  no operation moved by 1% of the time
where the time goes in v12:
time: 106 us; the launch traced here: 105 us
  blocking collectives  62.7 us (59%)
  starting transfers between devices  19.8 us (19%)
  Pallas kernels  11.6 us (11%)
  waiting for transfers between devices  7.21 us (7%)
  other arithmetic  2.09 us (2%)
  local copies, waits for them, and re-layouts  1.85 us (2%)
    all_gather x1, blocking collectives, shards(): wire = lax.all_gather(wire.astype(jnp.float16), 'z', axis=1, tiled=True)  44.3 us
    all_to_all x1, blocking collectives, shards(): lax.all_to_all(values, 'z', split_axis=0, concat_axis=0, tiled=True)  18.5 us
    all_to_all x1, starting transfers between devices, shards(): lax.all_to_all(sent, ex + ('x',), split_axis=0, concat_axis=0, tiled=True)  14.8 us
    pallas_call x1, Pallas kernels, shards(): pl.pallas_call(main_kernel, out_shape=jax.ShapeDtypeStruct((TILES, NX, 2,...  8.94 us
    all_to_all x1, waiting for transfers between devices, shards(): lax.all_to_all(sent, ex + ('x',), split_axis=0, concat_axis=0, tiled=True)  7.21 us
    all_to_all x1, starting transfers between devices, shards(): lax.all_to_all(packed, 'x', split_axis=0, concat_axis=0, tiled=True)  4.99 us
    pallas_call x1, Pallas kernels, shards(): pl.pallas_call(pack_kernel, out_shape=jax.ShapeDtypeStruct((NX, 2 * TOK +...  2.61 us
  transfers between devices with their start and end apart: 2, of which 1 were waited for; matrix products, arithmetic and copies ran while one was open for 1% of the time, Pallas kernels for 0%

profile of v12, /device:TPU:1, one launch (start us, length us, event | category | flops | bytes accessed | tf_op | source)
XLA Modules:
  0.0 105.3 jit_solution(6088274683000171112)
XLA Ops:
  0.0 2.6 %pack_columns_and_words.1 = bf16[4,1152,256]{2,1,0:T(8,128)(2,1)} custom-call(bf16[2,512,256]{2,1,0:T(8,128)(2,1)} %acts_in.1, s32[16,4096]{1,0:T(8,128)} %bitcast.16), custom_call_target="tpu_custom_call" | custom-call | tf_op jit(solution)/shard_map/pack_columns_and_words/pallas_call | solution.py:135
  2.6 0.0 copy-start.2
  2.6 5.0 %all-to-all-start = ((bf16[4,1152,256]{2,1,0:T(8,128)(2,1)}), bf16[4,1152,256]{2,1,0:T(8,128)(2,1)S(1)}, u32[]{:S(2)}, u32[]{:S(2)}) async-start(bf16[4,1152,256]{2,1,0:T(8,128)(2,1)} %pack_columns_and_words.1), calls=%async_computation | async-start | bytes 4718592 | tf_op jit(solution)/shard_map/all_to_all | solution.py:151
  7.6 0.0 copy-done.2
  7.7 44.3 %all-gather.1 = f16[2,1024,512]{2,1,0:T(8,128)(2,1)S(1)} all-gather(f16[2,64,512]{2,1,0:T(8,128)(2,1)S(1)} %fusion.2), channel_id=1, replica_groups=mesh['y'=4,'core'=2,'x'=4,'z'=16] {'z'}, dimensions={1}, use_global_device_ids=true | all-gather | bytes 2228224 | tf_op jit(solution)/shard_map/all_gather | solution.py:154
  51.9 0.0 copy-start.1
  51.9 1.4 %fusion.1 = (bf16[1024,512]{1,0:T(8,128)(2,1)S(1)}, bf16[1024,512]{1,0:T(8,128)(2,1)}) fusion(f16[2,1024,512]{2,1,0:T(8,128)(2,1)S(1)} %all-gather.1), kind=kLoop, calls=%fused_computation.3 | loop fusion | flops 2097152 | bytes 4194304 | tf_op jit(solution)/shard_map/convert_element_type | solution.py:155
  53.3 0.0 all-to-all-done.columns
  53.3 0.0 copy-done.1
  53.3 0.0 copy-start
  53.3 1.2 %copy-done = bf16[1024,512]{1,0:T(8,128)(2,1)S(1)} copy-done((bf16[1024,512]{1,0:T(8,128)(2,1)S(1)}, bf16[1024,512]{1,0:T(8,128)(2,1)}, u32[]{:S(2)}) %copy-start) | copy-done | bytes 1048600
  54.5 8.9 %gradient_transform_sample.1 = f32[16,4,2,128]{3,2,1,0:T(2,128)S(1)} custom-call(s32[64,128]{1,0:T(8,128)S(1)} %bitcast.15, bf16[1024,512]{1,0:T(8,128)(2,1)S(1)} %copy-done, bf16[1024,512]{1,0:T(8,128)(2,1)S(1)} %get-tuple-element.5.grads_1, bf16[4,1152,256]{2,1,0:T(8,128)(2,1)S(1)} %all-to-all-done.columns), custom_call_target="tpu_custom_call" | custom-call | flops 7000000000 | bytes 8388608 | tf_op jit(solution)/shard_map/gradient_transform_sample/pallas_call | solution.py:157
  63.5 18.5 %all_to_all.15 = f32[16,4,2,128]{3,2,1,0:T(2,128)S(1)} all-to-all(f32[16,4,2,128]{3,2,1,0:T(2,128)S(1)} %gradient_transform_sample.1), channel_id=1, replica_groups=mesh['y'=4,'core'=2,'x'=4,'z'=16] {'z'}, dimensions={0} | all-to-all | bytes 131072 | tf_op jit(solution)/shard_map/all_to_all | solution.py:174
  82.0 0.6 broadcast_in_dim.2
  82.6 14.8 %all-to-all-start.2 = ((f32[32,2,128]{2,1,0:T(2,128)}), f32[32,2,128]{2,1,0:T(2,128)S(1)}, u32[]{:S(2)}, u32[]{:S(2)}) async-start(f32[32,2,128]{2,1,0:T(2,128)} %bitcast.5), calls=%async_computation.2 | async-start | bytes 65536 | tf_op jit(solution)/shard_map/all_to_all | solution.py:177
  97.4 7.2 %all-to-all-done.2 = f32[32,2,128]{2,1,0:T(2,128)S(1)} async-done(((f32[32,2,128]{2,1,0:T(2,128)}), f32[32,2,128]{2,1,0:T(2,128)S(1)}, u32[]{:S(2)}, u32[]{:S(2)}) %all-to-all-start.2) | async-done | bytes 32800 | tf_op jit(solution)/shard_map/all_to_all | solution.py:177
  104.6 0.1 reduce_sum.29
  104.7 0.6 bitcast_subtract_fusion
  (5 shorter events, 0.1 us)
Async XLA Ops:
  2.6 5.0 %copy-start.2 = (bf16[2,512,64]{1,2,0:T(8,128)(2,1)S(1)}, bf16[2,512,64]{1,2,0:T(8,128)(2,1)}, u32[]{:S(2)}) copy-start(bf16[2,512,64]{1,2,0:T(8,128)(2,1)} %param.5) | copy-start | bytes 393220
  2.6 50.6 %all-to-all-start = ((bf16[4,1152,256]{2,1,0:T(8,128)(2,1)}), bf16[4,1152,256]{2,1,0:T(8,128)(2,1)S(1)}, u32[]{:S(2)}, u32[]{:S(2)}) async-start(bf16[4,1152,256]{2,1,0:T(8,128)(2,1)} %pack_columns_and_words.1), calls=%async_computation | async-start | bytes 4718592 | tf_op jit(solution)/shard_map/all_to_all | solution.py:151
  51.9 1.4 %copy-start.1 = (s32[8192]{0:T(1024)S(1)}, s32[8192]{0:T(1024)}, u32[]{:S(2)}) copy-start(s32[8192]{0:T(1024)} %param.7) | copy-start | bytes 98308
  53.3 1.2 %copy-start = (bf16[1024,512]{1,0:T(8,128)(2,1)S(1)}, bf16[1024,512]{1,0:T(8,128)(2,1)}, u32[]{:S(2)}) copy-start(bf16[1024,512]{1,0:T(8,128)(2,1)} %get-tuple-element.6.grads_0) | copy-start | bytes 3145732
  82.6 22.0 %all-to-all-start.2 = ((f32[32,2,128]{2,1,0:T(2,128)}), f32[32,2,128]{2,1,0:T(2,128)S(1)}, u32[]{:S(2)}, u32[]{:S(2)}) async-start(f32[32,2,128]{2,1,0:T(2,128)} %bitcast.5), calls=%async_computation.2 | async-start | bytes 65536 | tf_op jit(solution)/shard_map/all_to_all | solution.py:177
